TPU v7x, 512 devices: a whole 4x4x16 slice. The times are simulated.
512 devices in a mesh: gx: 32 (over y, z_lo), gy: 16 (over x, z_hi, core).
Axes of the slice: x: 4, y: 4, z: 16 (z_hi: 2, z_lo: 8; z = z_hi * 8 + z_lo), core: 2. Of those that a mesh axis runs over, the one named last changes fastest.
Arguments:
- velocity: bfloat16 [3, 8, 256, 2048], P(None, None, 'gx', 'gy'), may hold values from -6 to 6
- kept_lm_qn: float32 [2, 8, 256, 2048], P(None, None, 'gx', 'gy'), may hold values from -3 to 3
- kept_mm_nn: float32 [2, 8, 256, 2048], P(None, None, 'gx', 'gy'), may hold values from 0.5 to 4
- back_src: int32 [8, 256, 256], P(None, 'gx', 'gy'), may hold values from 0 to 255, as said below
- solid_flags: int32 [8, 256, 2048], P(None, 'gx', 'gy'), may hold values from 0 to 1, as said below
- clip_flags: int32 [8, 256, 2048], P(None, 'gx', 'gy'), may hold values 0 or 1
Outputs:
- stress: float32 [6, 8, 256, 2048], P(None, None, 'gx', 'gy')
- kept_new: float32 [4, 8, 256, 2048], P(None, None, 'gx', 'gy')
Inputs may be any that keep to these rules, and one draw needn't show every extreme that they name: `back_src`: each block's source row lies 0 to 16 rows upstream of the block's own row, cyclically along the streamwise dimension; on one wall-normal level every block lies exactly 16 rows upstream. `solid_flags`: the ones form one pipe lying along the spanwise dimension, of circular section with radius max(2, 1) cells, centred that many levels above the bed.
All inputs are finite; a program needn't handle non-finite values. No bound on the sum of `clip_flags` on one device may be relied on, other than what follows from the above.
Results may differ from a plain program's by a relative error of at most 0.00105.
Values may be sent and summed in bfloat16 or wider, within the bound.
No kernel may reach another device: no remote copies, remote signals or barrier semaphores. Data moves between devices by JAX's collectives and lax.ppermute only.
A program may use at most 64 MiB of HBM per device.

v0:
```python
import jax
import jax.numpy as jnp
from jax import lax
from jax.sharding import PartitionSpec as P

TEST_NARROW = (0.25, 0.5, 0.25)
TEST_WIDE = (0.125, 0.25, 0.25, 0.25, 0.125)
PRODUCT_FLOOR = 0.05
RATE_SCALE = 0.5
CLIP_CAP = 0.1
RATIO_FLOOR = 0.02
PAIRS = ((0, 0), (1, 1), (2, 2), (0, 1), (0, 2), (1, 2))


def with_halo(cells, sides, width):
    for axis, dim in sides:
        count = lax.axis_size(axis)
        head = lax.slice_in_dim(cells, 0, width, axis=dim)
        tail = lax.slice_in_dim(cells, cells.shape[dim] - width, cells.shape[dim], axis=dim)
        cells = jnp.concatenate(
            [
                lax.ppermute(tail, axis, [(i, (i + 1) % count) for i in range(count)]),
                cells,
                lax.ppermute(head, axis, [((i + 1) % count, i) for i in range(count)]),
            ],
            axis=dim,
        )
    return cells


def passed_along(x, axis, by):
    count = lax.axis_size(axis)
    return lax.ppermute(x, axis, [(i, (i + by) % count) for i in range(count)])


def box_filter(field, weights):
    reach = (len(weights) - 1) // 2
    span_x = field.shape[-2] - 2 * reach
    along_x = sum((weights[k] * field[..., k : k + span_x, :] for k in range(len(weights))))
    span_y = field.shape[-1] - 2 * reach
    return sum((weights[k] * along_x[..., k : k + span_y] for k in range(len(weights))))


def contract(left, right):
    return jnp.sum(left[:3] * right[:3], axis=0) + 2.0 * jnp.sum(left[3:] * right[3:], axis=0)


def vertical_diff(field):
    padded = jnp.concatenate([field[..., :1, :, :], field, field[..., -1:, :, :]], axis=-3)
    return (padded[..., 2:, :, :] - padded[..., :-2, :, :]) * 0.5


def strain_rate(vel):
    grad_x = (vel[..., 2:, 1:-1] - vel[..., :-2, 1:-1]) * 0.5
    grad_y = (vel[..., 1:-1, 2:] - vel[..., 1:-1, :-2]) * 0.5
    grad_z = vertical_diff(vel)[..., 1:-1, 1:-1]
    grads = (grad_x, grad_y, grad_z)
    tensor = jnp.stack([0.5 * (grads[j][i] + grads[i][j]) for i, j in PAIRS])
    return (tensor, jnp.sqrt(2.0 * contract(tensor, tensor)))


def pair_products(vel):
    return jnp.stack([vel[i] * vel[j] for i, j in PAIRS])


def channels(vel):
    tensor, mag = strain_rate(vel)
    inner = vel[..., 1:-1, 1:-1]
    return (jnp.concatenate([inner, pair_products(inner), mag[None] * tensor], axis=0), tensor, mag)


def relax_weight(product):
    rate = RATE_SCALE * jnp.power(jnp.maximum(product, PRODUCT_FLOOR), 0.125)
    return rate / (1.0 + rate)


def finish(chans, strain_in, mag_in, sources, solid, clipped):
    narrow = box_filter(chans, TEST_NARROW)
    wide = box_filter(chans, TEST_WIDE)
    strain_narrow, mag_narrow = strain_rate(narrow[:3, ..., 1:-1, 1:-1])
    strain_wide, mag_wide = strain_rate(wide[:3])
    narrow_in = narrow[..., 2:-2, 2:-2]
    wide_in = wide[..., 1:-1, 1:-1]
    leonard_narrow = narrow_in[3:9] - pair_products(narrow_in[:3])
    leonard_wide = wide_in[3:9] - pair_products(wide_in[:3])
    model_narrow = 2.0 * (narrow_in[9:15] - 4.0 * mag_narrow[None] * strain_narrow)
    model_wide = 2.0 * (wide_in[9:15] - 16.0 * mag_wide[None] * strain_wide)
    lm_now = contract(leonard_narrow, model_narrow)
    mm_now = contract(model_narrow, model_narrow)
    qn_now = contract(leonard_wide, model_wide)
    nn_now = contract(model_wide, model_wide)
    old_lm, old_qn, old_mm, old_nn = (sources[0], sources[1], sources[2], sources[3])
    weight_narrow = relax_weight(old_lm * old_mm)
    weight_wide = relax_weight(old_qn * old_nn)
    new_lm = weight_narrow * lm_now + (1.0 - weight_narrow) * old_lm
    new_mm = weight_narrow * mm_now + (1.0 - weight_narrow) * old_mm
    new_qn = weight_wide * qn_now + (1.0 - weight_wide) * old_qn
    new_nn = weight_wide * nn_now + (1.0 - weight_wide) * old_nn
    coeff_narrow = jnp.maximum(new_lm, 0.0) / new_mm
    coeff_wide = jnp.maximum(new_qn, 0.0) / new_nn
    coeff = (
        coeff_narrow
        * coeff_narrow
        / jnp.maximum(jnp.maximum(coeff_wide, 0.125 * coeff_narrow), RATIO_FLOOR)
    )
    coeff = jnp.where(clipped == 1, jnp.minimum(coeff, CLIP_CAP), coeff)
    stress = -2.0 * coeff[None] * mag_in[None] * strain_in
    stress = jnp.where(solid[None] == 1, 0.0, stress)
    return (stress, jnp.stack([new_lm, new_mm, new_qn, new_nn]))


def local(velocity, kept_lm_qn, kept_mm_nn, back_src, solid_flags, clip_flags):
    masked = jnp.where(solid_flags[None] == 1, jnp.zeros((), velocity.dtype), velocity)
    near_vel = with_halo(masked, (("gx", 2), ("gy", 3)), 1)
    own_chans, strain_in, mag_in = channels(near_vel.astype(jnp.float32))
    chans = with_halo(own_chans, (("gx", 2), ("gy", 3)), 3)
    own = jnp.concatenate([kept_lm_qn, kept_mm_nn], axis=0)
    pieces = [own]
    for step_back in (1, 2):
        pieces.insert(0, passed_along(own, "gx", step_back))
    stacked = jnp.concatenate(pieces, axis=2)
    rows_dev = velocity.shape[2]
    width = velocity.shape[3]
    total_rows = rows_dev * lax.axis_size("gx")
    first = lax.axis_index("gx") * rows_dev
    local_rows = (back_src - first + 2 * rows_dev) % total_rows
    blocks = back_src.shape[2]
    local_rows = jnp.broadcast_to(local_rows[..., None], local_rows.shape + (width // blocks,))
    local_rows = local_rows.reshape(local_rows.shape[0], rows_dev, width)
    candidates = jnp.arange(3 * rows_dev, dtype=jnp.int32)[None, None, :, None]
    selector = (local_rows[:, :, None, :] == candidates).astype(jnp.float32)
    picked = jnp.sum(selector[None] * stacked[:, :, None, :, :], axis=3)
    return finish(chans, strain_in, mag_in, picked, solid_flags, clip_flags)


def solution(mesh):
    in_specs = (
        P(None, None, "gx", "gy"),
        P(None, None, "gx", "gy"),
        P(None, None, "gx", "gy"),
        P(None, "gx", "gy"),
        P(None, "gx", "gy"),
        P(None, "gx", "gy"),
    )
    out_specs = (P(None, None, "gx", "gy"), P(None, None, "gx", "gy"))
    return jax.shard_map(local, mesh=mesh, in_specs=in_specs, out_specs=out_specs, check_vma=False)
```

profile of v0, /device:TPU:1, one launch (start us, length us, event | category | flops | bytes accessed | tf_op | source)
XLA Modules:
  0.0 117.5 jit_solution(17802959188030117672)
XLA Ops:
  2.2 4.4 %collective-permute-start.2 = (bf16[3,8,1,128]{3,2,1,0:T(2,128)(2,1)S(1)}, bf16[3,8,1,128]{3,2,1,0:T(2,128)(2,1)S(1)}, u32[]{:S(2)}, u32[]{:S(2)}) collective-permute-start(bf16[3,8,1,128]{3,2,1,0:T(2,128)(2,1)S(1)} %get-tuple-element.79), channel_id=1, source_target_pairs={{0,16},{16,32},{32,48},{48,64},{64,80},{80,96},{96,112},{112,128},... | collective-permute-start | bytes 18440 | tf_op jit(solution)/shard_map/ppermute | solution.py:22
  6.6 13.7 %collective-permute-start.3 = (bf16[3,8,1,128]{3,2,1,0:T(2,128)(2,1)S(1)}, bf16[3,8,1,128]{3,2,1,0:T(2,128)(2,1)S(1)}, u32[]{:S(2)}, u32[]{:S(2)}) collective-permute-start(bf16[3,8,1,128]{3,2,1,0:T(2,128)(2,1)S(1)} %get-tuple-element.80), channel_id=1, source_target_pairs={{16,0},{32,16},{48,32},{64,48},{80,64},{96,80},{112,96},{128,112},... | collective-permute-start | bytes 18440 | tf_op jit(solution)/shard_map/ppermute | solution.py:24
  20.3 0.8 constant_dynamic-update-slice_fusion.1
  21.2 0.8 constant_dynamic-update-slice_fusion
  22.0 1.9 %collective-permute-start = (f32[4,8,8,128]{3,2,1,0:T(8,128)S(1)}, f32[4,8,8,128]{3,2,1,0:T(8,128)S(1)}, u32[]{:S(2)}, u32[]{:S(2)}) collective-permute-start(f32[4,8,8,128]{3,2,1,0:T(8,128)S(1)} %constant_dynamic-update-slice_fusion), channel_id=1, source_target_pairs={{0,32},{16,48},{32,64},{48,80},{64,96},{80,112},{96,128},{112,144}... | collective-permute-start | bytes 393224 | tf_op jit(solution)/shard_map/ppermute | solution.py:33
  23.9 1.9 %collective-permute-start.1 = (f32[4,8,8,128]{3,2,1,0:T(8,128)S(1)}, f32[4,8,8,128]{3,2,1,0:T(8,128)S(1)}, u32[]{:S(2)}, u32[]{:S(2)}) collective-permute-start(f32[4,8,8,128]{3,2,1,0:T(8,128)S(1)} %constant_dynamic-update-slice_fusion), channel_id=1, source_target_pairs={{0,16},{16,32},{32,48},{48,64},{64,80},{80,96},{96,112},{112,128},... | collective-permute-start | bytes 393224 | tf_op jit(solution)/shard_map/ppermute | solution.py:33
  26.0 13.3 %collective-permute-start.4 = (bf16[3,8,10,1]{3,2,1,0:T(8,128)(2,1)S(1)}, bf16[3,8,10,1]{3,2,1,0:T(8,128)(2,1)S(1)}, u32[]{:S(2)}, u32[]{:S(2)}) collective-permute-start(bf16[3,8,10,1]{3,2,1,0:T(8,128)(2,1)S(1)} %get-tuple-element.77), channel_id=1, source_target_pairs={{0,1},{1,2},{2,3},{3,4},{4,5},{5,6},{6,7},{7,8},{8,9},{9,10},{10,1... | collective-permute-start | bytes 1448 | tf_op jit(solution)/shard_map/ppermute | solution.py:22
  39.4 1.9 %collective-permute-start.5 = (bf16[3,8,10,1]{3,2,1,0:T(8,128)(2,1)S(1)}, bf16[3,8,10,1]{3,2,1,0:T(8,128)(2,1)S(1)}, u32[]{:S(2)}, u32[]{:S(2)}) collective-permute-start(bf16[3,8,10,1]{3,2,1,0:T(8,128)(2,1)S(1)} %get-tuple-element.78), channel_id=1, source_target_pairs={{1,0},{2,1},{3,2},{4,3},{5,4},{6,5},{7,6},{8,7},{9,8},{10,9},{11,1... | collective-permute-start | bytes 1448 | tf_op jit(solution)/shard_map/ppermute | solution.py:24
  42.5 13.7 %collective-permute-done.5 = bf16[3,8,10,1]{3,2,1,0:T(8,128)(2,1)S(1)} collective-permute-done((bf16[3,8,10,1]{3,2,1,0:T(8,128)(2,1)S(1)}, bf16[3,8,10,1]{3,2,1,0:T(8,128)(2,1)S(1)}, u32[]{:S(2)}, u32[]{:S(2)}) %collective-permute-start.5) | collective-permute-done | bytes 512 | tf_op jit(solution)/shard_map/ppermute | solution.py:24
  58.3 1.9 %collective-permute-start.6 = (f32[15,8,3,128]{3,2,1,0:T(4,128)S(1)}, f32[15,8,3,128]{3,2,1,0:T(4,128)S(1)}, u32[]{:S(2)}, u32[]{:S(2)}) collective-permute-start(f32[15,8,3,128]{3,2,1,0:T(4,128)S(1)} %get-tuple-element.48), channel_id=1, source_target_pairs={{0,16},{16,32},{32,48},{48,64},{64,80},{80,96},{96,112},{112,128},... | collective-permute-start | bytes 552968 | tf_op jit(solution)/shard_map/ppermute | solution.py:22
  60.2 12.1 %collective-permute-start.7 = (f32[15,8,3,128]{3,2,1,0:T(4,128)S(1)}, f32[15,8,3,128]{3,2,1,0:T(4,128)S(1)}, u32[]{:S(2)}, u32[]{:S(2)}) collective-permute-start(f32[15,8,3,128]{3,2,1,0:T(4,128)S(1)} %get-tuple-element.49), channel_id=1, source_target_pairs={{16,0},{32,16},{48,32},{64,48},{80,64},{96,80},{112,96},{128,112},... | collective-permute-start | bytes 552968 | tf_op jit(solution)/shard_map/ppermute | solution.py:24
  73.2 0.9 collective-permute-done.6
  74.1 1.3 %collective-permute-done.7 = f32[15,8,3,128]{3,2,1,0:T(4,128)S(1)} collective-permute-done((f32[15,8,3,128]{3,2,1,0:T(4,128)S(1)}, f32[15,8,3,128]{3,2,1,0:T(4,128)S(1)}, u32[]{:S(2)}, u32[]{:S(2)}) %collective-permute-start.7) | collective-permute-done | bytes 184352 | tf_op jit(solution)/shard_map/ppermute | solution.py:24
  76.6 1.5 %copy.42 = f32[15,8,14,3]{0,1,3,2:T(8,128)} copy(f32[15,8,14,3]{3,2,1,0:T(8,128)S(1)} %get-tuple-element.46) | data formatting | bytes 40320 | tf_op jit(solution)/shard_map/slice | solution.py:19
  78.1 4.6 %collective-permute-start.8 = (f32[15,8,14,3]{0,1,3,2:T(8,128)}, f32[15,8,14,3]{0,1,3,2:T(8,128)S(1)}, u32[]{:S(2)}, u32[]{:S(2)}) collective-permute-start(f32[15,8,14,3]{0,1,3,2:T(8,128)} %copy.42), channel_id=1, source_target_pairs={{0,1},{1,2},{2,3},{3,4},{4,5},{5,6},{6,7},{7,8},{8,9},{9,10},{10,1... | collective-permute-start | bytes 60488 | tf_op jit(solution)/shard_map/ppermute | solution.py:22
  83.5 2.1 %collective-permute-start.9 = (f32[15,8,14,3]{0,1,3,2:T(8,128)S(1)}, f32[15,8,14,3]{0,1,3,2:T(8,128)}, u32[]{:S(2)}, u32[]{:S(2)}) collective-permute-start(f32[15,8,14,3]{0,1,3,2:T(8,128)S(1)} %copy.43), channel_id=1, source_target_pairs={{1,0},{2,1},{3,2},{4,3},{5,4},{6,5},{7,6},{8,7},{9,8},{10,9},{11,1... | collective-permute-start | bytes 60488 | tf_op jit(solution)/shard_map/ppermute | solution.py:24
  85.7 1.7 %multiply_reduce_fusion = f32[4,8,8,128]{3,2,1,0:T(8,128)S(1)} fusion(f32[4,8,24,128]{3,2,1,0:T(8,128)} %pad_maximum_fusion.8, f32[8,8,24,128]{3,2,1,0:T(8,128)S(1)} %fusion.12), kind=kLoop, calls=%fused_computation | loop fusion | flops 1540096 | bytes 1310720 | tf_op jit(solution)/shard_map/reduce_sum | solution.py:132
  87.4 1.2 %copy.44 = f32[15,8,14,3]{3,2,1,0:T(8,128)S(1)} copy(f32[15,8,14,3]{0,1,3,2:T(8,128)S(1)} %collective-permute-done.8) | data formatting | bytes 40320 | tf_op jit(solution)/shard_map/ppermute | solution.py:22
  88.6 13.3 %collective-permute-done.9 = f32[15,8,14,3]{0,1,3,2:T(8,128)} collective-permute-done((f32[15,8,14,3]{0,1,3,2:T(8,128)S(1)}, f32[15,8,14,3]{0,1,3,2:T(8,128)}, u32[]{:S(2)}, u32[]{:S(2)}) %collective-permute-start.9) | collective-permute-done | bytes 20192 | tf_op jit(solution)/shard_map/ppermute | solution.py:24
  101.9 2.1 %copy.45 = f32[15,8,14,3]{3,2,1,0:T(8,128)S(1)} copy(f32[15,8,14,3]{0,1,3,2:T(8,128)} %collective-permute-done.9) | data formatting | bytes 40320 | tf_op jit(solution)/shard_map/ppermute | solution.py:24
  104.0 2.4 %pad_maximum_fusion = f32[15,8,14,134]{3,2,1,0:T(8,128)S(1)} fusion(f32[15,8,14,3]{3,2,1,0:T(8,128)S(1)} %copy.45, f32[15,8,3,128]{3,2,1,0:T(4,128)} %copy-done.3, f32[15,8,8,128]{3,2,1,0:T(8,128)S(1)} %multiply_dynamic-update-slice_fusion, f32[15,8,3,128]{3,2,1,0:T(4,128)} %copy-done.2, f32[15,8,14,3]{3,2,1,0:T(8,128)S(1)} %copy.44), kind=kLoop, calls=%fused_computation.29 | loop fusion | flops 900480 | bytes 1800960 | tf_op jit(solution)/shard_map/concatenate | solution.py:20
  106.4 1.1 fusion.4
  107.5 2.1 %fusion = f32[15,8,10,130]{3,2,1,0:T(8,128)S(1)} fusion(f32[15,8,10,134]{3,2,1,0:T(8,128)S(1)} %fusion.4), kind=kLoop, calls=%fused_computation.2 | loop fusion | flops 1404000 | bytes 3744000 | tf_op jit(solution)/shard_map/add | solution.py:41
  110.9 1.1 fusion.8
  (101 shorter events, 14.4 us)
Async XLA Ops:
  2.2 23.6 %collective-permute-start.2 = (bf16[3,8,1,128]{3,2,1,0:T(2,128)(2,1)S(1)}, bf16[3,8,1,128]{3,2,1,0:T(2,128)(2,1)S(1)}, u32[]{:S(2)}, u32[]{:S(2)}) collective-permute-start(bf16[3,8,1,128]{3,2,1,0:T(2,128)(2,1)S(1)} %get-tuple-element.79), channel_id=1, source_target_pairs={{0,16},{16,32},{32,48},{48,64},{64,80},{80,96},{96,112},{112,128},... | collective-permute-start | bytes 18440 | tf_op jit(solution)/shard_map/ppermute | solution.py:22
  6.6 19.3 %collective-permute-start.3 = (bf16[3,8,1,128]{3,2,1,0:T(2,128)(2,1)S(1)}, bf16[3,8,1,128]{3,2,1,0:T(2,128)(2,1)S(1)}, u32[]{:S(2)}, u32[]{:S(2)}) collective-permute-start(bf16[3,8,1,128]{3,2,1,0:T(2,128)(2,1)S(1)} %get-tuple-element.80), channel_id=1, source_target_pairs={{16,0},{32,16},{48,32},{64,48},{80,64},{96,80},{112,96},{128,112},... | collective-permute-start | bytes 18440 | tf_op jit(solution)/shard_map/ppermute | solution.py:24
  22.0 50.4 %collective-permute-start = (f32[4,8,8,128]{3,2,1,0:T(8,128)S(1)}, f32[4,8,8,128]{3,2,1,0:T(8,128)S(1)}, u32[]{:S(2)}, u32[]{:S(2)}) collective-permute-start(f32[4,8,8,128]{3,2,1,0:T(8,128)S(1)} %constant_dynamic-update-slice_fusion), channel_id=1, source_target_pairs={{0,32},{16,48},{32,64},{48,80},{64,96},{80,112},{96,128},{112,144}... | collective-permute-start | bytes 393224 | tf_op jit(solution)/shard_map/ppermute | solution.py:33
  23.9 48.5 %collective-permute-start.1 = (f32[4,8,8,128]{3,2,1,0:T(8,128)S(1)}, f32[4,8,8,128]{3,2,1,0:T(8,128)S(1)}, u32[]{:S(2)}, u32[]{:S(2)}) collective-permute-start(f32[4,8,8,128]{3,2,1,0:T(8,128)S(1)} %constant_dynamic-update-slice_fusion), channel_id=1, source_target_pairs={{0,16},{16,32},{32,48},{48,64},{64,80},{80,96},{96,112},{112,128},... | collective-permute-start | bytes 393224 | tf_op jit(solution)/shard_map/ppermute | solution.py:33
  26.0 16.5 %collective-permute-start.4 = (bf16[3,8,10,1]{3,2,1,0:T(8,128)(2,1)S(1)}, bf16[3,8,10,1]{3,2,1,0:T(8,128)(2,1)S(1)}, u32[]{:S(2)}, u32[]{:S(2)}) collective-permute-start(bf16[3,8,10,1]{3,2,1,0:T(8,128)(2,1)S(1)} %get-tuple-element.77), channel_id=1, source_target_pairs={{0,1},{1,2},{2,3},{3,4},{4,5},{5,6},{6,7},{7,8},{8,9},{9,10},{10,1... | collective-permute-start | bytes 1448 | tf_op jit(solution)/shard_map/ppermute | solution.py:22
  39.4 16.8 %collective-permute-start.5 = (bf16[3,8,10,1]{3,2,1,0:T(8,128)(2,1)S(1)}, bf16[3,8,10,1]{3,2,1,0:T(8,128)(2,1)S(1)}, u32[]{:S(2)}, u32[]{:S(2)}) collective-permute-start(bf16[3,8,10,1]{3,2,1,0:T(8,128)(2,1)S(1)} %get-tuple-element.78), channel_id=1, source_target_pairs={{1,0},{2,1},{3,2},{4,3},{5,4},{6,5},{7,6},{8,7},{9,8},{10,9},{11,1... | collective-permute-start | bytes 1448 | tf_op jit(solution)/shard_map/ppermute | solution.py:24
  57.4 0.7 copy-start.4
  58.3 15.8 %collective-permute-start.6 = (f32[15,8,3,128]{3,2,1,0:T(4,128)S(1)}, f32[15,8,3,128]{3,2,1,0:T(4,128)S(1)}, u32[]{:S(2)}, u32[]{:S(2)}) collective-permute-start(f32[15,8,3,128]{3,2,1,0:T(4,128)S(1)} %get-tuple-element.48), channel_id=1, source_target_pairs={{0,16},{16,32},{32,48},{48,64},{64,80},{80,96},{96,112},{112,128},... | collective-permute-start | bytes 552968 | tf_op jit(solution)/shard_map/ppermute | solution.py:22
  60.2 15.2 %collective-permute-start.7 = (f32[15,8,3,128]{3,2,1,0:T(4,128)S(1)}, f32[15,8,3,128]{3,2,1,0:T(4,128)S(1)}, u32[]{:S(2)}, u32[]{:S(2)}) collective-permute-start(f32[15,8,3,128]{3,2,1,0:T(4,128)S(1)} %get-tuple-element.49), channel_id=1, source_target_pairs={{16,0},{32,16},{48,32},{64,48},{80,64},{96,80},{112,96},{128,112},... | collective-permute-start | bytes 552968 | tf_op jit(solution)/shard_map/ppermute | solution.py:24
  74.1 1.3 %copy-start.2 = (f32[15,8,3,128]{3,2,1,0:T(4,128)}, f32[15,8,3,128]{3,2,1,0:T(4,128)S(1)}, u32[]{:S(2)}) copy-start(f32[15,8,3,128]{3,2,1,0:T(4,128)S(1)} %collective-permute-done.6) | copy-start | bytes 552964
  75.4 0.7 copy-start.3
  78.1 9.3 %collective-permute-start.8 = (f32[15,8,14,3]{0,1,3,2:T(8,128)}, f32[15,8,14,3]{0,1,3,2:T(8,128)S(1)}, u32[]{:S(2)}, u32[]{:S(2)}) collective-permute-start(f32[15,8,14,3]{0,1,3,2:T(8,128)} %copy.42), channel_id=1, source_target_pairs={{0,1},{1,2},{2,3},{3,4},{4,5},{5,6},{6,7},{7,8},{8,9},{9,10},{10,1... | collective-permute-start | bytes 60488 | tf_op jit(solution)/shard_map/ppermute | solution.py:22
  83.5 18.3 %collective-permute-start.9 = (f32[15,8,14,3]{0,1,3,2:T(8,128)S(1)}, f32[15,8,14,3]{0,1,3,2:T(8,128)}, u32[]{:S(2)}, u32[]{:S(2)}) collective-permute-start(f32[15,8,14,3]{0,1,3,2:T(8,128)S(1)} %copy.43), channel_id=1, source_target_pairs={{1,0},{2,1},{3,2},{4,3},{5,4},{6,5},{7,6},{8,7},{9,8},{10,9},{11,1... | collective-permute-start | bytes 60488 | tf_op jit(solution)/shard_map/ppermute | solution.py:24
  109.6 1.3 %copy-start = (f32[15,8,10,130]{3,2,1,0:T(8,128)}, f32[15,8,10,130]{3,2,1,0:T(8,128)S(1)}, u32[]{:S(2)}) copy-start(f32[15,8,10,130]{3,2,1,0:T(8,128)S(1)} %fusion) | copy-start | bytes 1872004
  112.0 1.0 slice-start
  112.0 1.7 %copy-start.1 = (f32[15,8,10,130]{3,2,1,0:T(8,128)S(1)}, f32[15,8,10,130]{3,2,1,0:T(8,128)}, u32[]{:S(2)}) copy-start(f32[15,8,10,130]{3,2,1,0:T(8,128)} %copy-done) | copy-start | bytes 1872004
  115.0 0.8 copy-start.6
  115.2 0.9 copy-start.5
where the time goes:
time: 118 us; the launch traced here: 117 us
  starting transfers between devices  57.8 us (49%)
  waiting for transfers between devices  29.2 us (25%)
  other arithmetic  17.7 us (15%)
  local copies, waits for them, and re-layouts  11.6 us (10%)
  between operations  1.24 us (1%)
    ppermute x4, starting transfers between devices, with_halo(): lax.ppermute(head, axis, [((i + 1) % count, i) for i in range(count)])  29.8 us
    ppermute x4, waiting for transfers between devices, with_halo(): lax.ppermute(head, axis, [((i + 1) % count, i) for i in range(count)])  28.2 us
    ppermute x4, starting transfers between devices, with_halo(): lax.ppermute(tail, axis, [(i, (i + 1) % count) for i in range(count)])  24.2 us
    ppermute x2, starting transfers between devices, passed_along(): return lax.ppermute(x, axis, [(i, (i + by) % count) for i in range(count)])  3.83 us
    unnamed x15, local copies, waits for them, and re-layouts  3.39 us
    add x2, other arithmetic, box_filter(): sum((weights[k] * along_x[..., k:k + span_y] for k in range(len(weights))))  3.17 us
    concatenate x3, other arithmetic, with_halo(): jnp.concatenate([lax.ppermute(tail, axis, [(i, (i + 1) % count) for i in...  2.65 us
  transfers between devices with their start and end apart: 10, of which 4 were waited for; matrix products, arithmetic and copies ran while one was open for 8% of the time, Pallas kernels for 0%

commit v1 on v0

v1 whole, which is shorter than its diff:
```python
import jax
import jax.numpy as jnp
from jax import lax
from jax.experimental import pallas as pl
from jax.experimental.pallas import tpu as pltpu
from jax.sharding import PartitionSpec as P

PRODUCT_FLOOR = 0.05
RATE_SCALE = 0.5
CLIP_CAP = 0.1
RATIO_FLOOR = 0.02
PAIRS = ((0, 0), (1, 1), (2, 2), (0, 1), (0, 2), (1, 2))
KEPT_SCALE = 32767.0 / 1.4142137
F32 = jnp.float32
BF16 = jnp.bfloat16
VMEM_LIMIT = 32 * 1024 * 1024


def row(ref, x, lead=None):
    at = (pl.ds(x, 8, stride=8), slice(None))
    return ref[at] if lead is None else ref[(lead,) + at]


def masked_rows(vel_ref, solid_ref, scratch):
    solid = solid_ref[...] == 1
    for c in range(3):
        scratch[c] = jnp.where(solid, 0.0, vel_ref[c].astype(F32))


def encode(x):
    root = jnp.sqrt(jnp.sqrt(jnp.abs(x)))
    scaled = jnp.where(x < 0, -root, root) * KEPT_SCALE
    return jnp.round(scaled).astype(jnp.int32).astype(jnp.int16)


def decode(code):
    y = code.astype(jnp.int32).astype(F32) * (1.0 / KEPT_SCALE)
    y2 = y * y
    return jnp.where(y < 0, -y2, y2) * y2


def pack_kernel(vel_ref, solid_ref, lq_ref, mn_ref, head_ref, tail_ref, kept_ref, scratch):
    masked_rows(vel_ref, solid_ref, scratch)
    for first, out in ((0, head_ref), (4, tail_ref)):
        rows = [row(scratch, first + x, c) for c in range(3) for x in range(4)]
        out[...] = jnp.concatenate(rows, axis=0).astype(BF16)
    kept_ref[pl.ds(0, 128), :] = encode(lq_ref[...])
    kept_ref[pl.ds(128, 128), :] = encode(mn_ref[...])


def halo_rows(scratch, lo_ref, hi_ref):
    lo = lo_ref[...].astype(F32).reshape(3, 4, 8, 128)
    hi = hi_ref[...].astype(F32).reshape(3, 4, 8, 128)
    out = []
    for c in range(3):
        rows = [lo[c, x] for x in (1, 2, 3)]
        rows += [row(scratch, x, c) for x in range(8)]
        rows += [hi[c, x] for x in (0, 1, 2)]
        out.append(rows)
    return out


def strip_kernel(par_ref, vel_ref, solid_ref, lo_ref, hi_ref, near_ref, far_ref, scratch):
    masked_rows(vel_ref, solid_ref, scratch)
    rows = halo_rows(scratch, lo_ref, hi_ref)
    lane = lax.broadcasted_iota(jnp.int32, (8, 128), 1)
    left, right = [], []
    for c in range(3):
        lefts = jnp.zeros((8, 128), F32)
        rights = jnp.zeros((8, 128), F32)
        for i in range(14):
            here = (lane >= 4 * i) & (lane < 4 * i + 4)
            lefts = jnp.where(here, pltpu.roll(rows[c][i], 4 * i, 1) if i else rows[c][i], lefts)
            rights = jnp.where(here, pltpu.roll(rows[c][i], 4 * i + 4, 1), rights)
        left.append(lefts)
        right.append(rights)
    left = jnp.concatenate(left + [jnp.zeros((8, 128), F32)], axis=0)
    right = jnp.concatenate(right + [jnp.zeros((8, 128), F32)], axis=0)
    even = par_ref[0] == 0
    near_ref[...] = jnp.where(even, right, left).astype(BF16)
    far_ref[...] = jnp.where(even, left, right).astype(BF16)


def shift_y(a, b, k, lane):
    if k > 0:
        return pltpu.roll(jnp.where(lane < k, b, a), 128 - k, 1)
    return pltpu.roll(jnp.where(lane >= 128 + k, b, a), -k, 1)


def diff_z(f, sub):
    up = jnp.where(sub == 7, f, pltpu.roll(f, 7, 0))
    down = jnp.where(sub == 0, f, pltpu.roll(f, 1, 0))
    return up - down


def strain(dx, dy, dz):
    d = (dx, dy, dz)
    s = [0.5 * d[i][i] for i in range(3)] + [0.25 * (d[j][i] + d[i][j]) for i, j in PAIRS[3:]]
    diag = s[0] * s[0] + s[1] * s[1] + s[2] * s[2]
    off = s[3] * s[3] + s[4] * s[4] + s[5] * s[5]
    return s, jnp.sqrt(2.0 * diag + 4.0 * off)


def contract(a, b):
    return (a[0] * b[0] + a[1] * b[1] + a[2] * b[2]) + 2.0 * (a[3] * b[3] + a[4] * b[4] + a[5] * b[5])


def relax_weight(product):
    r = RATE_SCALE * jnp.sqrt(jnp.sqrt(jnp.sqrt(jnp.maximum(product, PRODUCT_FLOOR))))
    return r / (1.0 + r)


def main_kernel(par_ref, vel_ref, solid_ref, clip_ref, lo_ref, hi_ref, near_ref, far_ref, src_ref,
                lq_ref, mn_ref, up1_ref, up2_ref, stress_ref, new_ref, scratch, old):
    lane = lax.broadcasted_iota(jnp.int32, (8, 128), 1)
    sub = lax.broadcasted_iota(jnp.int32, (8, 128), 0)
    here = lax.broadcasted_iota(jnp.int32, (64, 16), 0) % 8
    back = (par_ref[1] + here - src_ref[...] + 512) % 256
    spread = (lax.broadcasted_iota(jnp.int32, (16, 128), 1) // 8 == lax.broadcasted_iota(jnp.int32, (16, 128), 0))
    local = jnp.dot((16 + here - back).astype(F32), spread.astype(F32), preferred_element_type=F32)
    local = (local + 0.5).astype(jnp.int32)
    for z in range(8):
        at = pl.ds(8 * z, 8)
        idx = local[8 * z : 8 * z + 8]
        inner = idx & 7
        for f in range(4):
            rows = pl.ds(64 * f + 8 * z, 8)
            own_ref = lq_ref if f < 2 else mn_ref
            own = own_ref[pl.ds(64 * (f % 2) + 8 * z, 8), :]
            got = jnp.take_along_axis(own, inner, axis=0)
            one = jnp.take_along_axis(decode(up1_ref[f, at, :]), inner, axis=0)
            two = jnp.take_along_axis(decode(up2_ref[f, at, :]), inner, axis=0)
            old[f, at, :] = jnp.where(idx < 8, two, jnp.where(idx < 16, one, got))
    masked_rows(vel_ref, solid_ref, scratch)
    core = halo_rows(scratch, lo_ref, hi_ref)
    near = near_ref[...].astype(F32)
    far = far_ref[...].astype(F32)
    even = par_ref[0] == 0
    left = jnp.where(even, far, near).reshape(4, 8, 128)
    right = jnp.where(even, near, far).reshape(4, 8, 128)
    edge = []
    for c in range(3):
        rows = []
        for i in range(14):
            r = pltpu.roll(right[c], 128 - 4 * i, 1) if i else right[c]
            l = pltpu.roll(left[c], 124 - 4 * i, 1)
            rows.append(jnp.where(lane < 64, r, l))
        edge.append(rows)
    vn, vw, vdn, vdw = ([[None] * 14 for _ in range(3)] for _ in range(4))
    near_y = [[None] * 14 for _ in range(3)]
    for c in range(3):
        for i in range(14):
            a, b = core[c][i], edge[c][i]
            p1, m1 = shift_y(a, b, 1, lane), shift_y(a, b, -1, lane)
            p2, m2 = shift_y(a, b, 2, lane), shift_y(a, b, -2, lane)
            s1, d1, s2, d2 = p1 + m1, p1 - m1, p2 + m2, p2 - m2
            near_y[c][i] = d1
            if 1 <= i <= 12:
                vn[c][i] = a + a + s1
            t = a + s1
            vw[c][i] = t + t + s2
            if 2 <= i <= 11:
                vdn[c][i] = d1 + d1 + d2
            if 1 <= i <= 12:
                d3 = shift_y(a, b, 3, lane) - shift_y(a, b, -3, lane)
                vdw[c][i] = d1 + d2 + d2 + d3
    yn, yw = [None] * 14, [None] * 14
    own_flux = [None] * 14
    for i in range(1, 13):
        flux = []
        for t, o in ((core, edge), (edge, core)):
            dx = [t[c][i + 1] - t[c][i - 1] for c in range(3)]
            if t is core:
                dy = [near_y[c][i] for c in range(3)]
            else:
                dy = [shift_y(t[c][i], o[c][i], 1, lane) - shift_y(t[c][i], o[c][i], -1, lane) for c in range(3)]
            dz = [diff_z(t[c][i], sub) for c in range(3)]
            s, mag = strain(dx, dy, dz)
            prods = [t[p][i] * t[q][i] for p, q in PAIRS]
            flux.append(prods + [mag * e for e in s])
        own_flux[i] = flux[0][6:]
        ns, ws = [], []
        for a, b in zip(*flux):
            s1 = shift_y(a, b, 1, lane) + shift_y(a, b, -1, lane)
            s2 = shift_y(a, b, 2, lane) + shift_y(a, b, -2, lane)
            t = a + s1
            ns.append(a + t)
            ws.append(t + t + s2)
        yn[i], yw[i] = ns, ws

    def filt_n(r, i):
        return (r[i - 1] + r[i + 1] + (r[i] + r[i])) * 0.0625

    def filt_w(r, i):
        t = r[i - 1] + r[i] + r[i + 1]
        return (r[i - 2] + r[i + 2] + (t + t)) * 0.015625

    def column(r, k):
        return [None if v is None else v[k] for v in r]

    un = [[filt_n(vn[c], i) if 2 <= i <= 11 else None for i in range(14)] for c in range(3)]
    uw = [[filt_w(vw[c], i) if 2 <= i <= 11 else None for i in range(14)] for c in range(3)]
    for x in range(8):
        i = x + 3
        result = []
        for u, ydiff, filt, flux, factor in ((un, vdn, filt_n, yn, 4.0), (uw, vdw, filt_w, yw, 16.0)):
            dx = [u[c][i + 1] - u[c][i - 1] for c in range(3)]
            dy = [filt(ydiff[c], i) for c in range(3)]
            dz = [diff_z(u[c][i], sub) for c in range(3)]
            s, mag = strain(dx, dy, dz)
            f = [filt(column(flux, k), i) for k in range(12)]
            lhs = [f[k] - u[p][i] * u[q][i] for k, (p, q) in enumerate(PAIRS)]
            fm = factor * mag
            rhs = [f[6 + k] - fm * s[k] for k in range(6)]
            result.append((2.0 * contract(lhs, rhs), 4.0 * contract(rhs, rhs)))
        (lm, mm), (qn, nn) = result
        o_lm, o_qn, o_mm, o_nn = (row(old, x, f) for f in range(4))
        wn = relax_weight(o_lm * o_mm)
        ww = relax_weight(o_qn * o_nn)
        new_lm = wn * lm + (1.0 - wn) * o_lm
        new_mm = wn * mm + (1.0 - wn) * o_mm
        new_qn = ww * qn + (1.0 - ww) * o_qn
        new_nn = ww * nn + (1.0 - ww) * o_nn
        c2 = jnp.maximum(new_lm, 0.0) / new_mm
        c4 = jnp.maximum(new_qn, 0.0) / new_nn
        cs = c2 * c2 / jnp.maximum(jnp.maximum(c4, 0.125 * c2), RATIO_FLOOR)
        cs = jnp.where(row(clip_ref, x) == 1, jnp.minimum(cs, CLIP_CAP), cs)
        cs = jnp.where(row(solid_ref, x) == 1, 0.0, -2.0 * cs)
        at = (pl.ds(x, 8, stride=8), slice(None))
        for k in range(6):
            stress_ref[(k,) + at] = cs * own_flux[i][k]
        for k, v in enumerate((new_lm, new_mm, new_qn, new_nn)):
            new_ref[(k,) + at] = v


SMEM = pl.BlockSpec(memory_space=pltpu.SMEM)
VM = pl.BlockSpec(memory_space=pltpu.VMEM)


def call(kernel, outs, specs, scratch):
    return pl.pallas_call(
        kernel, out_shape=outs, in_specs=specs, out_specs=[VM] * len(outs), scratch_shapes=scratch,
        compiler_params=pltpu.CompilerParams(vmem_limit_bytes=VMEM_LIMIT),
    )


def ring(n, by):
    return [(i, (i + by) % n) for i in range(n)]


def local(velocity, kept_lm_qn, kept_mm_nn, back_src, solid_flags, clip_flags):
    sds = jax.ShapeDtypeStruct
    vel = velocity.reshape(3, 64, 128)
    solid = solid_flags.reshape(64, 128)
    clip = clip_flags.reshape(64, 128)
    lq = kept_lm_qn.reshape(128, 128)
    mn = kept_mm_nn.reshape(128, 128)
    src = back_src.reshape(64, 16)
    gx, gy = lax.axis_index("gx"), lax.axis_index("gy")
    par = jnp.stack([gy % 2, gx * 8]).astype(jnp.int32)
    trans = pltpu.VMEM((3, 64, 128), F32)
    head, tail, kept = call(
        pack_kernel, [sds((96, 128), BF16), sds((96, 128), BF16), sds((256, 128), jnp.int16)], [VM] * 4, [trans]
    )(vel, solid, lq, mn)
    up2 = lax.ppermute(kept, "gx", ring(32, 2))
    up1 = lax.ppermute(kept, "gx", ring(32, 1))
    lo = lax.ppermute(tail, "gx", ring(32, 1))
    hi = lax.ppermute(head, "gx", ring(32, -1))
    near, far = call(strip_kernel, [sds((32, 128), BF16)] * 2, [SMEM] + [VM] * 4, [trans])(par, vel, solid, lo, hi)
    near = lax.ppermute(near, "gy", [(i, i ^ 1) for i in range(16)])
    far = lax.ppermute(far, "gy", [(i, (i + 1) % 16 if i % 2 else (i - 1) % 16) for i in range(16)])
    stress, new = call(
        main_kernel, [sds((6, 64, 128), F32), sds((4, 64, 128), F32)], [SMEM] + [VM] * 12,
        [trans, pltpu.VMEM((4, 64, 128), F32)],
    )(par, vel, solid, clip, lo, hi, near, far, src, lq, mn, up1.reshape(4, 64, 128), up2.reshape(4, 64, 128))
    return stress.reshape(6, 8, 8, 128), new.reshape(4, 8, 8, 128)


def solution(mesh):
    in_specs = (
        P(None, None, "gx", "gy"),
        P(None, None, "gx", "gy"),
        P(None, None, "gx", "gy"),
        P(None, "gx", "gy"),
        P(None, "gx", "gy"),
        P(None, "gx", "gy"),
    )
    out_specs = (P(None, None, "gx", "gy"), P(None, None, "gx", "gy"))
    return jax.shard_map(local, mesh=mesh, in_specs=in_specs, out_specs=out_specs, check_vma=False)
```

time: 118 us -> 54.1 us (0.46)
  the two profiles are of different devices: /device:TPU:1 before, /device:TPU:495 now
where the time goes in v1:
time: 54.1 us; the launch traced here: 53.5 us
  waiting for transfers between devices  23.2 us (43%)
  starting transfers between devices  22.4 us (41%)
  Pallas kernels  3.86 us (7%)
  local copies, waits for them, and re-layouts  3.25 us (6%)
  between operations  0.76 us (1%)
    ppermute x1, waiting for transfers between devices, local(): lax.ppermute(far, 'gy', [(i, (i + 1) % 16 if i % 2 else (i - 1) % 16) for...  13.9 us
    ppermute x1, waiting for transfers between devices, local(): hi = lax.ppermute(head, 'gx', ring(32, -1))  9.34 us
    ppermute x1, starting transfers between devices, local(): up2 = lax.ppermute(kept, 'gx', ring(32, 2))  7.08 us
    ppermute x1, starting transfers between devices, local(): near = lax.ppermute(near, 'gy', [(i, i ^ 1) for i in range(16)])  4.57 us
    ppermute x1, starting transfers between devices, local(): up1 = lax.ppermute(kept, 'gx', ring(32, 1))  3.55 us
    unnamed x20, local copies, waits for them, and re-layouts  3.25 us
    pallas_call x1, Pallas kernels, local(): call(main_kernel, [sds((6, 64, 128), F32), sds((4, 64, 128), F32)], [SMEM...  3.07 us
    ppermute x1, starting transfers between devices, local(): lo = lax.ppermute(tail, 'gx', ring(32, 1))  2.65 us
  transfers between devices with their start and end apart: 6, of which 2 were waited for; matrix products, arithmetic and copies ran while one was open for 0% of the time, Pallas kernels for 1%

profile of v1, /device:TPU:495, one launch (start us, length us, event | category | flops | bytes accessed | tf_op | source)
XLA Modules:
  0.0 53.5 jit_solution(13555794707004671966)
XLA Ops:
  0.6 0.0 copy-start
  0.6 0.8 %copy-done = bf16[3,8,8,128]{3,2,1,0:T(8,128)(2,1)S(1)} copy-done((bf16[3,8,8,128]{3,2,1,0:T(8,128)(2,1)S(1)}, bf16[3,8,8,128]{3,2,1,0:T(8,128)(2,1)}, u32[]{:S(2)}) %copy-start) | copy-done | bytes 49176
  1.4 0.8 %copy-done.2 = s32[8,8,128]{2,1,0:T(8,128)S(1)} copy-done((s32[8,8,128]{2,1,0:T(8,128)S(1)}, s32[8,8,128]{2,1,0:T(8,128)}, u32[]{:S(2)}) %copy-start.2) | copy-done | bytes 32792
  2.2 0.8 %copy-done.4 = f32[2,8,8,128]{3,2,1,0:T(8,128)S(1)} copy-done((f32[2,8,8,128]{3,2,1,0:T(8,128)S(1)}, f32[2,8,8,128]{3,2,1,0:T(8,128)}, u32[]{:S(2)}) %copy-start.4) | copy-done | bytes 65560
  3.0 0.8 %copy-done.6 = f32[2,8,8,128]{3,2,1,0:T(8,128)S(1)} copy-done((f32[2,8,8,128]{3,2,1,0:T(8,128)S(1)}, f32[2,8,8,128]{3,2,1,0:T(8,128)}, u32[]{:S(2)}) %copy-start.6) | copy-done | bytes 65560
  3.9 0.1 shard_map.77
  4.0 0.0 copy-start.3
  4.0 7.1 %collective-permute-start.5 = (s16[256,128]{1,0:T(8,128)(2,1)S(1)}, s16[256,128]{1,0:T(8,128)(2,1)S(1)}, u32[]{:S(2)}, u32[]{:S(2)}) collective-permute-start(s16[256,128]{1,0:T(8,128)(2,1)S(1)} %get-tuple-element.13), channel_id=1, source_target_pairs={{0,32},{16,48},{32,64},{48,80},{64,96},{80,112},{96,128},{112,144}... | collective-permute-start | bytes 196616 | tf_op jit(solution)/shard_map/ppermute | solution.py:265
  11.1 3.5 %collective-permute-start.4 = (s16[256,128]{1,0:T(8,128)(2,1)S(1)}, s16[256,128]{1,0:T(8,128)(2,1)S(1)}, u32[]{:S(2)}, u32[]{:S(2)}) collective-permute-start(s16[256,128]{1,0:T(8,128)(2,1)S(1)} %get-tuple-element.13), channel_id=1, source_target_pairs={{0,16},{16,32},{32,48},{48,64},{64,80},{80,96},{96,112},{112,128},... | collective-permute-start | bytes 196616 | tf_op jit(solution)/shard_map/ppermute | solution.py:266
  14.7 2.6 %collective-permute-start = (bf16[96,128]{1,0:T(8,128)(2,1)S(1)}, bf16[96,128]{1,0:T(8,128)(2,1)S(1)}, u32[]{:S(2)}, u32[]{:S(2)}) collective-permute-start(bf16[96,128]{1,0:T(8,128)(2,1)S(1)} %get-tuple-element.9), channel_id=1, source_target_pairs={{0,16},{16,32},{32,48},{48,64},{64,80},{80,96},{96,112},{112,128},... | collective-permute-start | bytes 73736 | tf_op jit(solution)/shard_map/ppermute | solution.py:267
  17.3 2.6 %collective-permute-start.1 = (bf16[96,128]{1,0:T(8,128)(2,1)S(1)}, bf16[96,128]{1,0:T(8,128)(2,1)S(1)}, u32[]{:S(2)}, u32[]{:S(2)}) collective-permute-start(bf16[96,128]{1,0:T(8,128)(2,1)S(1)} %get-tuple-element.10), channel_id=1, source_target_pairs={{0,496},{16,0},{32,16},{48,32},{64,48},{80,64},{96,80},{112,96},{1... | collective-permute-start | bytes 73736 | tf_op jit(solution)/shard_map/ppermute | solution.py:268
  20.0 0.1 pad_add_fusion.par_ref
  20.0 0.0 collective-permute-done.lo_ref
  20.0 9.3 %collective-permute-done.1.hi_ref = bf16[96,128]{1,0:T(8,128)(2,1)S(1)} collective-permute-done((bf16[96,128]{1,0:T(8,128)(2,1)S(1)}, bf16[96,128]{1,0:T(8,128)(2,1)S(1)}, u32[]{:S(2)}, u32[]{:S(2)}) %collective-permute-start.1) | collective-permute-done | bytes 24608 | tf_op jit(solution)/shard_map/ppermute | solution.py:268
  29.4 0.7 %shard_map.78 = (bf16[32,128]{1,0:T(8,128)(2,1)S(1)}, bf16[32,128]{1,0:T(8,128)(2,1)S(1)}) custom-call(s32[2]{0:T(128)S(1)} %pad_add_fusion.par_ref, bf16[3,64,128]{2,1,0:T(8,128)(2,1)S(1)} %bitcast.13, s32[64,128]{1,0:T(8,128)S(1)} %bitcast.16, bf16[96,128]{1,0:T(8,128)(2,1)S(1)} %collective-permute-done.lo_ref, ...), custom_call_target="tpu_custom_call" | custom-call | tf_op jit(solution)/shard_map/pallas_call | solution.py:269
  30.1 4.6 %collective-permute-start.2 = (bf16[32,128]{1,0:T(8,128)(2,1)S(1)}, bf16[32,128]{1,0:T(8,128)(2,1)S(1)}, u32[]{:S(2)}, u32[]{:S(2)}) collective-permute-start(bf16[32,128]{1,0:T(8,128)(2,1)S(1)} %get-tuple-element.11), channel_id=1, source_target_pairs={{0,1},{1,0},{2,3},{3,2},{4,5},{5,4},{6,7},{7,6},{8,9},{9,8},{10,11... | collective-permute-start | bytes 24584 | tf_op jit(solution)/shard_map/ppermute | solution.py:270
  34.6 1.9 %collective-permute-start.3 = (bf16[32,128]{1,0:T(8,128)(2,1)S(1)}, bf16[32,128]{1,0:T(8,128)(2,1)S(1)}, u32[]{:S(2)}, u32[]{:S(2)}) collective-permute-start(bf16[32,128]{1,0:T(8,128)(2,1)S(1)} %get-tuple-element.12), channel_id=1, source_target_pairs={{0,15},{1,2},{2,1},{3,4},{4,3},{5,6},{6,5},{7,8},{8,7},{9,10},{10,... | collective-permute-start | bytes 24584 | tf_op jit(solution)/shard_map/ppermute | solution.py:271
  36.6 0.0 collective-permute-done.2.near_ref
  36.6 13.9 %collective-permute-done.3.far_ref = bf16[32,128]{1,0:T(8,128)(2,1)S(1)} collective-permute-done((bf16[32,128]{1,0:T(8,128)(2,1)S(1)}, bf16[32,128]{1,0:T(8,128)(2,1)S(1)}, u32[]{:S(2)}, u32[]{:S(2)}) %collective-permute-start.3) | collective-permute-done | bytes 8224 | tf_op jit(solution)/shard_map/ppermute | solution.py:271
  50.4 0.0 collective-permute-done.5
  50.4 0.0 collective-permute-done.4
  50.4 0.0 copy-done.9
  50.5 0.0 copy-done.5
  50.5 3.1 %shard_map.79 = (f32[6,64,128]{2,1,0:T(8,128)}, f32[4,64,128]{2,1,0:T(8,128)}) custom-call(s32[2]{0:T(128)S(1)} %pad_add_fusion.par_ref, bf16[3,64,128]{2,1,0:T(8,128)(2,1)S(1)} %bitcast.14, s32[64,128]{1,0:T(8,128)S(1)} %bitcast.17, s32[64,128]{1,0:T(8,128)S(1)} %bitcast.24, bf16[96,128]{1,0:T(8,128)(2,1)S(1)} %collective-permute-done.lo_ref, ...), custom_call_target="tpu_custom_call" | custom-call | tf_op jit(solution)/shard_map/pallas_call | solution.py:272
  (12 shorter events, 0.0 us)
Async XLA Ops:
  0.6 0.8 %copy-start = (bf16[3,8,8,128]{3,2,1,0:T(8,128)(2,1)S(1)}, bf16[3,8,8,128]{3,2,1,0:T(8,128)(2,1)}, u32[]{:S(2)}) copy-start(bf16[3,8,8,128]{3,2,1,0:T(8,128)(2,1)} %param.6) | copy-start | bytes 147460
  1.4 0.8 %copy-start.2 = (s32[8,8,128]{2,1,0:T(8,128)S(1)}, s32[8,8,128]{2,1,0:T(8,128)}, u32[]{:S(2)}) copy-start(s32[8,8,128]{2,1,0:T(8,128)} %param.10) | copy-start | bytes 98308
  2.2 0.8 %copy-start.4 = (f32[2,8,8,128]{3,2,1,0:T(8,128)S(1)}, f32[2,8,8,128]{3,2,1,0:T(8,128)}, u32[]{:S(2)}) copy-start(f32[2,8,8,128]{3,2,1,0:T(8,128)} %param.7) | copy-start | bytes 196612
  3.0 0.8 %copy-start.6 = (f32[2,8,8,128]{3,2,1,0:T(8,128)S(1)}, f32[2,8,8,128]{3,2,1,0:T(8,128)}, u32[]{:S(2)}) copy-start(f32[2,8,8,128]{3,2,1,0:T(8,128)} %param.8) | copy-start | bytes 196612
  3.9 25.5 %copy-start.1 = (bf16[3,8,8,128]{3,2,1,0:T(8,128)(2,1)S(1)}, bf16[3,8,8,128]{3,2,1,0:T(8,128)(2,1)}, u32[]{:S(2)}) copy-start(bf16[3,8,8,128]{3,2,1,0:T(8,128)(2,1)} %param.6) | copy-start | bytes 147460
  3.9 46.6 %copy-start.8 = (s32[8,8,128]{2,1,0:T(8,128)S(1)}, s32[8,8,128]{2,1,0:T(8,128)}, u32[]{:S(2)}) copy-start(s32[8,8,128]{2,1,0:T(8,128)} %param.11) | copy-start | bytes 98308
  3.9 46.6 %copy-start.9 = (s32[8,8,16]{2,1,0:T(8,128)S(1)}, s32[8,8,16]{2,1,0:T(8,128)}, u32[]{:S(2)}) copy-start(s32[8,8,16]{2,1,0:T(8,128)} %param.9) | copy-start | bytes 12292
  4.0 25.4 %copy-start.3 = (s32[8,8,128]{2,1,0:T(8,128)S(1)}, s32[8,8,128]{2,1,0:T(8,128)}, u32[]{:S(2)}) copy-start(s32[8,8,128]{2,1,0:T(8,128)} %param.10) | copy-start | bytes 98308
  4.0 46.4 %collective-permute-start.5 = (s16[256,128]{1,0:T(8,128)(2,1)S(1)}, s16[256,128]{1,0:T(8,128)(2,1)S(1)}, u32[]{:S(2)}, u32[]{:S(2)}) collective-permute-start(s16[256,128]{1,0:T(8,128)(2,1)S(1)} %get-tuple-element.13), channel_id=1, source_target_pairs={{0,32},{16,48},{32,64},{48,80},{64,96},{80,112},{96,128},{112,144}... | collective-permute-start | bytes 196616 | tf_op jit(solution)/shard_map/ppermute | solution.py:265
  11.1 39.3 %collective-permute-start.4 = (s16[256,128]{1,0:T(8,128)(2,1)S(1)}, s16[256,128]{1,0:T(8,128)(2,1)S(1)}, u32[]{:S(2)}, u32[]{:S(2)}) collective-permute-start(s16[256,128]{1,0:T(8,128)(2,1)S(1)} %get-tuple-element.13), channel_id=1, source_target_pairs={{0,16},{16,32},{32,48},{48,64},{64,80},{80,96},{96,112},{112,128},... | collective-permute-start | bytes 196616 | tf_op jit(solution)/shard_map/ppermute | solution.py:266
  14.7 5.4 %collective-permute-start = (bf16[96,128]{1,0:T(8,128)(2,1)S(1)}, bf16[96,128]{1,0:T(8,128)(2,1)S(1)}, u32[]{:S(2)}, u32[]{:S(2)}) collective-permute-start(bf16[96,128]{1,0:T(8,128)(2,1)S(1)} %get-tuple-element.9), channel_id=1, source_target_pairs={{0,16},{16,32},{32,48},{48,64},{64,80},{80,96},{96,112},{112,128},... | collective-permute-start | bytes 73736 | tf_op jit(solution)/shard_map/ppermute | solution.py:267
  17.3 12.1 %collective-permute-start.1 = (bf16[96,128]{1,0:T(8,128)(2,1)S(1)}, bf16[96,128]{1,0:T(8,128)(2,1)S(1)}, u32[]{:S(2)}, u32[]{:S(2)}) collective-permute-start(bf16[96,128]{1,0:T(8,128)(2,1)S(1)} %get-tuple-element.10), channel_id=1, source_target_pairs={{0,496},{16,0},{32,16},{48,32},{64,48},{80,64},{96,80},{112,96},{1... | collective-permute-start | bytes 73736 | tf_op jit(solution)/shard_map/ppermute | solution.py:268
  20.0 30.4 %copy-start.5 = (f32[2,8,8,128]{3,2,1,0:T(8,128)S(1)}, f32[2,8,8,128]{3,2,1,0:T(8,128)}, u32[]{:S(2)}) copy-start(f32[2,8,8,128]{3,2,1,0:T(8,128)} %param.7) | copy-start | bytes 196612
  20.0 30.4 %copy-start.7 = (f32[2,8,8,128]{3,2,1,0:T(8,128)S(1)}, f32[2,8,8,128]{3,2,1,0:T(8,128)}, u32[]{:S(2)}) copy-start(f32[2,8,8,128]{3,2,1,0:T(8,128)} %param.8) | copy-start | bytes 196612
  30.1 6.5 %collective-permute-start.2 = (bf16[32,128]{1,0:T(8,128)(2,1)S(1)}, bf16[32,128]{1,0:T(8,128)(2,1)S(1)}, u32[]{:S(2)}, u32[]{:S(2)}) collective-permute-start(bf16[32,128]{1,0:T(8,128)(2,1)S(1)} %get-tuple-element.11), channel_id=1, source_target_pairs={{0,1},{1,0},{2,3},{3,2},{4,5},{5,4},{6,7},{7,6},{8,9},{9,8},{10,11... | collective-permute-start | bytes 24584 | tf_op jit(solution)/shard_map/ppermute | solution.py:270
  34.6 15.8 %collective-permute-start.3 = (bf16[32,128]{1,0:T(8,128)(2,1)S(1)}, bf16[32,128]{1,0:T(8,128)(2,1)S(1)}, u32[]{:S(2)}, u32[]{:S(2)}) collective-permute-start(bf16[32,128]{1,0:T(8,128)(2,1)S(1)} %get-tuple-element.12), channel_id=1, source_target_pairs={{0,15},{1,2},{2,1},{3,4},{4,3},{5,6},{6,5},{7,8},{8,7},{9,10},{10,... | collective-permute-start | bytes 24584 | tf_op jit(solution)/shard_map/ppermute | solution.py:271

commit v2 on v1

--- a/solution.py
+++ b/solution.py
@@ -14,6 +14,7 @@
 F32 = jnp.float32
 BF16 = jnp.bfloat16
 VMEM_LIMIT = 32 * 1024 * 1024
+PACK_LIMIT = 60 * 1024 * 1024
 
 
 def row(ref, x, lead=None):
@@ -39,17 +40,33 @@
     return jnp.where(y < 0, -y2, y2) * y2
 
 
-def pack_kernel(vel_ref, solid_ref, lq_ref, mn_ref, head_ref, tail_ref, kept_ref, scratch):
-    masked_rows(vel_ref, solid_ref, scratch)
-    for first, out in ((0, head_ref), (4, tail_ref)):
-        rows = [row(scratch, first + x, c) for c in range(3) for x in range(4)]
-        out[...] = jnp.concatenate(rows, axis=0).astype(BF16)
-    kept_ref[pl.ds(0, 128), :] = encode(lq_ref[...])
-    kept_ref[pl.ds(128, 128), :] = encode(mn_ref[...])
+def pack_kernel(vel_hbm, solid_hbm, lq_hbm, mn_hbm, head_ref, tail_ref, kept_ref, vel, solid, kept, scratch, sems):
+    copies = [
+        pltpu.make_async_copy(vel_hbm, vel, sems.at[0]),
+        pltpu.make_async_copy(solid_hbm, solid, sems.at[1]),
+        pltpu.make_async_copy(lq_hbm, kept.at[pl.ds(0, 128)], sems.at[2]),
+        pltpu.make_async_copy(mn_hbm, kept.at[pl.ds(128, 128)], sems.at[3]),
+    ]
+    for copy in copies:
+        copy.start()
+    copies[0].wait()
+    copies[1].wait()
+    masked_rows(vel, solid, scratch)
+    head = [row(scratch, x, c) for c in range(3) for x in range(4)]
+    head_ref[...] = jnp.concatenate(head, axis=0).astype(BF16)
+    tail = [row(scratch, 4 + x, c) for c in range(3) for x in range(4)]
+    tail_ref[pl.ds(0, 96), :] = jnp.concatenate(tail, axis=0).astype(BF16)
+    copies[2].wait()
+    copies[3].wait()
+    old = kept[...]
+    kept_ref[...] = encode(old)
+    high = old.astype(BF16)
+    tail_ref[pl.ds(96, 256), :] = high
+    tail_ref[pl.ds(352, 256), :] = (old - high.astype(F32)).astype(BF16)
 
 
 def halo_rows(scratch, lo_ref, hi_ref):
-    lo = lo_ref[...].astype(F32).reshape(3, 4, 8, 128)
+    lo = lo_ref[pl.ds(0, 96), :].astype(F32).reshape(3, 4, 8, 128)
     hi = hi_ref[...].astype(F32).reshape(3, 4, 8, 128)
     out = []
     for c in range(3):
@@ -60,7 +77,7 @@
     return out
 
 
-def strip_kernel(par_ref, vel_ref, solid_ref, lo_ref, hi_ref, near_ref, far_ref, scratch):
+def strip_kernel(par_ref, vel_ref, solid_ref, lo_ref, hi_ref, far_ref, near_ref, scratch):
     masked_rows(vel_ref, solid_ref, scratch)
     rows = halo_rows(scratch, lo_ref, hi_ref)
     lane = lax.broadcasted_iota(jnp.int32, (8, 128), 1)
@@ -110,8 +127,8 @@
     return r / (1.0 + r)
 
 
-def main_kernel(par_ref, vel_ref, solid_ref, clip_ref, lo_ref, hi_ref, near_ref, far_ref, src_ref,
-                lq_ref, mn_ref, up1_ref, up2_ref, stress_ref, new_ref, scratch, old):
+def main_kernel(par_ref, vel_ref, solid_ref, clip_ref, lo_ref, hi_ref, far_ref, near_ref, src_ref,
+                lq_ref, mn_ref, up2_ref, stress_ref, new_ref, scratch, old):
     lane = lax.broadcasted_iota(jnp.int32, (8, 128), 1)
     sub = lax.broadcasted_iota(jnp.int32, (8, 128), 0)
     here = lax.broadcasted_iota(jnp.int32, (64, 16), 0) % 8
@@ -119,17 +136,20 @@
     spread = (lax.broadcasted_iota(jnp.int32, (16, 128), 1) // 8 == lax.broadcasted_iota(jnp.int32, (16, 128), 0))
     local = jnp.dot((16 + here - back).astype(F32), spread.astype(F32), preferred_element_type=F32)
     local = (local + 0.5).astype(jnp.int32)
+    one_high = lo_ref[pl.ds(96, 256), :].astype(F32).reshape(4, 64, 128)
+    one_low = lo_ref[pl.ds(352, 256), :].astype(F32).reshape(4, 64, 128)
+    up2 = decode(up2_ref[...]).reshape(4, 64, 128)
     for z in range(8):
         at = pl.ds(8 * z, 8)
         idx = local[8 * z : 8 * z + 8]
         inner = idx & 7
         for f in range(4):
-            rows = pl.ds(64 * f + 8 * z, 8)
             own_ref = lq_ref if f < 2 else mn_ref
             own = own_ref[pl.ds(64 * (f % 2) + 8 * z, 8), :]
             got = jnp.take_along_axis(own, inner, axis=0)
-            one = jnp.take_along_axis(decode(up1_ref[f, at, :]), inner, axis=0)
-            two = jnp.take_along_axis(decode(up2_ref[f, at, :]), inner, axis=0)
+            up1 = one_high[f, 8 * z : 8 * z + 8] + one_low[f, 8 * z : 8 * z + 8]
+            one = jnp.take_along_axis(up1, inner, axis=0)
+            two = jnp.take_along_axis(up2[f, 8 * z : 8 * z + 8], inner, axis=0)
             old[f, at, :] = jnp.where(idx < 8, two, jnp.where(idx < 16, one, got))
     masked_rows(vel_ref, solid_ref, scratch)
     core = halo_rows(scratch, lo_ref, hi_ref)
@@ -235,12 +255,13 @@
 
 SMEM = pl.BlockSpec(memory_space=pltpu.SMEM)
 VM = pl.BlockSpec(memory_space=pltpu.VMEM)
-
-
-def call(kernel, outs, specs, scratch):
+HBM = pl.BlockSpec(memory_space=pltpu.HBM)
+
+
+def call(kernel, outs, specs, scratch, limit=VMEM_LIMIT):
     return pl.pallas_call(
         kernel, out_shape=outs, in_specs=specs, out_specs=[VM] * len(outs), scratch_shapes=scratch,
-        compiler_params=pltpu.CompilerParams(vmem_limit_bytes=VMEM_LIMIT),
+        compiler_params=pltpu.CompilerParams(vmem_limit_bytes=limit),
     )
 
 
@@ -260,19 +281,23 @@
     par = jnp.stack([gy % 2, gx * 8]).astype(jnp.int32)
     trans = pltpu.VMEM((3, 64, 128), F32)
     head, tail, kept = call(
-        pack_kernel, [sds((96, 128), BF16), sds((96, 128), BF16), sds((256, 128), jnp.int16)], [VM] * 4, [trans]
+        pack_kernel,
+        [sds((96, 128), BF16), sds((608, 128), BF16), sds((256, 128), jnp.int16)],
+        [HBM] * 4,
+        [pltpu.VMEM((3, 64, 128), BF16), pltpu.VMEM((64, 128), jnp.int32), pltpu.VMEM((256, 128), F32), trans,
+         pltpu.SemaphoreType.DMA((4,))],
+        PACK_LIMIT,
     )(vel, solid, lq, mn)
-    up2 = lax.ppermute(kept, "gx", ring(32, 2))
-    up1 = lax.ppermute(kept, "gx", ring(32, 1))
     lo = lax.ppermute(tail, "gx", ring(32, 1))
     hi = lax.ppermute(head, "gx", ring(32, -1))
-    near, far = call(strip_kernel, [sds((32, 128), BF16)] * 2, [SMEM] + [VM] * 4, [trans])(par, vel, solid, lo, hi)
+    up2 = lax.ppermute(kept, "gx", ring(32, 2))
+    far, near = call(strip_kernel, [sds((32, 128), BF16)] * 2, [SMEM] + [VM] * 4, [trans])(par, vel, solid, lo, hi)
+    far = lax.ppermute(far, "gy", [(i, (i + 1) % 16 if i % 2 else (i - 1) % 16) for i in range(16)])
     near = lax.ppermute(near, "gy", [(i, i ^ 1) for i in range(16)])
-    far = lax.ppermute(far, "gy", [(i, (i + 1) % 16 if i % 2 else (i - 1) % 16) for i in range(16)])
     stress, new = call(
-        main_kernel, [sds((6, 64, 128), F32), sds((4, 64, 128), F32)], [SMEM] + [VM] * 12,
+        main_kernel, [sds((6, 64, 128), F32), sds((4, 64, 128), F32)], [SMEM] + [VM] * 11,
         [trans, pltpu.VMEM((4, 64, 128), F32)],
-    )(par, vel, solid, clip, lo, hi, near, far, src, lq, mn, up1.reshape(4, 64, 128), up2.reshape(4, 64, 128))
+    )(par, vel, solid, clip, lo, hi, far, near, src, lq, mn, up2)
     return stress.reshape(6, 8, 8, 128), new.reshape(4, 8, 8, 128)
 
 

time: 54.1 us -> 44.1 us (0.82)
  the two profiles are of different devices: /device:TPU:495 before, /device:TPU:1 now
where the time goes in v2:
time: 44.1 us; the launch traced here: 43.8 us
  starting transfers between devices  36.7 us (83%)
  Pallas kernels  5.42 us (12%)
  waiting for transfers between devices  0.8 us (2%)
  between operations  0.77 us (2%)
    ppermute x1, starting transfers between devices, local(): hi = lax.ppermute(head, 'gx', ring(32, -1))  13.7 us
    ppermute x1, starting transfers between devices, local(): lax.ppermute(far, 'gy', [(i, (i + 1) % 16 if i % 2 else (i - 1) % 16) for...  13.6 us
    ppermute x1, starting transfers between devices, local(): lo = lax.ppermute(tail, 'gx', ring(32, 1))  4.37 us
    ppermute x1, starting transfers between devices, local(): near = lax.ppermute(near, 'gy', [(i, i ^ 1) for i in range(16)])  3.12 us
    pallas_call x1, Pallas kernels, local(): call(main_kernel, [sds((6, 64, 128), F32), sds((4, 64, 128), F32)], [SMEM...  3.05 us
    ppermute x1, starting transfers between devices, local(): up2 = lax.ppermute(kept, 'gx', ring(32, 2))  1.92 us
    pallas_call x1, Pallas kernels, local(): call(pack_kernel, [sds((96, 128), BF16), sds((608, 128), BF16), sds((256,...  1.7 us
  transfers between devices with their start and end apart: 5, of which 1 were waited for; matrix products, arithmetic and copies ran while one was open for 0% of the time, Pallas kernels for 2%

profile of v2, /device:TPU:1, one launch (start us, length us, event | category | flops | bytes accessed | tf_op | source)
XLA Modules:
  0.0 43.8 jit_solution(1811647774968214608)
XLA Ops:
  0.6 0.0 copy-start
  0.6 1.7 %shard_map.77 = (bf16[96,128]{1,0:T(8,128)(2,1)}, bf16[608,128]{1,0:T(8,128)(2,1)}, s16[256,128]{1,0:T(8,128)(2,1)}) custom-call(bf16[3,64,128]{2,1,0:T(8,128)(2,1)} %bitcast.10, s32[64,128]{1,0:T(8,128)} %bitcast.13, f32[128,128]{1,0:T(8,128)} %bitcast.16, f32[128,128]{1,0:T(8,128)} %bitcast.18), custom_call_target="tpu_custom_call" | custom-call | tf_op jit(solution)/shard_map/pallas_call | solution.py:283
  2.3 0.0 copy-start.1
  2.4 4.4 %collective-permute-start = (bf16[608,128]{1,0:T(8,128)(2,1)}, bf16[608,128]{1,0:T(8,128)(2,1)S(1)}, u32[]{:S(2)}, u32[]{:S(2)}) collective-permute-start(bf16[608,128]{1,0:T(8,128)(2,1)} %get-tuple-element.9), channel_id=1, source_target_pairs={{0,16},{16,32},{32,48},{48,64},{64,80},{80,96},{96,112},{112,128},... | collective-permute-start | bytes 466952 | tf_op jit(solution)/shard_map/ppermute | solution.py:291
  6.7 13.7 %collective-permute-start.1 = (bf16[96,128]{1,0:T(8,128)(2,1)}, bf16[96,128]{1,0:T(8,128)(2,1)S(1)}, u32[]{:S(2)}, u32[]{:S(2)}) collective-permute-start(bf16[96,128]{1,0:T(8,128)(2,1)} %get-tuple-element.10), channel_id=1, source_target_pairs={{0,496},{16,0},{32,16},{48,32},{64,48},{80,64},{96,80},{112,96},{1... | collective-permute-start | bytes 73736 | tf_op jit(solution)/shard_map/ppermute | solution.py:292
  20.5 1.9 %collective-permute-start.4 = (s16[256,128]{1,0:T(8,128)(2,1)}, s16[256,128]{1,0:T(8,128)(2,1)S(1)}, u32[]{:S(2)}, u32[]{:S(2)}) collective-permute-start(s16[256,128]{1,0:T(8,128)(2,1)} %get-tuple-element.13), channel_id=1, source_target_pairs={{0,32},{16,48},{32,64},{48,80},{64,96},{80,112},{96,128},{112,144}... | collective-permute-start | bytes 196616 | tf_op jit(solution)/shard_map/ppermute | solution.py:293
  22.4 0.1 pad_add_fusion.par_ref
  22.5 0.0 copy-start.2
  22.5 0.0 copy-start.3
  22.5 0.0 collective-permute-done.1.hi_ref
  22.5 0.0 collective-permute-done.lo_ref
  22.5 0.0 copy-done
  22.5 0.0 copy-done.1
  22.5 0.7 %shard_map.78 = (bf16[32,128]{1,0:T(8,128)(2,1)S(1)}, bf16[32,128]{1,0:T(8,128)(2,1)S(1)}) custom-call(s32[2]{0:T(128)S(1)} %pad_add_fusion.par_ref, bf16[3,64,128]{2,1,0:T(8,128)(2,1)S(1)} %bitcast.11, s32[64,128]{1,0:T(8,128)S(1)} %bitcast.14, bf16[608,128]{1,0:T(8,128)(2,1)S(1)} %collective-permute-done.lo_ref, ...), custom_call_target="tpu_custom_call" | custom-call | tf_op jit(solution)/shard_map/pallas_call | solution.py:294
  23.2 13.6 %collective-permute-start.2 = (bf16[32,128]{1,0:T(8,128)(2,1)S(1)}, bf16[32,128]{1,0:T(8,128)(2,1)S(1)}, u32[]{:S(2)}, u32[]{:S(2)}) collective-permute-start(bf16[32,128]{1,0:T(8,128)(2,1)S(1)} %get-tuple-element.11), channel_id=1, source_target_pairs={{0,15},{1,2},{2,1},{3,4},{4,3},{5,6},{6,5},{7,8},{8,7},{9,10},{10,... | collective-permute-start | bytes 24584 | tf_op jit(solution)/shard_map/ppermute | solution.py:295
  36.8 3.1 %collective-permute-start.3 = (bf16[32,128]{1,0:T(8,128)(2,1)S(1)}, bf16[32,128]{1,0:T(8,128)(2,1)S(1)}, u32[]{:S(2)}, u32[]{:S(2)}) collective-permute-start(bf16[32,128]{1,0:T(8,128)(2,1)S(1)} %get-tuple-element.12), channel_id=1, source_target_pairs={{0,1},{1,0},{2,3},{3,2},{4,5},{5,4},{6,7},{7,6},{8,9},{9,8},{10,11... | collective-permute-start | bytes 24584 | tf_op jit(solution)/shard_map/ppermute | solution.py:296
  39.9 0.0 collective-permute-done.4.up2_ref
  39.9 0.0 collective-permute-done.2.far_ref
  39.9 0.8 %collective-permute-done.3.near_ref = bf16[32,128]{1,0:T(8,128)(2,1)S(1)} collective-permute-done((bf16[32,128]{1,0:T(8,128)(2,1)S(1)}, bf16[32,128]{1,0:T(8,128)(2,1)S(1)}, u32[]{:S(2)}, u32[]{:S(2)}) %collective-permute-start.3) | collective-permute-done | bytes 8224 | tf_op jit(solution)/shard_map/ppermute | solution.py:296
  40.7 0.0 copy-done.2
  40.7 0.0 copy-done.3
  40.7 0.0 copy-done.4
  40.7 0.0 copy-done.5
  40.7 3.1 %shard_map.79 = (f32[6,64,128]{2,1,0:T(8,128)}, f32[4,64,128]{2,1,0:T(8,128)}) custom-call(s32[2]{0:T(128)S(1)} %pad_add_fusion.par_ref, bf16[3,64,128]{2,1,0:T(8,128)(2,1)S(1)} %bitcast.12, s32[64,128]{1,0:T(8,128)S(1)} %bitcast.15, s32[64,128]{1,0:T(8,128)S(1)} %bitcast.20, bf16[608,128]{1,0:T(8,128)(2,1)S(1)} %collective-permute-done.lo_ref, ...), custom_call_target="tpu_custom_call" | custom-call | tf_op jit(solution)/shard_map/pallas_call | solution.py:297
  (2 shorter events, 0.0 us)
Async XLA Ops:
  0.6 21.9 %copy-start = (bf16[3,8,8,128]{3,2,1,0:T(8,128)(2,1)S(1)}, bf16[3,8,8,128]{3,2,1,0:T(8,128)(2,1)}, u32[]{:S(2)}) copy-start(bf16[3,8,8,128]{3,2,1,0:T(8,128)(2,1)} %param.6) | copy-start | bytes 147460
  2.3 20.2 %copy-start.1 = (s32[8,8,128]{2,1,0:T(8,128)S(1)}, s32[8,8,128]{2,1,0:T(8,128)}, u32[]{:S(2)}) copy-start(s32[8,8,128]{2,1,0:T(8,128)} %param.10) | copy-start | bytes 98308
  2.4 20.1 %collective-permute-start = (bf16[608,128]{1,0:T(8,128)(2,1)}, bf16[608,128]{1,0:T(8,128)(2,1)S(1)}, u32[]{:S(2)}, u32[]{:S(2)}) collective-permute-start(bf16[608,128]{1,0:T(8,128)(2,1)} %get-tuple-element.9), channel_id=1, source_target_pairs={{0,16},{16,32},{32,48},{48,64},{64,80},{80,96},{96,112},{112,128},... | collective-permute-start | bytes 466952 | tf_op jit(solution)/shard_map/ppermute | solution.py:291
  6.7 15.7 %collective-permute-start.1 = (bf16[96,128]{1,0:T(8,128)(2,1)}, bf16[96,128]{1,0:T(8,128)(2,1)S(1)}, u32[]{:S(2)}, u32[]{:S(2)}) collective-permute-start(bf16[96,128]{1,0:T(8,128)(2,1)} %get-tuple-element.10), channel_id=1, source_target_pairs={{0,496},{16,0},{32,16},{48,32},{64,48},{80,64},{96,80},{112,96},{1... | collective-permute-start | bytes 73736 | tf_op jit(solution)/shard_map/ppermute | solution.py:292
  20.5 19.4 %collective-permute-start.4 = (s16[256,128]{1,0:T(8,128)(2,1)}, s16[256,128]{1,0:T(8,128)(2,1)S(1)}, u32[]{:S(2)}, u32[]{:S(2)}) collective-permute-start(s16[256,128]{1,0:T(8,128)(2,1)} %get-tuple-element.13), channel_id=1, source_target_pairs={{0,32},{16,48},{32,64},{48,80},{64,96},{80,112},{96,128},{112,144}... | collective-permute-start | bytes 196616 | tf_op jit(solution)/shard_map/ppermute | solution.py:293
  22.5 18.2 %copy-start.2 = (f32[2,8,8,128]{3,2,1,0:T(8,128)S(1)}, f32[2,8,8,128]{3,2,1,0:T(8,128)}, u32[]{:S(2)}) copy-start(f32[2,8,8,128]{3,2,1,0:T(8,128)} %param.7) | copy-start | bytes 196612
  22.5 18.2 %copy-start.3 = (f32[2,8,8,128]{3,2,1,0:T(8,128)S(1)}, f32[2,8,8,128]{3,2,1,0:T(8,128)}, u32[]{:S(2)}) copy-start(f32[2,8,8,128]{3,2,1,0:T(8,128)} %param.8) | copy-start | bytes 196612
  22.5 18.2 %copy-start.4 = (s32[8,8,128]{2,1,0:T(8,128)S(1)}, s32[8,8,128]{2,1,0:T(8,128)}, u32[]{:S(2)}) copy-start(s32[8,8,128]{2,1,0:T(8,128)} %param.11) | copy-start | bytes 98308
  22.5 18.2 %copy-start.5 = (s32[8,8,16]{2,1,0:T(8,128)S(1)}, s32[8,8,16]{2,1,0:T(8,128)}, u32[]{:S(2)}) copy-start(s32[8,8,16]{2,1,0:T(8,128)} %param.9) | copy-start | bytes 12292
  23.2 16.7 %collective-permute-start.2 = (bf16[32,128]{1,0:T(8,128)(2,1)S(1)}, bf16[32,128]{1,0:T(8,128)(2,1)S(1)}, u32[]{:S(2)}, u32[]{:S(2)}) collective-permute-start(bf16[32,128]{1,0:T(8,128)(2,1)S(1)} %get-tuple-element.11), channel_id=1, source_target_pairs={{0,15},{1,2},{2,1},{3,4},{4,3},{5,6},{6,5},{7,8},{8,7},{9,10},{10,... | collective-permute-start | bytes 24584 | tf_op jit(solution)/shard_map/ppermute | solution.py:295
  36.8 3.9 %collective-permute-start.3 = (bf16[32,128]{1,0:T(8,128)(2,1)S(1)}, bf16[32,128]{1,0:T(8,128)(2,1)S(1)}, u32[]{:S(2)}, u32[]{:S(2)}) collective-permute-start(bf16[32,128]{1,0:T(8,128)(2,1)S(1)} %get-tuple-element.12), channel_id=1, source_target_pairs={{0,1},{1,0},{2,3},{3,2},{4,5},{5,4},{6,7},{7,6},{8,9},{9,8},{10,11... | collective-permute-start | bytes 24584 | tf_op jit(solution)/shard_map/ppermute | solution.py:296

commit v3 on v2

--- a/solution.py
+++ b/solution.py
@@ -15,6 +15,7 @@
 BF16 = jnp.bfloat16
 VMEM_LIMIT = 32 * 1024 * 1024
 PACK_LIMIT = 60 * 1024 * 1024
+STRIP_FLOPS = 1_000_000_000
 
 
 def row(ref, x, lead=None):
@@ -77,7 +78,7 @@
     return out
 
 
-def strip_kernel(par_ref, vel_ref, solid_ref, lo_ref, hi_ref, far_ref, near_ref, scratch):
+def strip_kernel(vel_ref, solid_ref, lo_ref, hi_ref, far_ref, near_ref, scratch):
     masked_rows(vel_ref, solid_ref, scratch)
     rows = halo_rows(scratch, lo_ref, hi_ref)
     lane = lax.broadcasted_iota(jnp.int32, (8, 128), 1)
@@ -93,7 +94,7 @@
         right.append(rights)
     left = jnp.concatenate(left + [jnp.zeros((8, 128), F32)], axis=0)
     right = jnp.concatenate(right + [jnp.zeros((8, 128), F32)], axis=0)
-    even = par_ref[0] == 0
+    even = lax.axis_index("gy") % 2 == 0
     near_ref[...] = jnp.where(even, right, left).astype(BF16)
     far_ref[...] = jnp.where(even, left, right).astype(BF16)
 
@@ -123,16 +124,16 @@
 
 
 def relax_weight(product):
-    r = RATE_SCALE * jnp.sqrt(jnp.sqrt(jnp.sqrt(jnp.maximum(product, PRODUCT_FLOOR))))
-    return r / (1.0 + r)
-
-
-def main_kernel(par_ref, vel_ref, solid_ref, clip_ref, lo_ref, hi_ref, far_ref, near_ref, src_ref,
+    inverse = lax.rsqrt(lax.rsqrt(lax.rsqrt(jnp.maximum(product, PRODUCT_FLOOR))))
+    return 1.0 / (1.0 + (1.0 / RATE_SCALE) * inverse)
+
+
+def main_kernel(vel_ref, solid_ref, clip_ref, lo_ref, hi_ref, far_ref, near_ref, src_ref,
                 lq_ref, mn_ref, up2_ref, stress_ref, new_ref, scratch, old):
     lane = lax.broadcasted_iota(jnp.int32, (8, 128), 1)
     sub = lax.broadcasted_iota(jnp.int32, (8, 128), 0)
     here = lax.broadcasted_iota(jnp.int32, (64, 16), 0) % 8
-    back = (par_ref[1] + here - src_ref[...] + 512) % 256
+    back = (lax.axis_index("gx") * 8 + here - src_ref[...] + 512) & 255
     spread = (lax.broadcasted_iota(jnp.int32, (16, 128), 1) // 8 == lax.broadcasted_iota(jnp.int32, (16, 128), 0))
     local = jnp.dot((16 + here - back).astype(F32), spread.astype(F32), preferred_element_type=F32)
     local = (local + 0.5).astype(jnp.int32)
@@ -155,7 +156,7 @@
     core = halo_rows(scratch, lo_ref, hi_ref)
     near = near_ref[...].astype(F32)
     far = far_ref[...].astype(F32)
-    even = par_ref[0] == 0
+    even = lax.axis_index("gy") % 2 == 0
     left = jnp.where(even, far, near).reshape(4, 8, 128)
     right = jnp.where(even, near, far).reshape(4, 8, 128)
     edge = []
@@ -253,15 +254,15 @@
             new_ref[(k,) + at] = v
 
 
-SMEM = pl.BlockSpec(memory_space=pltpu.SMEM)
 VM = pl.BlockSpec(memory_space=pltpu.VMEM)
 HBM = pl.BlockSpec(memory_space=pltpu.HBM)
 
 
-def call(kernel, outs, specs, scratch, limit=VMEM_LIMIT):
+def call(kernel, outs, specs, scratch, limit=VMEM_LIMIT, flops=0):
     return pl.pallas_call(
         kernel, out_shape=outs, in_specs=specs, out_specs=[VM] * len(outs), scratch_shapes=scratch,
         compiler_params=pltpu.CompilerParams(vmem_limit_bytes=limit),
+        cost_estimate=pl.CostEstimate(flops=flops, bytes_accessed=400_000, transcendentals=0),
     )
 
 
@@ -277,8 +278,6 @@
     lq = kept_lm_qn.reshape(128, 128)
     mn = kept_mm_nn.reshape(128, 128)
     src = back_src.reshape(64, 16)
-    gx, gy = lax.axis_index("gx"), lax.axis_index("gy")
-    par = jnp.stack([gy % 2, gx * 8]).astype(jnp.int32)
     trans = pltpu.VMEM((3, 64, 128), F32)
     head, tail, kept = call(
         pack_kernel,
@@ -291,13 +290,13 @@
     lo = lax.ppermute(tail, "gx", ring(32, 1))
     hi = lax.ppermute(head, "gx", ring(32, -1))
     up2 = lax.ppermute(kept, "gx", ring(32, 2))
-    far, near = call(strip_kernel, [sds((32, 128), BF16)] * 2, [SMEM] + [VM] * 4, [trans])(par, vel, solid, lo, hi)
+    far, near = call(strip_kernel, [sds((32, 128), BF16)] * 2, [VM] * 4, [trans], flops=STRIP_FLOPS)(vel, solid, lo, hi)
     far = lax.ppermute(far, "gy", [(i, (i + 1) % 16 if i % 2 else (i - 1) % 16) for i in range(16)])
     near = lax.ppermute(near, "gy", [(i, i ^ 1) for i in range(16)])
     stress, new = call(
-        main_kernel, [sds((6, 64, 128), F32), sds((4, 64, 128), F32)], [SMEM] + [VM] * 11,
+        main_kernel, [sds((6, 64, 128), F32), sds((4, 64, 128), F32)], [VM] * 11,
         [trans, pltpu.VMEM((4, 64, 128), F32)],
-    )(par, vel, solid, clip, lo, hi, far, near, src, lq, mn, up2)
+    )(vel, solid, clip, lo, hi, far, near, src, lq, mn, up2)
     return stress.reshape(6, 8, 8, 128), new.reshape(4, 8, 8, 128)
 
 

time: 44.1 us -> 43.1 us (0.977)
  Pallas kernels: 5.42 us -> 4.34 us
    pallas_call x2, Pallas kernels: 3.72 us -> 2.63 us  [the longest x1 2.51 us: local(): call(main_kernel, [sds((6, 64, 128), F32), sds((4, 64, 128), F32)], [VM]...]
  transfers between devices with their start and end apart: 5 -> 5, of which waited for: 1 -> 1; matrix products, arithmetic and copies ran while one was open for 0% -> 0% of each run, Pallas kernels for 2% -> 0%
where the time goes in v3:
time: 43.1 us; the launch traced here: 42.8 us
  starting transfers between devices  36.8 us (85%)
  Pallas kernels  4.34 us (10%)
  waiting for transfers between devices  0.8 us (2%)
  between operations  0.78 us (2%)
    ppermute x1, starting transfers between devices, local(): hi = lax.ppermute(head, 'gx', ring(32, -1))  13.7 us
    ppermute x1, starting transfers between devices, local(): lax.ppermute(far, 'gy', [(i, (i + 1) % 16 if i % 2 else (i - 1) % 16) for...  13.5 us
    ppermute x1, starting transfers between devices, local(): lo = lax.ppermute(tail, 'gx', ring(32, 1))  4.37 us
    ppermute x1, starting transfers between devices, local(): near = lax.ppermute(near, 'gy', [(i, i ^ 1) for i in range(16)])  3.17 us
    pallas_call x1, Pallas kernels, local(): call(main_kernel, [sds((6, 64, 128), F32), sds((4, 64, 128), F32)], [VM]...  2.51 us
    ppermute x1, starting transfers between devices, local(): up2 = lax.ppermute(kept, 'gx', ring(32, 2))  2.05 us
    pallas_call x1, Pallas kernels, local(): call(pack_kernel, [sds((96, 128), BF16), sds((608, 128), BF16), sds((256,...  1.7 us
  transfers between devices with their start and end apart: 5, of which 1 were waited for; matrix products, arithmetic and copies ran while one was open for 0% of the time, Pallas kernels for 0%

profile of v3, /device:TPU:1, one launch (start us, length us, event | category | flops | bytes accessed | tf_op | source)
XLA Modules:
  0.0 42.8 jit_solution(2234641443057898631)
XLA Ops:
  0.6 0.0 copy-start.2
  0.6 0.0 copy-start.3
  0.6 1.7 %shard_map.77 = (bf16[96,128]{1,0:T(8,128)(2,1)}, bf16[608,128]{1,0:T(8,128)(2,1)}, s16[256,128]{1,0:T(8,128)(2,1)}) custom-call(bf16[3,64,128]{2,1,0:T(8,128)(2,1)} %bitcast.12, s32[64,128]{1,0:T(8,128)} %bitcast.15, f32[128,128]{1,0:T(8,128)} %bitcast.8, f32[128,128]{1,0:T(8,128)} %bitcast.10), custom_call_target="tpu_custom_call" | custom-call | bytes 400000 | tf_op jit(solution)/shard_map/pallas_call | solution.py:282
  2.4 4.4 %collective-permute-start = (bf16[608,128]{1,0:T(8,128)(2,1)}, bf16[608,128]{1,0:T(8,128)(2,1)S(1)}, u32[]{:S(2)}, u32[]{:S(2)}) collective-permute-start(bf16[608,128]{1,0:T(8,128)(2,1)} %get-tuple-element.9), channel_id=1, source_target_pairs={{0,16},{16,32},{32,48},{48,64},{64,80},{80,96},{96,112},{112,128},... | collective-permute-start | bytes 466952 | tf_op jit(solution)/shard_map/ppermute | solution.py:290
  6.7 13.7 %collective-permute-start.1 = (bf16[96,128]{1,0:T(8,128)(2,1)}, bf16[96,128]{1,0:T(8,128)(2,1)S(1)}, u32[]{:S(2)}, u32[]{:S(2)}) collective-permute-start(bf16[96,128]{1,0:T(8,128)(2,1)} %get-tuple-element.10), channel_id=1, source_target_pairs={{0,496},{16,0},{32,16},{48,32},{64,48},{80,64},{96,80},{112,96},{1... | collective-permute-start | bytes 73736 | tf_op jit(solution)/shard_map/ppermute | solution.py:291
  20.5 0.0 copy-start
  20.5 0.0 copy-start.1
  20.5 0.0 copy-start.4
  20.5 0.0 copy-start.5
  20.5 2.1 %collective-permute-start.4 = (s16[256,128]{1,0:T(8,128)(2,1)}, s16[256,128]{1,0:T(8,128)(2,1)S(1)}, u32[]{:S(2)}, u32[]{:S(2)}) collective-permute-start(s16[256,128]{1,0:T(8,128)(2,1)} %get-tuple-element.13), channel_id=1, source_target_pairs={{0,32},{16,48},{32,64},{48,80},{64,96},{80,112},{96,128},{112,144}... | collective-permute-start | bytes 196616 | tf_op jit(solution)/shard_map/ppermute | solution.py:292
  22.6 0.0 collective-permute-done.1.hi_ref
  22.6 0.0 collective-permute-done.lo_ref
  22.6 0.0 copy-done.2
  22.6 0.0 copy-done.3
  22.6 0.1 shard_map.78
  22.7 13.5 %collective-permute-start.2 = (bf16[32,128]{1,0:T(8,128)(2,1)S(1)}, bf16[32,128]{1,0:T(8,128)(2,1)S(1)}, u32[]{:S(2)}, u32[]{:S(2)}) collective-permute-start(bf16[32,128]{1,0:T(8,128)(2,1)S(1)} %get-tuple-element.11), channel_id=1, source_target_pairs={{0,15},{1,2},{2,1},{3,4},{4,3},{5,6},{6,5},{7,8},{8,7},{9,10},{10,... | collective-permute-start | bytes 24584 | tf_op jit(solution)/shard_map/ppermute | solution.py:294
  36.3 3.2 %collective-permute-start.3 = (bf16[32,128]{1,0:T(8,128)(2,1)S(1)}, bf16[32,128]{1,0:T(8,128)(2,1)S(1)}, u32[]{:S(2)}, u32[]{:S(2)}) collective-permute-start(bf16[32,128]{1,0:T(8,128)(2,1)S(1)} %get-tuple-element.12), channel_id=1, source_target_pairs={{0,1},{1,0},{2,3},{3,2},{4,5},{5,4},{6,7},{7,6},{8,9},{9,8},{10,11... | collective-permute-start | bytes 24584 | tf_op jit(solution)/shard_map/ppermute | solution.py:295
  39.4 0.0 collective-permute-done.4.up2_ref
  39.4 0.0 collective-permute-done.2.far_ref
  39.5 0.8 %collective-permute-done.3.near_ref = bf16[32,128]{1,0:T(8,128)(2,1)S(1)} collective-permute-done((bf16[32,128]{1,0:T(8,128)(2,1)S(1)}, bf16[32,128]{1,0:T(8,128)(2,1)S(1)}, u32[]{:S(2)}, u32[]{:S(2)}) %collective-permute-start.3) | collective-permute-done | bytes 8224 | tf_op jit(solution)/shard_map/ppermute | solution.py:295
  40.2 0.0 copy-done
  40.2 0.0 copy-done.1
  40.3 0.0 copy-done.4
  40.3 2.5 %shard_map.79 = (f32[6,64,128]{2,1,0:T(8,128)}, f32[4,64,128]{2,1,0:T(8,128)}) custom-call(bf16[3,64,128]{2,1,0:T(8,128)(2,1)S(1)} %bitcast.14, s32[64,128]{1,0:T(8,128)S(1)} %bitcast.17, s32[64,128]{1,0:T(8,128)S(1)} %bitcast.18, bf16[608,128]{1,0:T(8,128)(2,1)S(1)} %collective-permute-done.lo_ref, bf16[96,128]{1,0:T(8,128)(2,1)S(1)} %collective-permute-done.1.hi_ref, ...), custom_call_target="tpu_custom_call" | custom-call | bytes 400000 | tf_op jit(solution)/shard_map/pallas_call | solution.py:296
  (1 shorter events, 0.0 us)
Async XLA Ops:
  0.6 22.0 %copy-start.2 = (bf16[3,8,8,128]{3,2,1,0:T(8,128)(2,1)S(1)}, bf16[3,8,8,128]{3,2,1,0:T(8,128)(2,1)}, u32[]{:S(2)}) copy-start(bf16[3,8,8,128]{3,2,1,0:T(8,128)(2,1)} %param.6) | copy-start | bytes 147460
  0.6 22.0 %copy-start.3 = (s32[8,8,128]{2,1,0:T(8,128)S(1)}, s32[8,8,128]{2,1,0:T(8,128)}, u32[]{:S(2)}) copy-start(s32[8,8,128]{2,1,0:T(8,128)} %param.10) | copy-start | bytes 98308
  2.4 20.2 %collective-permute-start = (bf16[608,128]{1,0:T(8,128)(2,1)}, bf16[608,128]{1,0:T(8,128)(2,1)S(1)}, u32[]{:S(2)}, u32[]{:S(2)}) collective-permute-start(bf16[608,128]{1,0:T(8,128)(2,1)} %get-tuple-element.9), channel_id=1, source_target_pairs={{0,16},{16,32},{32,48},{48,64},{64,80},{80,96},{96,112},{112,128},... | collective-permute-start | bytes 466952 | tf_op jit(solution)/shard_map/ppermute | solution.py:290
  6.7 15.8 %collective-permute-start.1 = (bf16[96,128]{1,0:T(8,128)(2,1)}, bf16[96,128]{1,0:T(8,128)(2,1)S(1)}, u32[]{:S(2)}, u32[]{:S(2)}) collective-permute-start(bf16[96,128]{1,0:T(8,128)(2,1)} %get-tuple-element.10), channel_id=1, source_target_pairs={{0,496},{16,0},{32,16},{48,32},{64,48},{80,64},{96,80},{112,96},{1... | collective-permute-start | bytes 73736 | tf_op jit(solution)/shard_map/ppermute | solution.py:291
  20.5 19.8 %copy-start = (f32[2,8,8,128]{3,2,1,0:T(8,128)S(1)}, f32[2,8,8,128]{3,2,1,0:T(8,128)}, u32[]{:S(2)}) copy-start(f32[2,8,8,128]{3,2,1,0:T(8,128)} %param.7) | copy-start | bytes 196612
  20.5 19.8 %copy-start.1 = (f32[2,8,8,128]{3,2,1,0:T(8,128)S(1)}, f32[2,8,8,128]{3,2,1,0:T(8,128)}, u32[]{:S(2)}) copy-start(f32[2,8,8,128]{3,2,1,0:T(8,128)} %param.8) | copy-start | bytes 196612
  20.5 19.8 %copy-start.4 = (s32[8,8,128]{2,1,0:T(8,128)S(1)}, s32[8,8,128]{2,1,0:T(8,128)}, u32[]{:S(2)}) copy-start(s32[8,8,128]{2,1,0:T(8,128)} %param.11) | copy-start | bytes 98308
  20.5 19.8 %copy-start.5 = (s32[8,8,16]{2,1,0:T(8,128)S(1)}, s32[8,8,16]{2,1,0:T(8,128)}, u32[]{:S(2)}) copy-start(s32[8,8,16]{2,1,0:T(8,128)} %param.9) | copy-start | bytes 12292
  20.5 18.9 %collective-permute-start.4 = (s16[256,128]{1,0:T(8,128)(2,1)}, s16[256,128]{1,0:T(8,128)(2,1)S(1)}, u32[]{:S(2)}, u32[]{:S(2)}) collective-permute-start(s16[256,128]{1,0:T(8,128)(2,1)} %get-tuple-element.13), channel_id=1, source_target_pairs={{0,32},{16,48},{32,64},{48,80},{64,96},{80,112},{96,128},{112,144}... | collective-permute-start | bytes 196616 | tf_op jit(solution)/shard_map/ppermute | solution.py:292
  22.7 16.7 %collective-permute-start.2 = (bf16[32,128]{1,0:T(8,128)(2,1)S(1)}, bf16[32,128]{1,0:T(8,128)(2,1)S(1)}, u32[]{:S(2)}, u32[]{:S(2)}) collective-permute-start(bf16[32,128]{1,0:T(8,128)(2,1)S(1)} %get-tuple-element.11), channel_id=1, source_target_pairs={{0,15},{1,2},{2,1},{3,4},{4,3},{5,6},{6,5},{7,8},{8,7},{9,10},{10,... | collective-permute-start | bytes 24584 | tf_op jit(solution)/shard_map/ppermute | solution.py:294
  36.3 4.0 %collective-permute-start.3 = (bf16[32,128]{1,0:T(8,128)(2,1)S(1)}, bf16[32,128]{1,0:T(8,128)(2,1)S(1)}, u32[]{:S(2)}, u32[]{:S(2)}) collective-permute-start(bf16[32,128]{1,0:T(8,128)(2,1)S(1)} %get-tuple-element.12), channel_id=1, source_target_pairs={{0,1},{1,0},{2,3},{3,2},{4,5},{5,4},{6,7},{7,6},{8,9},{9,8},{10,11... | collective-permute-start | bytes 24584 | tf_op jit(solution)/shard_map/ppermute | solution.py:295

commit v4 on v3

--- a/solution.py
+++ b/solution.py
@@ -15,18 +15,13 @@
 BF16 = jnp.bfloat16
 VMEM_LIMIT = 32 * 1024 * 1024
 PACK_LIMIT = 60 * 1024 * 1024
-STRIP_FLOPS = 1_000_000_000
+BIG = 1_000_000_000
+SIDE = 256
 
 
 def row(ref, x, lead=None):
     at = (pl.ds(x, 8, stride=8), slice(None))
     return ref[at] if lead is None else ref[(lead,) + at]
-
-
-def masked_rows(vel_ref, solid_ref, scratch):
-    solid = solid_ref[...] == 1
-    for c in range(3):
-        scratch[c] = jnp.where(solid, 0.0, vel_ref[c].astype(F32))
 
 
 def encode(x):
@@ -41,7 +36,36 @@
     return jnp.where(y < 0, -y2, y2) * y2
 
 
-def pack_kernel(vel_hbm, solid_hbm, lq_hbm, mn_hbm, head_ref, tail_ref, kept_ref, vel, solid, kept, scratch, sems):
+def place():
+    return lax.axis_index("gx") & 7, (lax.axis_index("gy") & 1) == 0
+
+
+def edges(rows, first):
+    lane = lax.broadcasted_iota(jnp.int32, (8, 128), 1)
+    left, right = [], []
+    for c in range(3):
+        lefts = jnp.zeros((8, 128), F32)
+        rights = jnp.zeros((8, 128), F32)
+        for k, value in enumerate(rows[c]):
+            i = first + k
+            here = (lane >= 4 * i) & (lane < 4 * i + 4)
+            lefts = jnp.where(here, pltpu.roll(value, 4 * i, 1) if i else value, lefts)
+            rights = jnp.where(here, pltpu.roll(value, 4 * i + 4, 1), rights)
+        left.append(lefts)
+        right.append(rights)
+    none = [jnp.zeros((8, 128), F32)]
+    return jnp.concatenate(left + none, axis=0), jnp.concatenate(right + none, axis=0)
+
+
+def own_rows(vel_ref, solid_ref, scratch):
+    inside = solid_ref[...] == 1
+    for c in range(3):
+        scratch[c] = jnp.where(inside, 0.0, vel_ref[c].astype(F32))
+    return [[row(scratch, x, c) for x in range(8)] for c in range(3)]
+
+
+def pack_kernel(vel_hbm, solid_hbm, lq_hbm, mn_hbm, tail_ref, head_ref, side_ref, code_ref,
+                vel, solid, kept, scratch, sems):
     copies = [
         pltpu.make_async_copy(vel_hbm, vel, sems.at[0]),
         pltpu.make_async_copy(solid_hbm, solid, sems.at[1]),
@@ -52,51 +76,61 @@
         copy.start()
     copies[0].wait()
     copies[1].wait()
-    masked_rows(vel, solid, scratch)
-    head = [row(scratch, x, c) for c in range(3) for x in range(4)]
-    head_ref[...] = jnp.concatenate(head, axis=0).astype(BF16)
-    tail = [row(scratch, 4 + x, c) for c in range(3) for x in range(4)]
-    tail_ref[pl.ds(0, 96), :] = jnp.concatenate(tail, axis=0).astype(BF16)
+    rows = own_rows(vel, solid, scratch)
+    head_ref[...] = jnp.concatenate([rows[c][x] for c in range(3) for x in range(4)], axis=0).astype(BF16)
+    tail = jnp.concatenate([rows[c][4 + x] for c in range(3) for x in range(4)], axis=0).astype(BF16)
+    tail_ref[pl.ds(0, 96), :] = tail
+    side_ref[pl.ds(0, 96), :] = tail
+    side_ref[pl.ds(96, SIDE - 96), :] = jnp.zeros((SIDE - 96, 128), BF16)
     copies[2].wait()
     copies[3].wait()
     old = kept[...]
-    kept_ref[...] = encode(old)
+    code_ref[...] = encode(old)
     high = old.astype(BF16)
     tail_ref[pl.ds(96, 256), :] = high
     tail_ref[pl.ds(352, 256), :] = (old - high.astype(F32)).astype(BF16)
 
 
-def halo_rows(scratch, lo_ref, hi_ref):
-    lo = lo_ref[pl.ds(0, 96), :].astype(F32).reshape(3, 4, 8, 128)
-    hi = hi_ref[...].astype(F32).reshape(3, 4, 8, 128)
+def all_rows(own, lo, hi):
+    lo = lo.reshape(3, 4, 8, 128)
+    hi = hi.reshape(3, 4, 8, 128)
     out = []
     for c in range(3):
         rows = [lo[c, x] for x in (1, 2, 3)]
-        rows += [row(scratch, x, c) for x in range(8)]
+        rows += own[c]
         rows += [hi[c, x] for x in (0, 1, 2)]
         out.append(rows)
     return out
 
 
-def strip_kernel(vel_ref, solid_ref, lo_ref, hi_ref, far_ref, near_ref, scratch):
-    masked_rows(vel_ref, solid_ref, scratch)
-    rows = halo_rows(scratch, lo_ref, hi_ref)
-    lane = lax.broadcasted_iota(jnp.int32, (8, 128), 1)
-    left, right = [], []
-    for c in range(3):
-        lefts = jnp.zeros((8, 128), F32)
-        rights = jnp.zeros((8, 128), F32)
-        for i in range(14):
-            here = (lane >= 4 * i) & (lane < 4 * i + 4)
-            lefts = jnp.where(here, pltpu.roll(rows[c][i], 4 * i, 1) if i else rows[c][i], lefts)
-            rights = jnp.where(here, pltpu.roll(rows[c][i], 4 * i + 4, 1), rights)
-        left.append(lefts)
-        right.append(rights)
-    left = jnp.concatenate(left + [jnp.zeros((8, 128), F32)], axis=0)
-    right = jnp.concatenate(right + [jnp.zeros((8, 128), F32)], axis=0)
-    even = lax.axis_index("gy") % 2 == 0
-    near_ref[...] = jnp.where(even, right, left).astype(BF16)
-    far_ref[...] = jnp.where(even, left, right).astype(BF16)
+def lead(ref, n):
+    return ref[pl.ds(0, n), :].astype(F32)
+
+
+def far_kernel(vel_ref, solid_ref, lo_ref, hi_ref, wide_ref, strip_ref, scratch):
+    own = own_rows(vel_ref, solid_ref, scratch)
+    rows = all_rows(own, lead(lo_ref, 96), lead(hi_ref, 96))
+    left, right = edges(rows, 0)
+    _, even = place()
+    strip = jnp.where(even, left, right).astype(BF16)
+    strip_ref[...] = strip
+    wide_ref[pl.ds(96, 32), :] = strip
+    wide_ref[pl.ds(0, 96), :] = jnp.concatenate([own[c][x] for c in range(3) for x in range(4)], axis=0).astype(BF16)
+
+
+def relay_kernel(wide_ref, strip_ref, head_ref, side_ref, two_ref, relay_ref, strip_out):
+    relay_ref[pl.ds(0, 96), :] = wide_ref[pl.ds(0, 96), :]
+    relay_ref[pl.ds(96, 96), :] = head_ref[...]
+    strip_out[...] = strip_ref[...]
+
+
+def near_kernel(vel_ref, solid_ref, lo_ref, wrap_ref, hi_ref, relay_ref, strip_ref, scratch):
+    at, even = place()
+    own = own_rows(vel_ref, solid_ref, scratch)
+    lo = jnp.where(at == 0, lead(wrap_ref, 96), lead(lo_ref, 96))
+    hi = jnp.where(at == 7, lead(relay_ref, 96), lead(hi_ref, 96))
+    left, right = edges(all_rows(own, lo, hi), 0)
+    strip_ref[...] = jnp.where(even, right, left).astype(BF16)
 
 
 def shift_y(a, b, k, lane):
@@ -128,18 +162,20 @@
     return 1.0 / (1.0 + (1.0 / RATE_SCALE) * inverse)
 
 
-def main_kernel(vel_ref, solid_ref, clip_ref, lo_ref, hi_ref, far_ref, near_ref, src_ref,
-                lq_ref, mn_ref, up2_ref, stress_ref, new_ref, scratch, old):
+def main_kernel(vel_ref, solid_ref, clip_ref, lo_ref, wrap_ref, hi_ref, relay_ref, far_ref, wide_ref, side_ref,
+                near_ref, src_ref, lq_ref, mn_ref, two_ref, stress_ref, new_ref, scratch, old):
     lane = lax.broadcasted_iota(jnp.int32, (8, 128), 1)
     sub = lax.broadcasted_iota(jnp.int32, (8, 128), 0)
+    run, even = place()
     here = lax.broadcasted_iota(jnp.int32, (64, 16), 0) % 8
     back = (lax.axis_index("gx") * 8 + here - src_ref[...] + 512) & 255
     spread = (lax.broadcasted_iota(jnp.int32, (16, 128), 1) // 8 == lax.broadcasted_iota(jnp.int32, (16, 128), 0))
     local = jnp.dot((16 + here - back).astype(F32), spread.astype(F32), preferred_element_type=F32)
     local = (local + 0.5).astype(jnp.int32)
-    one_high = lo_ref[pl.ds(96, 256), :].astype(F32).reshape(4, 64, 128)
-    one_low = lo_ref[pl.ds(352, 256), :].astype(F32).reshape(4, 64, 128)
-    up2 = decode(up2_ref[...]).reshape(4, 64, 128)
+    tile = lo_ref[pl.ds(96, 256), :].astype(F32) + lo_ref[pl.ds(352, 256), :].astype(F32)
+    wrap = wrap_ref[pl.ds(96, 256), :].astype(F32) + wrap_ref[pl.ds(352, 256), :].astype(F32)
+    up1 = jnp.where(run == 0, wrap, tile).reshape(4, 64, 128)
+    up2 = decode(two_ref[...]).reshape(4, 64, 128)
     for z in range(8):
         at = pl.ds(8 * z, 8)
         idx = local[8 * z : 8 * z + 8]
@@ -148,24 +184,30 @@
             own_ref = lq_ref if f < 2 else mn_ref
             own = own_ref[pl.ds(64 * (f % 2) + 8 * z, 8), :]
             got = jnp.take_along_axis(own, inner, axis=0)
-            up1 = one_high[f, 8 * z : 8 * z + 8] + one_low[f, 8 * z : 8 * z + 8]
-            one = jnp.take_along_axis(up1, inner, axis=0)
+            one = jnp.take_along_axis(up1[f, 8 * z : 8 * z + 8], inner, axis=0)
             two = jnp.take_along_axis(up2[f, 8 * z : 8 * z + 8], inner, axis=0)
             old[f, at, :] = jnp.where(idx < 8, two, jnp.where(idx < 16, one, got))
-    masked_rows(vel_ref, solid_ref, scratch)
-    core = halo_rows(scratch, lo_ref, hi_ref)
-    near = near_ref[...].astype(F32)
-    far = far_ref[...].astype(F32)
-    even = lax.axis_index("gy") % 2 == 0
-    left = jnp.where(even, far, near).reshape(4, 8, 128)
-    right = jnp.where(even, near, far).reshape(4, 8, 128)
+    lo = jnp.where(run == 0, lead(wrap_ref, 96), lead(lo_ref, 96))
+    hi = jnp.where(run == 7, lead(relay_ref, 96), lead(hi_ref, 96))
+    core = all_rows(own_rows(vel_ref, solid_ref, scratch), lo, hi)
+    near = near_ref[...].astype(F32).reshape(4, 8, 128)
+    far = jnp.where(run == 0, wide_ref[pl.ds(96, 32), :].astype(F32), far_ref[...].astype(F32)).reshape(4, 8, 128)
+    below = lead(side_ref, 96).reshape(3, 4, 8, 128)
+    above = relay_ref[pl.ds(96, 96), :].astype(F32).reshape(3, 4, 8, 128)
     edge = []
     for c in range(3):
+        left = jnp.where(even, far[c], near[c])
+        right = jnp.where(even, near[c], far[c])
         rows = []
         for i in range(14):
-            r = pltpu.roll(right[c], 128 - 4 * i, 1) if i else right[c]
-            l = pltpu.roll(left[c], 124 - 4 * i, 1)
-            rows.append(jnp.where(lane < 64, r, l))
+            r = pltpu.roll(right, 128 - 4 * i, 1) if i else right
+            l = pltpu.roll(left, 124 - 4 * i, 1)
+            value = jnp.where(lane < 64, r, l)
+            if i < 3:
+                value = jnp.where((run == 0) & ((lane >= 64) == even), below[c, i + 1], value)
+            if i > 10:
+                value = jnp.where((run == 7) & ((lane >= 64) == even), above[c, i - 11], value)
+            rows.append(value)
         edge.append(rows)
     vn, vw, vdn, vdw = ([[None] * 14 for _ in range(3)] for _ in range(4))
     near_y = [[None] * 14 for _ in range(3)]
@@ -266,8 +308,18 @@
     )
 
 
-def ring(n, by):
-    return [(i, (i + by) % n) for i in range(n)]
+def far_side(gy):
+    return (gy + 1) % 16 if gy % 2 else (gy - 1) % 16
+
+
+def send(x, target):
+    pairs = []
+    for gx in range(32):
+        for gy in range(16):
+            to = target(gx % 8, gx, gy)
+            if to is not None:
+                pairs.append((gx * 16 + gy, to[0] % 32 * 16 + to[1]))
+    return lax.ppermute(x, ("gx", "gy"), pairs)
 
 
 def local(velocity, kept_lm_qn, kept_mm_nn, back_src, solid_flags, clip_flags):
@@ -278,25 +330,32 @@
     lq = kept_lm_qn.reshape(128, 128)
     mn = kept_mm_nn.reshape(128, 128)
     src = back_src.reshape(64, 16)
+    strip_type = sds((32, 128), BF16)
+    code_type = sds((256, 128), jnp.int16)
     trans = pltpu.VMEM((3, 64, 128), F32)
-    head, tail, kept = call(
+    tail, head, side, code = call(
         pack_kernel,
-        [sds((96, 128), BF16), sds((608, 128), BF16), sds((256, 128), jnp.int16)],
+        [sds((608, 128), BF16), sds((96, 128), BF16), sds((SIDE, 128), BF16), code_type],
         [HBM] * 4,
-        [pltpu.VMEM((3, 64, 128), BF16), pltpu.VMEM((64, 128), jnp.int32), pltpu.VMEM((256, 128), F32), trans,
-         pltpu.SemaphoreType.DMA((4,))],
+        [pltpu.VMEM((3, 64, 128), BF16), pltpu.VMEM((64, 128), jnp.int32), pltpu.VMEM((256, 128), F32),
+         trans, pltpu.SemaphoreType.DMA((4,))],
         PACK_LIMIT,
     )(vel, solid, lq, mn)
-    lo = lax.ppermute(tail, "gx", ring(32, 1))
-    hi = lax.ppermute(head, "gx", ring(32, -1))
-    up2 = lax.ppermute(kept, "gx", ring(32, 2))
-    far, near = call(strip_kernel, [sds((32, 128), BF16)] * 2, [VM] * 4, [trans], flops=STRIP_FLOPS)(vel, solid, lo, hi)
-    far = lax.ppermute(far, "gy", [(i, (i + 1) % 16 if i % 2 else (i - 1) % 16) for i in range(16)])
-    near = lax.ppermute(near, "gy", [(i, i ^ 1) for i in range(16)])
+    lo = send(tail, lambda run, gx, gy: (gx + 1, gy) if run < 7 else None)
+    hi = send(head, lambda run, gx, gy: (gx - 1, gy) if run > 0 else None)
+    side = send(side, lambda run, gx, gy: (gx + 1, far_side(gy)) if run == 7 else None)
+    wrap = send(tail, lambda run, gx, gy: (gx + 1, gy) if run == 7 else None)
+    two = send(code, lambda run, gx, gy: (gx + 2, gy))
+    wide, strip = call(far_kernel, [sds((128, 128), BF16), strip_type], [VM] * 4, [trans], flops=BIG)(vel, solid, lo, hi)
+    wide = send(wide, lambda run, gx, gy: (gx, far_side(gy)) if run == 0 else None)
+    relay, strip = call(relay_kernel, [sds((192, 128), BF16), strip_type], [VM] * 5, [])(wide, strip, head, side, two)
+    relay = send(relay, lambda run, gx, gy: (gx - 1, far_side(gy)) if run == 0 else None)
+    far = send(strip, lambda run, gx, gy: (gx, far_side(gy)) if run > 0 else None)
+    (near,) = call(near_kernel, [strip_type], [VM] * 6, [trans])(vel, solid, lo, wrap, hi, relay)
+    near = send(near, lambda run, gx, gy: (gx, gy ^ 1))
     stress, new = call(
-        main_kernel, [sds((6, 64, 128), F32), sds((4, 64, 128), F32)], [VM] * 11,
-        [trans, pltpu.VMEM((4, 64, 128), F32)],
-    )(vel, solid, clip, lo, hi, far, near, src, lq, mn, up2)
+        main_kernel, [sds((6, 64, 128), F32), sds((4, 64, 128), F32)], [VM] * 15, [trans, pltpu.VMEM((4, 64, 128), F32)],
+    )(vel, solid, clip, lo, wrap, hi, relay, far, wide, side, near, src, lq, mn, two)
     return stress.reshape(6, 8, 8, 128), new.reshape(4, 8, 8, 128)
 
 

time: 43.1 us -> 50.4 us (1.17)
  the two profiles are of different devices: /device:TPU:1 before, /device:TPU:32 now
where the time goes in v4:
time: 50.4 us; the launch traced here: 49.9 us
  starting transfers between devices  25.9 us (51%)
  waiting for transfers between devices  18.6 us (37%)
  Pallas kernels  4.55 us (9%)
  between operations  0.86 us (2%)
    ppermute x9, starting transfers between devices, send(): return lax.ppermute(x, ('gx', 'gy'), pairs)  25.9 us
    ppermute x9, waiting for transfers between devices, send(): return lax.ppermute(x, ('gx', 'gy'), pairs)  18.6 us
    pallas_call x1, Pallas kernels, local(): call(main_kernel, [sds((6, 64, 128), F32), sds((4, 64, 128), F32)], [VM]...  2.53 us
    pallas_call x1, Pallas kernels, local(): call(pack_kernel, [sds((608, 128), BF16), sds((96, 128), BF16), sds((SIDE...  1.76 us
  transfers between devices with their start and end apart: 9, of which 2 were waited for; matrix products, arithmetic and copies ran while one was open for 0% of the time, Pallas kernels for 1%

profile of v4, /device:TPU:32, one launch (start us, length us, event | category | flops | bytes accessed | tf_op | source)
XLA Modules:
  0.0 49.9 jit_solution(14592841367981603200)
XLA Ops:
  0.6 1.8 %shard_map.77 = (bf16[608,128]{1,0:T(8,128)(2,1)}, bf16[96,128]{1,0:T(8,128)(2,1)}, bf16[256,128]{1,0:T(8,128)(2,1)}, s16[256,128]{1,0:T(8,128)(2,1)}) custom-call(bf16[3,64,128]{2,1,0:T(8,128)(2,1)} %bitcast.8, s32[64,128]{1,0:T(8,128)} %bitcast.12, f32[128,128]{1,0:T(8,128)} %bitcast.16, f32[128,128]{1,0:T(8,128)} %bitcast.18), custom_call_target="tpu_custom_call" | custom-call | bytes 400000 | tf_op jit(solution)/shard_map/pallas_call | solution.py:336
  2.4 3.8 %collective-permute-start = (bf16[608,128]{1,0:T(8,128)(2,1)}, bf16[608,128]{1,0:T(8,128)(2,1)S(1)}, u32[]{:S(2)}, u32[]{:S(2)}) collective-permute-start(bf16[608,128]{1,0:T(8,128)(2,1)} %get-tuple-element.12), channel_id=1, source_target_pairs={{0,16},{1,17},{2,18},{3,19},{4,20},{5,21},{6,22},{7,23},{8,24},{9,... | collective-permute-start | bytes 466952 | tf_op jit(solution)/shard_map/ppermute | solution.py:322
  6.2 4.9 %collective-permute-start.2 = (bf16[96,128]{1,0:T(8,128)(2,1)}, bf16[96,128]{1,0:T(8,128)(2,1)S(1)}, u32[]{:S(2)}, u32[]{:S(2)}) collective-permute-start(bf16[96,128]{1,0:T(8,128)(2,1)} %get-tuple-element.13.head_ref), channel_id=1, source_target_pairs={{16,0},{17,1},{18,2},{19,3},{20,4},{21,5},{22,6},{23,7},{24,8},{25... | collective-permute-start | bytes 73736 | tf_op jit(solution)/shard_map/ppermute | solution.py:322
  11.1 0.7 %collective-permute-start.1 = (bf16[608,128]{1,0:T(8,128)(2,1)}, bf16[608,128]{1,0:T(8,128)(2,1)S(1)}, u32[]{:S(2)}, u32[]{:S(2)}) collective-permute-start(bf16[608,128]{1,0:T(8,128)(2,1)} %get-tuple-element.12), channel_id=1, source_target_pairs={{112,128},{113,129},{114,130},{115,131},{116,132},{117,133},{118,1... | collective-permute-start | bytes 466952 | tf_op jit(solution)/shard_map/ppermute | solution.py:322
  11.8 0.7 %collective-permute-start.4 = (bf16[256,128]{1,0:T(8,128)(2,1)}, bf16[256,128]{1,0:T(8,128)(2,1)S(1)}, u32[]{:S(2)}, u32[]{:S(2)}) collective-permute-start(bf16[256,128]{1,0:T(8,128)(2,1)} %get-tuple-element.16), channel_id=1, source_target_pairs={{112,143},{113,130},{114,129},{115,132},{116,131},{117,134},{118,1... | collective-permute-start | bytes 196616 | tf_op jit(solution)/shard_map/ppermute | solution.py:322
  12.5 3.4 %collective-permute-start.5 = (s16[256,128]{1,0:T(8,128)(2,1)}, s16[256,128]{1,0:T(8,128)(2,1)S(1)}, u32[]{:S(2)}, u32[]{:S(2)}) collective-permute-start(s16[256,128]{1,0:T(8,128)(2,1)} %get-tuple-element.17), channel_id=1, source_target_pairs={{0,32},{1,33},{2,34},{3,35},{4,36},{5,37},{6,38},{7,39},{8,40},{9,... | collective-permute-start | bytes 196616 | tf_op jit(solution)/shard_map/ppermute | solution.py:322
  15.9 0.0 collective-permute-done.2.hi_ref
  15.9 0.0 collective-permute-done.lo_ref
  16.0 0.1 shard_map.78
  16.1 0.7 %collective-permute-start.3 = (bf16[128,128]{1,0:T(8,128)(2,1)S(1)}, bf16[128,128]{1,0:T(8,128)(2,1)S(1)}, u32[]{:S(2)}, u32[]{:S(2)}) collective-permute-start(bf16[128,128]{1,0:T(8,128)(2,1)S(1)} %get-tuple-element.14), channel_id=1, source_target_pairs={{0,15},{1,2},{2,1},{3,4},{4,3},{5,6},{6,5},{7,8},{8,7},{9,10},{10,... | collective-permute-start | bytes 98312 | tf_op jit(solution)/shard_map/ppermute | solution.py:322
  16.8 0.0 collective-permute-done.4.side_ref
  16.8 13.9 %collective-permute-done.5.two_ref = s16[256,128]{1,0:T(8,128)(2,1)S(1)} collective-permute-done((s16[256,128]{1,0:T(8,128)(2,1)}, s16[256,128]{1,0:T(8,128)(2,1)S(1)}, u32[]{:S(2)}, u32[]{:S(2)}) %collective-permute-start.5) | collective-permute-done | bytes 65568 | tf_op jit(solution)/shard_map/ppermute | solution.py:322
  30.7 0.0 collective-permute-done.3.wide_ref
  30.7 0.7 %collective-permute-start.6 = (bf16[192,128]{1,0:T(8,128)(2,1)S(1)}, bf16[192,128]{1,0:T(8,128)(2,1)S(1)}, u32[]{:S(2)}, u32[]{:S(2)}) collective-permute-start(bf16[192,128]{1,0:T(8,128)(2,1)S(1)} %get-tuple-element.18), channel_id=1, source_target_pairs={{0,511},{1,498},{2,497},{3,500},{4,499},{5,502},{6,501},{7,504},{8... | collective-permute-start | bytes 147464 | tf_op jit(solution)/shard_map/ppermute | solution.py:322
  31.4 0.0 copy-start.2
  31.4 0.0 copy-start.3
  31.4 0.0 copy-start.4
  31.4 0.0 copy-start.5
  31.5 9.2 %collective-permute-start.7 = (bf16[32,128]{1,0:T(8,128)(2,1)S(1)}, bf16[32,128]{1,0:T(8,128)(2,1)S(1)}, u32[]{:S(2)}, u32[]{:S(2)}) collective-permute-start(bf16[32,128]{1,0:T(8,128)(2,1)S(1)} %get-tuple-element.19), channel_id=1, source_target_pairs={{16,31},{17,18},{18,17},{19,20},{20,19},{21,22},{22,21},{23,24},{2... | collective-permute-start | bytes 24584 | tf_op jit(solution)/shard_map/ppermute | solution.py:322
  40.6 0.1 shard_map.80
  40.8 1.9 %collective-permute-start.8 = (bf16[32,128]{1,0:T(8,128)(2,1)S(1)}, bf16[32,128]{1,0:T(8,128)(2,1)S(1)}, u32[]{:S(2)}, u32[]{:S(2)}) collective-permute-start(bf16[32,128]{1,0:T(8,128)(2,1)S(1)} %shard_map.80), channel_id=1, source_target_pairs={{0,1},{1,0},{2,3},{3,2},{4,5},{5,4},{6,7},{7,6},{8,9},{9,8},{10,11... | collective-permute-start | bytes 24584 | tf_op jit(solution)/shard_map/ppermute | solution.py:322
  42.7 4.7 %collective-permute-done.7.far_ref = bf16[32,128]{1,0:T(8,128)(2,1)S(1)} collective-permute-done((bf16[32,128]{1,0:T(8,128)(2,1)S(1)}, bf16[32,128]{1,0:T(8,128)(2,1)S(1)}, u32[]{:S(2)}, u32[]{:S(2)}) %collective-permute-start.7) | collective-permute-done | bytes 8224 | tf_op jit(solution)/shard_map/ppermute | solution.py:322
  47.4 0.0 collective-permute-done.8.near_ref
  47.4 2.5 %shard_map.81 = (f32[6,64,128]{2,1,0:T(8,128)}, f32[4,64,128]{2,1,0:T(8,128)}) custom-call(bf16[3,64,128]{2,1,0:T(8,128)(2,1)S(1)} %bitcast.11, s32[64,128]{1,0:T(8,128)S(1)} %bitcast.15, s32[64,128]{1,0:T(8,128)S(1)} %bitcast.20, bf16[608,128]{1,0:T(8,128)(2,1)S(1)} %collective-permute-done.lo_ref, bf16[608,128]{1,0:T(8,128)(2,1)S(1)} %collective-permute-done.1.wrap_ref, ...), custom_call_target="tpu_custom_call" | custom-call | bytes 400000 | tf_op jit(solution)/shard_map/pallas_call | solution.py:356
  (13 shorter events, 0.0 us)
Async XLA Ops:
  0.6 15.3 %copy-start = (bf16[3,8,8,128]{3,2,1,0:T(8,128)(2,1)S(1)}, bf16[3,8,8,128]{3,2,1,0:T(8,128)(2,1)}, u32[]{:S(2)}) copy-start(bf16[3,8,8,128]{3,2,1,0:T(8,128)(2,1)} %param.6) | copy-start | bytes 147460
  0.6 15.3 %copy-start.1 = (s32[8,8,128]{2,1,0:T(8,128)S(1)}, s32[8,8,128]{2,1,0:T(8,128)}, u32[]{:S(2)}) copy-start(s32[8,8,128]{2,1,0:T(8,128)} %param.10) | copy-start | bytes 98308
  2.4 13.5 %collective-permute-start = (bf16[608,128]{1,0:T(8,128)(2,1)}, bf16[608,128]{1,0:T(8,128)(2,1)S(1)}, u32[]{:S(2)}, u32[]{:S(2)}) collective-permute-start(bf16[608,128]{1,0:T(8,128)(2,1)} %get-tuple-element.12), channel_id=1, source_target_pairs={{0,16},{1,17},{2,18},{3,19},{4,20},{5,21},{6,22},{7,23},{8,24},{9,... | collective-permute-start | bytes 466952 | tf_op jit(solution)/shard_map/ppermute | solution.py:322
  6.2 9.7 %collective-permute-start.2 = (bf16[96,128]{1,0:T(8,128)(2,1)}, bf16[96,128]{1,0:T(8,128)(2,1)S(1)}, u32[]{:S(2)}, u32[]{:S(2)}) collective-permute-start(bf16[96,128]{1,0:T(8,128)(2,1)} %get-tuple-element.13.head_ref), channel_id=1, source_target_pairs={{16,0},{17,1},{18,2},{19,3},{20,4},{21,5},{22,6},{23,7},{24,8},{25... | collective-permute-start | bytes 73736 | tf_op jit(solution)/shard_map/ppermute | solution.py:322
  11.1 29.5 %collective-permute-start.1 = (bf16[608,128]{1,0:T(8,128)(2,1)}, bf16[608,128]{1,0:T(8,128)(2,1)S(1)}, u32[]{:S(2)}, u32[]{:S(2)}) collective-permute-start(bf16[608,128]{1,0:T(8,128)(2,1)} %get-tuple-element.12), channel_id=1, source_target_pairs={{112,128},{113,129},{114,130},{115,131},{116,132},{117,133},{118,1... | collective-permute-start | bytes 466952 | tf_op jit(solution)/shard_map/ppermute | solution.py:322
  11.8 5.0 %collective-permute-start.4 = (bf16[256,128]{1,0:T(8,128)(2,1)}, bf16[256,128]{1,0:T(8,128)(2,1)S(1)}, u32[]{:S(2)}, u32[]{:S(2)}) collective-permute-start(bf16[256,128]{1,0:T(8,128)(2,1)} %get-tuple-element.16), channel_id=1, source_target_pairs={{112,143},{113,130},{114,129},{115,132},{116,131},{117,134},{118,1... | collective-permute-start | bytes 196616 | tf_op jit(solution)/shard_map/ppermute | solution.py:322
  12.5 18.3 %copy-start.6 = (bf16[96,128]{1,0:T(8,128)(2,1)S(1)}, bf16[96,128]{1,0:T(8,128)(2,1)}, u32[]{:S(2)}) copy-start(bf16[96,128]{1,0:T(8,128)(2,1)} %get-tuple-element.13.head_ref) | copy-start | bytes 73732
  12.5 18.2 %collective-permute-start.5 = (s16[256,128]{1,0:T(8,128)(2,1)}, s16[256,128]{1,0:T(8,128)(2,1)S(1)}, u32[]{:S(2)}, u32[]{:S(2)}) collective-permute-start(s16[256,128]{1,0:T(8,128)(2,1)} %get-tuple-element.17), channel_id=1, source_target_pairs={{0,32},{1,33},{2,34},{3,35},{4,36},{5,37},{6,38},{7,39},{8,40},{9,... | collective-permute-start | bytes 196616 | tf_op jit(solution)/shard_map/ppermute | solution.py:322
  16.1 14.6 %collective-permute-start.3 = (bf16[128,128]{1,0:T(8,128)(2,1)S(1)}, bf16[128,128]{1,0:T(8,128)(2,1)S(1)}, u32[]{:S(2)}, u32[]{:S(2)}) collective-permute-start(bf16[128,128]{1,0:T(8,128)(2,1)S(1)} %get-tuple-element.14), channel_id=1, source_target_pairs={{0,15},{1,2},{2,1},{3,4},{4,3},{5,6},{6,5},{7,8},{8,7},{9,10},{10,... | collective-permute-start | bytes 98312 | tf_op jit(solution)/shard_map/ppermute | solution.py:322
  30.7 9.9 %collective-permute-start.6 = (bf16[192,128]{1,0:T(8,128)(2,1)S(1)}, bf16[192,128]{1,0:T(8,128)(2,1)S(1)}, u32[]{:S(2)}, u32[]{:S(2)}) collective-permute-start(bf16[192,128]{1,0:T(8,128)(2,1)S(1)} %get-tuple-element.18), channel_id=1, source_target_pairs={{0,511},{1,498},{2,497},{3,500},{4,499},{5,502},{6,501},{7,504},{8... | collective-permute-start | bytes 147464 | tf_op jit(solution)/shard_map/ppermute | solution.py:322
  31.4 16.0 %copy-start.2 = (f32[2,8,8,128]{3,2,1,0:T(8,128)S(1)}, f32[2,8,8,128]{3,2,1,0:T(8,128)}, u32[]{:S(2)}) copy-start(f32[2,8,8,128]{3,2,1,0:T(8,128)} %param.7) | copy-start | bytes 196612
  31.4 16.0 %copy-start.3 = (f32[2,8,8,128]{3,2,1,0:T(8,128)S(1)}, f32[2,8,8,128]{3,2,1,0:T(8,128)}, u32[]{:S(2)}) copy-start(f32[2,8,8,128]{3,2,1,0:T(8,128)} %param.8) | copy-start | bytes 196612
  31.4 16.0 %copy-start.4 = (s32[8,8,128]{2,1,0:T(8,128)S(1)}, s32[8,8,128]{2,1,0:T(8,128)}, u32[]{:S(2)}) copy-start(s32[8,8,128]{2,1,0:T(8,128)} %param.11) | copy-start | bytes 98308
  31.4 16.0 %copy-start.5 = (s32[8,8,16]{2,1,0:T(8,128)S(1)}, s32[8,8,16]{2,1,0:T(8,128)}, u32[]{:S(2)}) copy-start(s32[8,8,16]{2,1,0:T(8,128)} %param.9) | copy-start | bytes 12292
  31.5 15.9 %collective-permute-start.7 = (bf16[32,128]{1,0:T(8,128)(2,1)S(1)}, bf16[32,128]{1,0:T(8,128)(2,1)S(1)}, u32[]{:S(2)}, u32[]{:S(2)}) collective-permute-start(bf16[32,128]{1,0:T(8,128)(2,1)S(1)} %get-tuple-element.19), channel_id=1, source_target_pairs={{16,31},{17,18},{18,17},{19,20},{20,19},{21,22},{22,21},{23,24},{2... | collective-permute-start | bytes 24584 | tf_op jit(solution)/shard_map/ppermute | solution.py:322
  40.8 6.6 %collective-permute-start.8 = (bf16[32,128]{1,0:T(8,128)(2,1)S(1)}, bf16[32,128]{1,0:T(8,128)(2,1)S(1)}, u32[]{:S(2)}, u32[]{:S(2)}) collective-permute-start(bf16[32,128]{1,0:T(8,128)(2,1)S(1)} %shard_map.80), channel_id=1, source_target_pairs={{0,1},{1,0},{2,3},{3,2},{4,5},{5,4},{6,7},{7,6},{8,9},{9,8},{10,11... | collective-permute-start | bytes 24584 | tf_op jit(solution)/shard_map/ppermute | solution.py:322

commit v5 on v4

--- a/solution.py
+++ b/solution.py
@@ -163,7 +163,7 @@
 
 
 def main_kernel(vel_ref, solid_ref, clip_ref, lo_ref, wrap_ref, hi_ref, relay_ref, far_ref, wide_ref, side_ref,
-                near_ref, src_ref, lq_ref, mn_ref, two_ref, stress_ref, new_ref, scratch, old):
+                near_ref, src_ref, lq_ref, mn_ref, two_ref, two_wrap_ref, stress_ref, new_ref, scratch, old):
     lane = lax.broadcasted_iota(jnp.int32, (8, 128), 1)
     sub = lax.broadcasted_iota(jnp.int32, (8, 128), 0)
     run, even = place()
@@ -175,7 +175,7 @@
     tile = lo_ref[pl.ds(96, 256), :].astype(F32) + lo_ref[pl.ds(352, 256), :].astype(F32)
     wrap = wrap_ref[pl.ds(96, 256), :].astype(F32) + wrap_ref[pl.ds(352, 256), :].astype(F32)
     up1 = jnp.where(run == 0, wrap, tile).reshape(4, 64, 128)
-    up2 = decode(two_ref[...]).reshape(4, 64, 128)
+    up2 = decode(jnp.where(run == 0, two_wrap_ref[...].astype(jnp.int32), two_ref[...].astype(jnp.int32))).reshape(4, 64, 128)
     for z in range(8):
         at = pl.ds(8 * z, 8)
         idx = local[8 * z : 8 * z + 8]
@@ -345,17 +345,18 @@
     hi = send(head, lambda run, gx, gy: (gx - 1, gy) if run > 0 else None)
     side = send(side, lambda run, gx, gy: (gx + 1, far_side(gy)) if run == 7 else None)
     wrap = send(tail, lambda run, gx, gy: (gx + 1, gy) if run == 7 else None)
-    two = send(code, lambda run, gx, gy: (gx + 2, gy))
+    two_wrap = send(code, lambda run, gx, gy: (gx + 2, gy) if run == 6 else None)
+    two = send(code, lambda run, gx, gy: (gx + 2, gy) if run != 6 else None)
     wide, strip = call(far_kernel, [sds((128, 128), BF16), strip_type], [VM] * 4, [trans], flops=BIG)(vel, solid, lo, hi)
     wide = send(wide, lambda run, gx, gy: (gx, far_side(gy)) if run == 0 else None)
-    relay, strip = call(relay_kernel, [sds((192, 128), BF16), strip_type], [VM] * 5, [])(wide, strip, head, side, two)
+    relay, strip = call(relay_kernel, [sds((192, 128), BF16), strip_type], [VM] * 5, [])(wide, strip, head, side, two_wrap)
     relay = send(relay, lambda run, gx, gy: (gx - 1, far_side(gy)) if run == 0 else None)
     far = send(strip, lambda run, gx, gy: (gx, far_side(gy)) if run > 0 else None)
     (near,) = call(near_kernel, [strip_type], [VM] * 6, [trans])(vel, solid, lo, wrap, hi, relay)
     near = send(near, lambda run, gx, gy: (gx, gy ^ 1))
     stress, new = call(
-        main_kernel, [sds((6, 64, 128), F32), sds((4, 64, 128), F32)], [VM] * 15, [trans, pltpu.VMEM((4, 64, 128), F32)],
-    )(vel, solid, clip, lo, wrap, hi, relay, far, wide, side, near, src, lq, mn, two)
+        main_kernel, [sds((6, 64, 128), F32), sds((4, 64, 128), F32)], [VM] * 16, [trans, pltpu.VMEM((4, 64, 128), F32)],
+    )(vel, solid, clip, lo, wrap, hi, relay, far, wide, side, near, src, lq, mn, two, two_wrap)
     return stress.reshape(6, 8, 8, 128), new.reshape(4, 8, 8, 128)
 
 

time: 50.4 us -> 42.4 us (0.84)
  the two profiles are of different devices: /device:TPU:32 before, /device:TPU:1 now
where the time goes in v5:
time: 42.4 us; the launch traced here: 41.7 us
  starting transfers between devices  34.4 us (81%)
  Pallas kernels  4.55 us (11%)
  waiting for transfers between devices  1.76 us (4%)
  between operations  0.87 us (2%)
    ppermute x10, starting transfers between devices, send(): return lax.ppermute(x, ('gx', 'gy'), pairs)  34.4 us
    pallas_call x1, Pallas kernels, local(): call(main_kernel, [sds((6, 64, 128), F32), sds((4, 64, 128), F32)], [VM]...  2.54 us
    pallas_call x1, Pallas kernels, local(): call(pack_kernel, [sds((608, 128), BF16), sds((96, 128), BF16), sds((SIDE...  1.76 us
    ppermute x10, waiting for transfers between devices, send(): return lax.ppermute(x, ('gx', 'gy'), pairs)  1.76 us
  transfers between devices with their start and end apart: 10, of which 4 were waited for; matrix products, arithmetic and copies ran while one was open for 0% of the time, Pallas kernels for 1%

profile of v5, /device:TPU:1, one launch (start us, length us, event | category | flops | bytes accessed | tf_op | source)
XLA Modules:
  0.0 41.7 jit_solution(5042775944679485202)
XLA Ops:
  0.6 1.8 %shard_map.77 = (bf16[608,128]{1,0:T(8,128)(2,1)}, bf16[96,128]{1,0:T(8,128)(2,1)}, bf16[256,128]{1,0:T(8,128)(2,1)}, s16[256,128]{1,0:T(8,128)(2,1)}) custom-call(bf16[3,64,128]{2,1,0:T(8,128)(2,1)} %bitcast.8, s32[64,128]{1,0:T(8,128)} %bitcast.12, f32[128,128]{1,0:T(8,128)} %bitcast.16, f32[128,128]{1,0:T(8,128)} %bitcast.18), custom_call_target="tpu_custom_call" | custom-call | bytes 400000 | tf_op jit(solution)/shard_map/pallas_call | solution.py:336
  2.4 4.4 %collective-permute-start = (bf16[608,128]{1,0:T(8,128)(2,1)}, bf16[608,128]{1,0:T(8,128)(2,1)S(1)}, u32[]{:S(2)}, u32[]{:S(2)}) collective-permute-start(bf16[608,128]{1,0:T(8,128)(2,1)} %get-tuple-element.12), channel_id=1, source_target_pairs={{0,16},{1,17},{2,18},{3,19},{4,20},{5,21},{6,22},{7,23},{8,24},{9,... | collective-permute-start | bytes 466952 | tf_op jit(solution)/shard_map/ppermute | solution.py:322
  6.8 1.3 %collective-permute-start.2 = (bf16[96,128]{1,0:T(8,128)(2,1)}, bf16[96,128]{1,0:T(8,128)(2,1)S(1)}, u32[]{:S(2)}, u32[]{:S(2)}) collective-permute-start(bf16[96,128]{1,0:T(8,128)(2,1)} %get-tuple-element.13.head_ref), channel_id=1, source_target_pairs={{16,0},{17,1},{18,2},{19,3},{20,4},{21,5},{22,6},{23,7},{24,8},{25... | collective-permute-start | bytes 73736 | tf_op jit(solution)/shard_map/ppermute | solution.py:322
  8.1 1.3 %collective-permute-start.1 = (bf16[608,128]{1,0:T(8,128)(2,1)}, bf16[608,128]{1,0:T(8,128)(2,1)S(1)}, u32[]{:S(2)}, u32[]{:S(2)}) collective-permute-start(bf16[608,128]{1,0:T(8,128)(2,1)} %get-tuple-element.12), channel_id=1, source_target_pairs={{112,128},{113,129},{114,130},{115,131},{116,132},{117,133},{118,1... | collective-permute-start | bytes 466952 | tf_op jit(solution)/shard_map/ppermute | solution.py:322
  9.4 1.3 %collective-permute-start.4 = (bf16[256,128]{1,0:T(8,128)(2,1)}, bf16[256,128]{1,0:T(8,128)(2,1)S(1)}, u32[]{:S(2)}, u32[]{:S(2)}) collective-permute-start(bf16[256,128]{1,0:T(8,128)(2,1)} %get-tuple-element.16), channel_id=1, source_target_pairs={{112,143},{113,130},{114,129},{115,132},{116,131},{117,134},{118,1... | collective-permute-start | bytes 196616 | tf_op jit(solution)/shard_map/ppermute | solution.py:322
  10.7 1.4 %collective-permute-start.5 = (s16[256,128]{1,0:T(8,128)(2,1)}, s16[256,128]{1,0:T(8,128)(2,1)S(1)}, u32[]{:S(2)}, u32[]{:S(2)}) collective-permute-start(s16[256,128]{1,0:T(8,128)(2,1)} %get-tuple-element.17), channel_id=1, source_target_pairs={{96,128},{97,129},{98,130},{99,131},{100,132},{101,133},{102,134},... | collective-permute-start | bytes 196616 | tf_op jit(solution)/shard_map/ppermute | solution.py:322
  12.2 0.1 shard_map.78
  12.3 15.9 %collective-permute-start.3 = (bf16[128,128]{1,0:T(8,128)(2,1)S(1)}, bf16[128,128]{1,0:T(8,128)(2,1)S(1)}, u32[]{:S(2)}, u32[]{:S(2)}) collective-permute-start(bf16[128,128]{1,0:T(8,128)(2,1)S(1)} %get-tuple-element.14), channel_id=1, source_target_pairs={{0,15},{1,2},{2,1},{3,4},{4,3},{5,6},{6,5},{7,8},{8,7},{9,10},{10,... | collective-permute-start | bytes 98312 | tf_op jit(solution)/shard_map/ppermute | solution.py:322
  28.3 1.3 %collective-permute-start.9 = (s16[256,128]{1,0:T(8,128)(2,1)S(1)}, s16[256,128]{1,0:T(8,128)(2,1)S(1)}, u32[]{:S(2)}, u32[]{:S(2)}) collective-permute-start(s16[256,128]{1,0:T(8,128)(2,1)S(1)} %copy-done.7), channel_id=1, source_target_pairs={{0,32},{1,33},{2,34},{3,35},{4,36},{5,37},{6,38},{7,39},{8,40},{9,... | collective-permute-start | bytes 196616 | tf_op jit(solution)/shard_map/ppermute | solution.py:322
  29.6 0.4 collective-permute-done.4.side_ref
  30.0 0.3 collective-permute-done.3.wide_ref
  30.3 2.9 %collective-permute-start.6 = (bf16[192,128]{1,0:T(8,128)(2,1)S(1)}, bf16[192,128]{1,0:T(8,128)(2,1)S(1)}, u32[]{:S(2)}, u32[]{:S(2)}) collective-permute-start(bf16[192,128]{1,0:T(8,128)(2,1)S(1)} %get-tuple-element.18), channel_id=1, source_target_pairs={{0,511},{1,498},{2,497},{3,500},{4,499},{5,502},{6,501},{7,504},{8... | collective-permute-start | bytes 147464 | tf_op jit(solution)/shard_map/ppermute | solution.py:322
  33.1 0.0 copy-start.2
  33.2 0.0 copy-start.3
  33.2 0.0 copy-start.4
  33.2 0.0 copy-start.5
  33.2 0.8 %collective-permute-start.7 = (bf16[32,128]{1,0:T(8,128)(2,1)S(1)}, bf16[32,128]{1,0:T(8,128)(2,1)S(1)}, u32[]{:S(2)}, u32[]{:S(2)}) collective-permute-start(bf16[32,128]{1,0:T(8,128)(2,1)S(1)} %get-tuple-element.19), channel_id=1, source_target_pairs={{16,31},{17,18},{18,17},{19,20},{20,19},{21,22},{22,21},{23,24},{2... | collective-permute-start | bytes 24584 | tf_op jit(solution)/shard_map/ppermute | solution.py:322
  34.0 0.3 collective-permute-done.6.relay_ref
  34.3 0.1 shard_map.80
  34.4 3.9 %collective-permute-start.8 = (bf16[32,128]{1,0:T(8,128)(2,1)S(1)}, bf16[32,128]{1,0:T(8,128)(2,1)S(1)}, u32[]{:S(2)}, u32[]{:S(2)}) collective-permute-start(bf16[32,128]{1,0:T(8,128)(2,1)S(1)} %shard_map.80), channel_id=1, source_target_pairs={{0,1},{1,0},{2,3},{3,2},{4,5},{5,4},{6,7},{7,6},{8,9},{9,8},{10,11... | collective-permute-start | bytes 24584 | tf_op jit(solution)/shard_map/ppermute | solution.py:322
  38.3 0.0 collective-permute-done.9.two_ref
  38.3 0.0 collective-permute-done.7.far_ref
  38.3 0.8 %collective-permute-done.8.near_ref = bf16[32,128]{1,0:T(8,128)(2,1)S(1)} collective-permute-done((bf16[32,128]{1,0:T(8,128)(2,1)S(1)}, bf16[32,128]{1,0:T(8,128)(2,1)S(1)}, u32[]{:S(2)}, u32[]{:S(2)}) %collective-permute-start.8) | collective-permute-done | bytes 8224 | tf_op jit(solution)/shard_map/ppermute | solution.py:322
  39.1 2.5 %shard_map.81 = (f32[6,64,128]{2,1,0:T(8,128)}, f32[4,64,128]{2,1,0:T(8,128)}) custom-call(bf16[3,64,128]{2,1,0:T(8,128)(2,1)S(1)} %bitcast.11, s32[64,128]{1,0:T(8,128)S(1)} %bitcast.15, s32[64,128]{1,0:T(8,128)S(1)} %bitcast.20, bf16[608,128]{1,0:T(8,128)(2,1)S(1)} %collective-permute-done.lo_ref, bf16[608,128]{1,0:T(8,128)(2,1)S(1)} %collective-permute-done.1.wrap_ref, ...), custom_call_target="tpu_custom_call" | custom-call | bytes 400000 | tf_op jit(solution)/shard_map/pallas_call | solution.py:357
  (17 shorter events, 0.0 us)
Async XLA Ops:
  0.6 11.5 %copy-start = (bf16[3,8,8,128]{3,2,1,0:T(8,128)(2,1)S(1)}, bf16[3,8,8,128]{3,2,1,0:T(8,128)(2,1)}, u32[]{:S(2)}) copy-start(bf16[3,8,8,128]{3,2,1,0:T(8,128)(2,1)} %param.6) | copy-start | bytes 147460
  0.6 11.5 %copy-start.1 = (s32[8,8,128]{2,1,0:T(8,128)S(1)}, s32[8,8,128]{2,1,0:T(8,128)}, u32[]{:S(2)}) copy-start(s32[8,8,128]{2,1,0:T(8,128)} %param.10) | copy-start | bytes 98308
  2.4 9.8 %collective-permute-start = (bf16[608,128]{1,0:T(8,128)(2,1)}, bf16[608,128]{1,0:T(8,128)(2,1)S(1)}, u32[]{:S(2)}, u32[]{:S(2)}) collective-permute-start(bf16[608,128]{1,0:T(8,128)(2,1)} %get-tuple-element.12), channel_id=1, source_target_pairs={{0,16},{1,17},{2,18},{3,19},{4,20},{5,21},{6,22},{7,23},{8,24},{9,... | collective-permute-start | bytes 466952 | tf_op jit(solution)/shard_map/ppermute | solution.py:322
  6.8 5.4 %collective-permute-start.2 = (bf16[96,128]{1,0:T(8,128)(2,1)}, bf16[96,128]{1,0:T(8,128)(2,1)S(1)}, u32[]{:S(2)}, u32[]{:S(2)}) collective-permute-start(bf16[96,128]{1,0:T(8,128)(2,1)} %get-tuple-element.13.head_ref), channel_id=1, source_target_pairs={{16,0},{17,1},{18,2},{19,3},{20,4},{21,5},{22,6},{23,7},{24,8},{25... | collective-permute-start | bytes 73736 | tf_op jit(solution)/shard_map/ppermute | solution.py:322
  8.1 25.9 %collective-permute-start.1 = (bf16[608,128]{1,0:T(8,128)(2,1)}, bf16[608,128]{1,0:T(8,128)(2,1)S(1)}, u32[]{:S(2)}, u32[]{:S(2)}) collective-permute-start(bf16[608,128]{1,0:T(8,128)(2,1)} %get-tuple-element.12), channel_id=1, source_target_pairs={{112,128},{113,129},{114,130},{115,131},{116,132},{117,133},{118,1... | collective-permute-start | bytes 466952 | tf_op jit(solution)/shard_map/ppermute | solution.py:322
  9.4 20.5 %collective-permute-start.4 = (bf16[256,128]{1,0:T(8,128)(2,1)}, bf16[256,128]{1,0:T(8,128)(2,1)S(1)}, u32[]{:S(2)}, u32[]{:S(2)}) collective-permute-start(bf16[256,128]{1,0:T(8,128)(2,1)} %get-tuple-element.16), channel_id=1, source_target_pairs={{112,143},{113,130},{114,129},{115,132},{116,131},{117,134},{118,1... | collective-permute-start | bytes 196616 | tf_op jit(solution)/shard_map/ppermute | solution.py:322
  10.7 17.6 %copy-start.7 = (s16[256,128]{1,0:T(8,128)(2,1)S(1)}, s16[256,128]{1,0:T(8,128)(2,1)}, u32[]{:S(2)}) copy-start(s16[256,128]{1,0:T(8,128)(2,1)} %get-tuple-element.17) | copy-start | bytes 196612
  10.7 19.5 %copy-start.6 = (bf16[96,128]{1,0:T(8,128)(2,1)S(1)}, bf16[96,128]{1,0:T(8,128)(2,1)}, u32[]{:S(2)}) copy-start(bf16[96,128]{1,0:T(8,128)(2,1)} %get-tuple-element.13.head_ref) | copy-start | bytes 73732
  10.7 19.2 %collective-permute-start.5 = (s16[256,128]{1,0:T(8,128)(2,1)}, s16[256,128]{1,0:T(8,128)(2,1)S(1)}, u32[]{:S(2)}, u32[]{:S(2)}) collective-permute-start(s16[256,128]{1,0:T(8,128)(2,1)} %get-tuple-element.17), channel_id=1, source_target_pairs={{96,128},{97,129},{98,130},{99,131},{100,132},{101,133},{102,134},... | collective-permute-start | bytes 196616 | tf_op jit(solution)/shard_map/ppermute | solution.py:322
  12.3 17.9 %collective-permute-start.3 = (bf16[128,128]{1,0:T(8,128)(2,1)S(1)}, bf16[128,128]{1,0:T(8,128)(2,1)S(1)}, u32[]{:S(2)}, u32[]{:S(2)}) collective-permute-start(bf16[128,128]{1,0:T(8,128)(2,1)S(1)} %get-tuple-element.14), channel_id=1, source_target_pairs={{0,15},{1,2},{2,1},{3,4},{4,3},{5,6},{6,5},{7,8},{8,7},{9,10},{10,... | collective-permute-start | bytes 98312 | tf_op jit(solution)/shard_map/ppermute | solution.py:322
  28.3 10.0 %collective-permute-start.9 = (s16[256,128]{1,0:T(8,128)(2,1)S(1)}, s16[256,128]{1,0:T(8,128)(2,1)S(1)}, u32[]{:S(2)}, u32[]{:S(2)}) collective-permute-start(s16[256,128]{1,0:T(8,128)(2,1)S(1)} %copy-done.7), channel_id=1, source_target_pairs={{0,32},{1,33},{2,34},{3,35},{4,36},{5,37},{6,38},{7,39},{8,40},{9,... | collective-permute-start | bytes 196616 | tf_op jit(solution)/shard_map/ppermute | solution.py:322
  30.3 4.0 %collective-permute-start.6 = (bf16[192,128]{1,0:T(8,128)(2,1)S(1)}, bf16[192,128]{1,0:T(8,128)(2,1)S(1)}, u32[]{:S(2)}, u32[]{:S(2)}) collective-permute-start(bf16[192,128]{1,0:T(8,128)(2,1)S(1)} %get-tuple-element.18), channel_id=1, source_target_pairs={{0,511},{1,498},{2,497},{3,500},{4,499},{5,502},{6,501},{7,504},{8... | collective-permute-start | bytes 147464 | tf_op jit(solution)/shard_map/ppermute | solution.py:322
  33.1 6.0 %copy-start.2 = (f32[2,8,8,128]{3,2,1,0:T(8,128)S(1)}, f32[2,8,8,128]{3,2,1,0:T(8,128)}, u32[]{:S(2)}) copy-start(f32[2,8,8,128]{3,2,1,0:T(8,128)} %param.7) | copy-start | bytes 196612
  33.2 6.0 %copy-start.3 = (f32[2,8,8,128]{3,2,1,0:T(8,128)S(1)}, f32[2,8,8,128]{3,2,1,0:T(8,128)}, u32[]{:S(2)}) copy-start(f32[2,8,8,128]{3,2,1,0:T(8,128)} %param.8) | copy-start | bytes 196612
  33.2 5.9 %copy-start.4 = (s32[8,8,128]{2,1,0:T(8,128)S(1)}, s32[8,8,128]{2,1,0:T(8,128)}, u32[]{:S(2)}) copy-start(s32[8,8,128]{2,1,0:T(8,128)} %param.11) | copy-start | bytes 98308
  33.2 5.9 %copy-start.5 = (s32[8,8,16]{2,1,0:T(8,128)S(1)}, s32[8,8,16]{2,1,0:T(8,128)}, u32[]{:S(2)}) copy-start(s32[8,8,16]{2,1,0:T(8,128)} %param.9) | copy-start | bytes 12292
  33.2 5.1 %collective-permute-start.7 = (bf16[32,128]{1,0:T(8,128)(2,1)S(1)}, bf16[32,128]{1,0:T(8,128)(2,1)S(1)}, u32[]{:S(2)}, u32[]{:S(2)}) collective-permute-start(bf16[32,128]{1,0:T(8,128)(2,1)S(1)} %get-tuple-element.19), channel_id=1, source_target_pairs={{16,31},{17,18},{18,17},{19,20},{20,19},{21,22},{22,21},{23,24},{2... | collective-permute-start | bytes 24584 | tf_op jit(solution)/shard_map/ppermute | solution.py:322
  34.4 4.7 %collective-permute-start.8 = (bf16[32,128]{1,0:T(8,128)(2,1)S(1)}, bf16[32,128]{1,0:T(8,128)(2,1)S(1)}, u32[]{:S(2)}, u32[]{:S(2)}) collective-permute-start(bf16[32,128]{1,0:T(8,128)(2,1)S(1)} %shard_map.80), channel_id=1, source_target_pairs={{0,1},{1,0},{2,3},{3,2},{4,5},{5,4},{6,7},{7,6},{8,9},{9,8},{10,11... | collective-permute-start | bytes 24584 | tf_op jit(solution)/shard_map/ppermute | solution.py:322

commit v6 on v5

--- a/solution.py
+++ b/solution.py
@@ -17,6 +17,9 @@
 PACK_LIMIT = 60 * 1024 * 1024
 BIG = 1_000_000_000
 SIDE = 256
+ROWS_A = 7
+ROWS_B = 4
+ROWS_C = 2
 
 
 def row(ref, x, lead=None):
@@ -107,15 +110,20 @@
     return ref[pl.ds(0, n), :].astype(F32)
 
 
-def far_kernel(vel_ref, solid_ref, lo_ref, hi_ref, wide_ref, strip_ref, scratch):
+def wide_kernel(vel_ref, solid_ref, hi_ref, wide_ref, scratch):
     own = own_rows(vel_ref, solid_ref, scratch)
-    rows = all_rows(own, lead(lo_ref, 96), lead(hi_ref, 96))
+    hi = lead(hi_ref, 96)
+    left, right = edges(all_rows(own, jnp.zeros_like(hi), hi), 0)
+    _, even = place()
+    wide_ref[pl.ds(96, 32), :] = jnp.where(even, left, right).astype(BF16)
+    wide_ref[pl.ds(0, 96), :] = jnp.concatenate([own[c][x] for c in range(3) for x in range(4)], axis=0).astype(BF16)
+
+
+def far_kernel(vel_ref, solid_ref, lo_ref, hi_ref, strip_ref, scratch):
+    rows = all_rows(own_rows(vel_ref, solid_ref, scratch), lead(lo_ref, 96), lead(hi_ref, 96))
     left, right = edges(rows, 0)
     _, even = place()
-    strip = jnp.where(even, left, right).astype(BF16)
-    strip_ref[...] = strip
-    wide_ref[pl.ds(96, 32), :] = strip
-    wide_ref[pl.ds(0, 96), :] = jnp.concatenate([own[c][x] for c in range(3) for x in range(4)], axis=0).astype(BF16)
+    strip_ref[...] = jnp.where(even, left, right).astype(BF16)
 
 
 def relay_kernel(wide_ref, strip_ref, head_ref, side_ref, two_ref, relay_ref, strip_out):
@@ -135,13 +143,13 @@
 
 def shift_y(a, b, k, lane):
     if k > 0:
-        return pltpu.roll(jnp.where(lane < k, b, a), 128 - k, 1)
-    return pltpu.roll(jnp.where(lane >= 128 + k, b, a), -k, 1)
+        return pltpu.roll(jnp.where(lane < k, b, a), 128 - k, a.ndim - 1)
+    return pltpu.roll(jnp.where(lane >= 128 + k, b, a), -k, a.ndim - 1)
 
 
 def diff_z(f, sub):
-    up = jnp.where(sub == 7, f, pltpu.roll(f, 7, 0))
-    down = jnp.where(sub == 0, f, pltpu.roll(f, 1, 0))
+    up = jnp.where(sub == 7, f, pltpu.roll(f, 7, f.ndim - 2))
+    down = jnp.where(sub == 0, f, pltpu.roll(f, 1, f.ndim - 2))
     return up - down
 
 
@@ -192,7 +200,8 @@
     core = all_rows(own_rows(vel_ref, solid_ref, scratch), lo, hi)
     near = near_ref[...].astype(F32).reshape(4, 8, 128)
     far = jnp.where(run == 0, wide_ref[pl.ds(96, 32), :].astype(F32), far_ref[...].astype(F32)).reshape(4, 8, 128)
-    below = lead(side_ref, 96).reshape(3, 4, 8, 128)
+    lower = (lax.axis_index("gy") & 3) < 2
+    below = jnp.where(lower, lead(side_ref, 96), lead(lo_ref, 96)).reshape(3, 4, 8, 128)
     above = relay_ref[pl.ds(96, 96), :].astype(F32).reshape(3, 4, 8, 128)
     edge = []
     for c in range(3):
@@ -208,76 +217,75 @@
             if i > 10:
                 value = jnp.where((run == 7) & ((lane >= 64) == even), above[c, i - 11], value)
             rows.append(value)
-        edge.append(rows)
-    vn, vw, vdn, vdw = ([[None] * 14 for _ in range(3)] for _ in range(4))
-    near_y = [[None] * 14 for _ in range(3)]
-    for c in range(3):
-        for i in range(14):
-            a, b = core[c][i], edge[c][i]
+        edge.append(jnp.stack(rows))
+    core = [jnp.stack(rows) for rows in core]
+
+    def chunks(first, last, size):
+        return [(k, min(k + size, last)) for k in range(first, last, size)]
+
+    flow = [[[] for _ in range(5)] for _ in range(3)]
+    for lo_i, hi_i in chunks(0, 14, ROWS_A):
+        for c in range(3):
+            a, b = core[c][lo_i:hi_i], edge[c][lo_i:hi_i]
             p1, m1 = shift_y(a, b, 1, lane), shift_y(a, b, -1, lane)
             p2, m2 = shift_y(a, b, 2, lane), shift_y(a, b, -2, lane)
+            p3, m3 = shift_y(a, b, 3, lane), shift_y(a, b, -3, lane)
             s1, d1, s2, d2 = p1 + m1, p1 - m1, p2 + m2, p2 - m2
-            near_y[c][i] = d1
-            if 1 <= i <= 12:
-                vn[c][i] = a + a + s1
             t = a + s1
-            vw[c][i] = t + t + s2
-            if 2 <= i <= 11:
-                vdn[c][i] = d1 + d1 + d2
-            if 1 <= i <= 12:
-                d3 = shift_y(a, b, 3, lane) - shift_y(a, b, -3, lane)
-                vdw[c][i] = d1 + d2 + d2 + d3
-    yn, yw = [None] * 14, [None] * 14
-    own_flux = [None] * 14
-    for i in range(1, 13):
+            for k, v in enumerate((a + t, t + t + s2, d1 + d1 + d2, d1 + d2 + d2 + (p3 - m3), d1)):
+                flow[c][k].append(v)
+    flow = [[jnp.concatenate(v, axis=0) for v in per] for per in flow]
+    yn, yw, own_flux = ([[] for _ in range(k)] for k in (12, 12, 6))
+    for lo_i, hi_i in chunks(1, 13, ROWS_B):
         flux = []
         for t, o in ((core, edge), (edge, core)):
-            dx = [t[c][i + 1] - t[c][i - 1] for c in range(3)]
+            mid = [t[c][lo_i:hi_i] for c in range(3)]
+            dx = [t[c][lo_i + 1 : hi_i + 1] - t[c][lo_i - 1 : hi_i - 1] for c in range(3)]
             if t is core:
-                dy = [near_y[c][i] for c in range(3)]
+                dy = [flow[c][4][lo_i:hi_i] for c in range(3)]
             else:
-                dy = [shift_y(t[c][i], o[c][i], 1, lane) - shift_y(t[c][i], o[c][i], -1, lane) for c in range(3)]
-            dz = [diff_z(t[c][i], sub) for c in range(3)]
+                oth = [o[c][lo_i:hi_i] for c in range(3)]
+                dy = [shift_y(mid[c], oth[c], 1, lane) - shift_y(mid[c], oth[c], -1, lane) for c in range(3)]
+            dz = [diff_z(mid[c], sub) for c in range(3)]
             s, mag = strain(dx, dy, dz)
-            prods = [t[p][i] * t[q][i] for p, q in PAIRS]
-            flux.append(prods + [mag * e for e in s])
-        own_flux[i] = flux[0][6:]
-        ns, ws = [], []
-        for a, b in zip(*flux):
+            flux.append([mid[p] * mid[q] for p, q in PAIRS] + [mag * e for e in s])
+        for k in range(6):
+            own_flux[k].append(flux[0][6 + k])
+        for k, (a, b) in enumerate(zip(*flux)):
             s1 = shift_y(a, b, 1, lane) + shift_y(a, b, -1, lane)
             s2 = shift_y(a, b, 2, lane) + shift_y(a, b, -2, lane)
             t = a + s1
-            ns.append(a + t)
-            ws.append(t + t + s2)
-        yn[i], yw[i] = ns, ws
-
-    def filt_n(r, i):
-        return (r[i - 1] + r[i + 1] + (r[i] + r[i])) * 0.0625
-
-    def filt_w(r, i):
-        t = r[i - 1] + r[i] + r[i + 1]
-        return (r[i - 2] + r[i + 2] + (t + t)) * 0.015625
-
-    def column(r, k):
-        return [None if v is None else v[k] for v in r]
-
-    un = [[filt_n(vn[c], i) if 2 <= i <= 11 else None for i in range(14)] for c in range(3)]
-    uw = [[filt_w(vw[c], i) if 2 <= i <= 11 else None for i in range(14)] for c in range(3)]
-    for x in range(8):
-        i = x + 3
+            yn[k].append(a + t)
+            yw[k].append(t + t + s2)
+    yn, yw, own_flux = ([jnp.concatenate(v, axis=0) for v in g] for g in (yn, yw, own_flux))
+
+    def filt_n(r, base, lo_i, hi_i):
+        at = lambda k: r[lo_i + k - base : hi_i + k - base]
+        return (at(-1) + at(1) + (at(0) + at(0))) * 0.0625
+
+    def filt_w(r, base, lo_i, hi_i):
+        at = lambda k: r[lo_i + k - base : hi_i + k - base]
+        t = at(-1) + at(0) + at(1)
+        return (at(-2) + at(2) + (t + t)) * 0.015625
+
+    un = [filt_n(flow[c][0], 0, 2, 12) for c in range(3)]
+    uw = [filt_w(flow[c][1], 0, 2, 12) for c in range(3)]
+    for lo_i, hi_i in chunks(3, 11, ROWS_C):
         result = []
-        for u, ydiff, filt, flux, factor in ((un, vdn, filt_n, yn, 4.0), (uw, vdw, filt_w, yw, 16.0)):
-            dx = [u[c][i + 1] - u[c][i - 1] for c in range(3)]
-            dy = [filt(ydiff[c], i) for c in range(3)]
-            dz = [diff_z(u[c][i], sub) for c in range(3)]
+        for u, which, filt, flux, factor in ((un, 2, filt_n, yn, 4.0), (uw, 3, filt_w, yw, 16.0)):
+            mid = [u[c][lo_i - 2 : hi_i - 2] for c in range(3)]
+            dx = [u[c][lo_i - 1 : hi_i - 1] - u[c][lo_i - 3 : hi_i - 3] for c in range(3)]
+            dy = [filt(flow[c][which], 0, lo_i, hi_i) for c in range(3)]
+            dz = [diff_z(mid[c], sub) for c in range(3)]
             s, mag = strain(dx, dy, dz)
-            f = [filt(column(flux, k), i) for k in range(12)]
-            lhs = [f[k] - u[p][i] * u[q][i] for k, (p, q) in enumerate(PAIRS)]
+            f = [filt(flux[k], 1, lo_i, hi_i) for k in range(12)]
+            lhs = [f[k] - mid[p] * mid[q] for k, (p, q) in enumerate(PAIRS)]
             fm = factor * mag
             rhs = [f[6 + k] - fm * s[k] for k in range(6)]
             result.append((2.0 * contract(lhs, rhs), 4.0 * contract(rhs, rhs)))
         (lm, mm), (qn, nn) = result
-        o_lm, o_qn, o_mm, o_nn = (row(old, x, f) for f in range(4))
+        span = range(lo_i - 3, hi_i - 3)
+        o_lm, o_qn, o_mm, o_nn = (jnp.stack([row(old, x, f) for x in span]) for f in range(4))
         wn = relax_weight(o_lm * o_mm)
         ww = relax_weight(o_qn * o_nn)
         new_lm = wn * lm + (1.0 - wn) * o_lm
@@ -287,13 +295,17 @@
         c2 = jnp.maximum(new_lm, 0.0) / new_mm
         c4 = jnp.maximum(new_qn, 0.0) / new_nn
         cs = c2 * c2 / jnp.maximum(jnp.maximum(c4, 0.125 * c2), RATIO_FLOOR)
-        cs = jnp.where(row(clip_ref, x) == 1, jnp.minimum(cs, CLIP_CAP), cs)
-        cs = jnp.where(row(solid_ref, x) == 1, 0.0, -2.0 * cs)
-        at = (pl.ds(x, 8, stride=8), slice(None))
-        for k in range(6):
-            stress_ref[(k,) + at] = cs * own_flux[i][k]
-        for k, v in enumerate((new_lm, new_mm, new_qn, new_nn)):
-            new_ref[(k,) + at] = v
+        clipped = jnp.stack([row(clip_ref, x) for x in span]) == 1
+        blocked = jnp.stack([row(solid_ref, x) for x in span]) == 1
+        cs = jnp.where(clipped, jnp.minimum(cs, CLIP_CAP), cs)
+        cs = jnp.where(blocked, 0.0, -2.0 * cs)
+        out = [cs * own_flux[k][lo_i - 1 : hi_i - 1] for k in range(6)]
+        for j, x in enumerate(span):
+            at = (pl.ds(x, 8, stride=8), slice(None))
+            for k in range(6):
+                stress_ref[(k,) + at] = out[k][j]
+            for k, v in enumerate((new_lm, new_mm, new_qn, new_nn)):
+                new_ref[(k,) + at] = v[j]
 
 
 VM = pl.BlockSpec(memory_space=pltpu.VMEM)
@@ -310,6 +322,10 @@
 
 def far_side(gy):
     return (gy + 1) % 16 if gy % 2 else (gy - 1) % 16
+
+
+def low(gy):
+    return gy % 4 < 2
 
 
 def send(x, target):
@@ -341,13 +357,14 @@
          trans, pltpu.SemaphoreType.DMA((4,))],
         PACK_LIMIT,
     )(vel, solid, lq, mn)
-    lo = send(tail, lambda run, gx, gy: (gx + 1, gy) if run < 7 else None)
+    lo = send(tail, lambda run, gx, gy: (gx + 1, gy) if run < 7 else (gx + 1, far_side(gy)) if low(gy) else None)
     hi = send(head, lambda run, gx, gy: (gx - 1, gy) if run > 0 else None)
-    side = send(side, lambda run, gx, gy: (gx + 1, far_side(gy)) if run == 7 else None)
+    side = send(side, lambda run, gx, gy: (gx + 1, far_side(gy)) if run == 7 and not low(gy) else None)
     wrap = send(tail, lambda run, gx, gy: (gx + 1, gy) if run == 7 else None)
     two_wrap = send(code, lambda run, gx, gy: (gx + 2, gy) if run == 6 else None)
     two = send(code, lambda run, gx, gy: (gx + 2, gy) if run != 6 else None)
-    wide, strip = call(far_kernel, [sds((128, 128), BF16), strip_type], [VM] * 4, [trans], flops=BIG)(vel, solid, lo, hi)
+    (wide,) = call(wide_kernel, [sds((128, 128), BF16)], [VM] * 3, [trans], flops=BIG)(vel, solid, hi)
+    (strip,) = call(far_kernel, [strip_type], [VM] * 4, [trans])(vel, solid, lo, hi)
     wide = send(wide, lambda run, gx, gy: (gx, far_side(gy)) if run == 0 else None)
     relay, strip = call(relay_kernel, [sds((192, 128), BF16), strip_type], [VM] * 5, [])(wide, strip, head, side, two_wrap)
     relay = send(relay, lambda run, gx, gy: (gx - 1, far_side(gy)) if run == 0 else None)

time: 42.4 us -> 41.9 us (0.988)
  no operation moved by 1% of the time
where the time goes in v6:
time: 41.9 us; the launch traced here: 41.4 us
  starting transfers between devices  34.7 us (83%)
  Pallas kernels  4.25 us (10%)
  waiting for transfers between devices  1.54 us (4%)
  between operations  0.88 us (2%)
    ppermute x10, starting transfers between devices, send(): return lax.ppermute(x, ('gx', 'gy'), pairs)  34.7 us
    pallas_call x1, Pallas kernels, local(): call(main_kernel, [sds((6, 64, 128), F32), sds((4, 64, 128), F32)], [VM]...  2.12 us
    pallas_call x1, Pallas kernels, local(): call(pack_kernel, [sds((608, 128), BF16), sds((96, 128), BF16), sds((SIDE...  1.76 us
    ppermute x10, waiting for transfers between devices, send(): return lax.ppermute(x, ('gx', 'gy'), pairs)  1.54 us
  transfers between devices with their start and end apart: 10, of which 4 were waited for; matrix products, arithmetic and copies ran while one was open for 0% of the time, Pallas kernels for 1%

profile of v6, /device:TPU:1, one launch (start us, length us, event | category | flops | bytes accessed | tf_op | source)
XLA Modules:
  0.0 41.4 jit_solution(4639793218364512761)
XLA Ops:
  0.6 1.8 %shard_map.77 = (bf16[608,128]{1,0:T(8,128)(2,1)}, bf16[96,128]{1,0:T(8,128)(2,1)}, bf16[256,128]{1,0:T(8,128)(2,1)}, s16[256,128]{1,0:T(8,128)(2,1)}) custom-call(bf16[3,64,128]{2,1,0:T(8,128)(2,1)} %bitcast.8, s32[64,128]{1,0:T(8,128)} %bitcast.13, f32[128,128]{1,0:T(8,128)} %bitcast.18, f32[128,128]{1,0:T(8,128)} %bitcast.20), custom_call_target="tpu_custom_call" | custom-call | bytes 400000 | tf_op jit(solution)/shard_map/pallas_call | solution.py:352
  2.4 4.4 %collective-permute-start = (bf16[608,128]{1,0:T(8,128)(2,1)}, bf16[608,128]{1,0:T(8,128)(2,1)S(1)}, u32[]{:S(2)}, u32[]{:S(2)}) collective-permute-start(bf16[608,128]{1,0:T(8,128)(2,1)} %get-tuple-element.10), channel_id=1, source_target_pairs={{0,16},{1,17},{2,18},{3,19},{4,20},{5,21},{6,22},{7,23},{8,24},{9,... | collective-permute-start | bytes 466952 | tf_op jit(solution)/shard_map/ppermute | solution.py:338
  6.8 1.3 %collective-permute-start.2 = (bf16[96,128]{1,0:T(8,128)(2,1)}, bf16[96,128]{1,0:T(8,128)(2,1)S(1)}, u32[]{:S(2)}, u32[]{:S(2)}) collective-permute-start(bf16[96,128]{1,0:T(8,128)(2,1)} %get-tuple-element.11.head_ref), channel_id=1, source_target_pairs={{16,0},{17,1},{18,2},{19,3},{20,4},{21,5},{22,6},{23,7},{24,8},{25... | collective-permute-start | bytes 73736 | tf_op jit(solution)/shard_map/ppermute | solution.py:338
  8.1 1.3 %collective-permute-start.1 = (bf16[608,128]{1,0:T(8,128)(2,1)}, bf16[608,128]{1,0:T(8,128)(2,1)S(1)}, u32[]{:S(2)}, u32[]{:S(2)}) collective-permute-start(bf16[608,128]{1,0:T(8,128)(2,1)} %get-tuple-element.10), channel_id=1, source_target_pairs={{112,128},{113,129},{114,130},{115,131},{116,132},{117,133},{118,1... | collective-permute-start | bytes 466952 | tf_op jit(solution)/shard_map/ppermute | solution.py:338
  9.4 1.3 %collective-permute-start.4 = (bf16[256,128]{1,0:T(8,128)(2,1)}, bf16[256,128]{1,0:T(8,128)(2,1)S(1)}, u32[]{:S(2)}, u32[]{:S(2)}) collective-permute-start(bf16[256,128]{1,0:T(8,128)(2,1)} %get-tuple-element.12), channel_id=1, source_target_pairs={{114,129},{115,132},{118,133},{119,136},{122,137},{123,140},{126,1... | collective-permute-start | bytes 196616 | tf_op jit(solution)/shard_map/ppermute | solution.py:338
  10.7 1.4 %collective-permute-start.5 = (s16[256,128]{1,0:T(8,128)(2,1)}, s16[256,128]{1,0:T(8,128)(2,1)S(1)}, u32[]{:S(2)}, u32[]{:S(2)}) collective-permute-start(s16[256,128]{1,0:T(8,128)(2,1)} %get-tuple-element.13), channel_id=1, source_target_pairs={{96,128},{97,129},{98,130},{99,131},{100,132},{101,133},{102,134},... | collective-permute-start | bytes 196616 | tf_op jit(solution)/shard_map/ppermute | solution.py:338
  12.2 0.1 shard_map.78
  12.3 15.9 %collective-permute-start.3 = (bf16[128,128]{1,0:T(8,128)(2,1)S(1)}, bf16[128,128]{1,0:T(8,128)(2,1)S(1)}, u32[]{:S(2)}, u32[]{:S(2)}) collective-permute-start(bf16[128,128]{1,0:T(8,128)(2,1)S(1)} %shard_map.78), channel_id=1, source_target_pairs={{0,15},{1,2},{2,1},{3,4},{4,3},{5,6},{6,5},{7,8},{8,7},{9,10},{10,... | collective-permute-start | bytes 98312 | tf_op jit(solution)/shard_map/ppermute | solution.py:338
  28.3 0.0 collective-permute-done.lo_ref
  28.3 1.3 %collective-permute-start.9 = (s16[256,128]{1,0:T(8,128)(2,1)S(1)}, s16[256,128]{1,0:T(8,128)(2,1)S(1)}, u32[]{:S(2)}, u32[]{:S(2)}) collective-permute-start(s16[256,128]{1,0:T(8,128)(2,1)S(1)} %copy-done.7), channel_id=1, source_target_pairs={{0,32},{1,33},{2,34},{3,35},{4,36},{5,37},{6,38},{7,39},{8,40},{9,... | collective-permute-start | bytes 196616 | tf_op jit(solution)/shard_map/ppermute | solution.py:338
  29.6 0.1 shard_map.79.strip_ref
  29.7 0.2 collective-permute-done.3.wide_ref
  29.9 0.2 collective-permute-done.4.side_ref
  30.2 3.1 %collective-permute-start.6 = (bf16[192,128]{1,0:T(8,128)(2,1)S(1)}, bf16[192,128]{1,0:T(8,128)(2,1)S(1)}, u32[]{:S(2)}, u32[]{:S(2)}) collective-permute-start(bf16[192,128]{1,0:T(8,128)(2,1)S(1)} %get-tuple-element.14), channel_id=1, source_target_pairs={{0,511},{1,498},{2,497},{3,500},{4,499},{5,502},{6,501},{7,504},{8... | collective-permute-start | bytes 147464 | tf_op jit(solution)/shard_map/ppermute | solution.py:338
  33.3 0.0 copy-start.2
  33.3 0.0 copy-start.3
  33.3 0.0 copy-start.4
  33.3 0.0 copy-start.5
  33.3 0.8 %collective-permute-start.7 = (bf16[32,128]{1,0:T(8,128)(2,1)S(1)}, bf16[32,128]{1,0:T(8,128)(2,1)S(1)}, u32[]{:S(2)}, u32[]{:S(2)}) collective-permute-start(bf16[32,128]{1,0:T(8,128)(2,1)S(1)} %get-tuple-element.15), channel_id=1, source_target_pairs={{16,31},{17,18},{18,17},{19,20},{20,19},{21,22},{22,21},{23,24},{2... | collective-permute-start | bytes 24584 | tf_op jit(solution)/shard_map/ppermute | solution.py:338
  34.1 0.3 collective-permute-done.6.relay_ref
  34.4 0.1 shard_map.81
  34.6 3.8 %collective-permute-start.8 = (bf16[32,128]{1,0:T(8,128)(2,1)S(1)}, bf16[32,128]{1,0:T(8,128)(2,1)S(1)}, u32[]{:S(2)}, u32[]{:S(2)}) collective-permute-start(bf16[32,128]{1,0:T(8,128)(2,1)S(1)} %shard_map.81), channel_id=1, source_target_pairs={{0,1},{1,0},{2,3},{3,2},{4,5},{5,4},{6,7},{7,6},{8,9},{9,8},{10,11... | collective-permute-start | bytes 24584 | tf_op jit(solution)/shard_map/ppermute | solution.py:338
  38.4 0.8 %collective-permute-done.8.near_ref = bf16[32,128]{1,0:T(8,128)(2,1)S(1)} collective-permute-done((bf16[32,128]{1,0:T(8,128)(2,1)S(1)}, bf16[32,128]{1,0:T(8,128)(2,1)S(1)}, u32[]{:S(2)}, u32[]{:S(2)}) %collective-permute-start.8) | collective-permute-done | bytes 8224 | tf_op jit(solution)/shard_map/ppermute | solution.py:338
  39.2 2.1 %shard_map.82 = (f32[6,64,128]{2,1,0:T(8,128)}, f32[4,64,128]{2,1,0:T(8,128)}) custom-call(bf16[3,64,128]{2,1,0:T(8,128)(2,1)S(1)} %bitcast.12, s32[64,128]{1,0:T(8,128)S(1)} %bitcast.17, s32[64,128]{1,0:T(8,128)S(1)} %bitcast.22, bf16[608,128]{1,0:T(8,128)(2,1)S(1)} %collective-permute-done.lo_ref, bf16[608,128]{1,0:T(8,128)(2,1)S(1)} %collective-permute-done.1.wrap_ref, ...), custom_call_target="tpu_custom_call" | custom-call | bytes 400000 | tf_op jit(solution)/shard_map/pallas_call | solution.py:374
  (18 shorter events, 0.0 us)
Async XLA Ops:
  0.6 11.5 %copy-start = (bf16[3,8,8,128]{3,2,1,0:T(8,128)(2,1)S(1)}, bf16[3,8,8,128]{3,2,1,0:T(8,128)(2,1)}, u32[]{:S(2)}) copy-start(bf16[3,8,8,128]{3,2,1,0:T(8,128)(2,1)} %param.6) | copy-start | bytes 147460
  0.6 11.5 %copy-start.1 = (s32[8,8,128]{2,1,0:T(8,128)S(1)}, s32[8,8,128]{2,1,0:T(8,128)}, u32[]{:S(2)}) copy-start(s32[8,8,128]{2,1,0:T(8,128)} %param.10) | copy-start | bytes 98308
  2.4 25.8 %collective-permute-start = (bf16[608,128]{1,0:T(8,128)(2,1)}, bf16[608,128]{1,0:T(8,128)(2,1)S(1)}, u32[]{:S(2)}, u32[]{:S(2)}) collective-permute-start(bf16[608,128]{1,0:T(8,128)(2,1)} %get-tuple-element.10), channel_id=1, source_target_pairs={{0,16},{1,17},{2,18},{3,19},{4,20},{5,21},{6,22},{7,23},{8,24},{9,... | collective-permute-start | bytes 466952 | tf_op jit(solution)/shard_map/ppermute | solution.py:338
  6.8 5.3 %collective-permute-start.2 = (bf16[96,128]{1,0:T(8,128)(2,1)}, bf16[96,128]{1,0:T(8,128)(2,1)S(1)}, u32[]{:S(2)}, u32[]{:S(2)}) collective-permute-start(bf16[96,128]{1,0:T(8,128)(2,1)} %get-tuple-element.11.head_ref), channel_id=1, source_target_pairs={{16,0},{17,1},{18,2},{19,3},{20,4},{21,5},{22,6},{23,7},{24,8},{25... | collective-permute-start | bytes 73736 | tf_op jit(solution)/shard_map/ppermute | solution.py:338
  8.1 26.0 %collective-permute-start.1 = (bf16[608,128]{1,0:T(8,128)(2,1)}, bf16[608,128]{1,0:T(8,128)(2,1)S(1)}, u32[]{:S(2)}, u32[]{:S(2)}) collective-permute-start(bf16[608,128]{1,0:T(8,128)(2,1)} %get-tuple-element.10), channel_id=1, source_target_pairs={{112,128},{113,129},{114,130},{115,131},{116,132},{117,133},{118,1... | collective-permute-start | bytes 466952 | tf_op jit(solution)/shard_map/ppermute | solution.py:338
  9.4 20.8 %collective-permute-start.4 = (bf16[256,128]{1,0:T(8,128)(2,1)}, bf16[256,128]{1,0:T(8,128)(2,1)S(1)}, u32[]{:S(2)}, u32[]{:S(2)}) collective-permute-start(bf16[256,128]{1,0:T(8,128)(2,1)} %get-tuple-element.12), channel_id=1, source_target_pairs={{114,129},{115,132},{118,133},{119,136},{122,137},{123,140},{126,1... | collective-permute-start | bytes 196616 | tf_op jit(solution)/shard_map/ppermute | solution.py:338
  10.7 17.6 %copy-start.7 = (s16[256,128]{1,0:T(8,128)(2,1)S(1)}, s16[256,128]{1,0:T(8,128)(2,1)}, u32[]{:S(2)}) copy-start(s16[256,128]{1,0:T(8,128)(2,1)} %get-tuple-element.13) | copy-start | bytes 196612
  10.7 19.4 %collective-permute-start.5 = (s16[256,128]{1,0:T(8,128)(2,1)}, s16[256,128]{1,0:T(8,128)(2,1)S(1)}, u32[]{:S(2)}, u32[]{:S(2)}) collective-permute-start(s16[256,128]{1,0:T(8,128)(2,1)} %get-tuple-element.13), channel_id=1, source_target_pairs={{96,128},{97,129},{98,130},{99,131},{100,132},{101,133},{102,134},... | collective-permute-start | bytes 196616 | tf_op jit(solution)/shard_map/ppermute | solution.py:338
  12.3 17.9 %copy-start.6 = (bf16[96,128]{1,0:T(8,128)(2,1)S(1)}, bf16[96,128]{1,0:T(8,128)(2,1)}, u32[]{:S(2)}) copy-start(bf16[96,128]{1,0:T(8,128)(2,1)} %get-tuple-element.11.head_ref) | copy-start | bytes 73732
  12.3 17.6 %collective-permute-start.3 = (bf16[128,128]{1,0:T(8,128)(2,1)S(1)}, bf16[128,128]{1,0:T(8,128)(2,1)S(1)}, u32[]{:S(2)}, u32[]{:S(2)}) collective-permute-start(bf16[128,128]{1,0:T(8,128)(2,1)S(1)} %shard_map.78), channel_id=1, source_target_pairs={{0,15},{1,2},{2,1},{3,4},{4,3},{5,6},{6,5},{7,8},{8,7},{9,10},{10,... | collective-permute-start | bytes 98312 | tf_op jit(solution)/shard_map/ppermute | solution.py:338
  28.3 10.1 %collective-permute-start.9 = (s16[256,128]{1,0:T(8,128)(2,1)S(1)}, s16[256,128]{1,0:T(8,128)(2,1)S(1)}, u32[]{:S(2)}, u32[]{:S(2)}) collective-permute-start(s16[256,128]{1,0:T(8,128)(2,1)S(1)} %copy-done.7), channel_id=1, source_target_pairs={{0,32},{1,33},{2,34},{3,35},{4,36},{5,37},{6,38},{7,39},{8,40},{9,... | collective-permute-start | bytes 196616 | tf_op jit(solution)/shard_map/ppermute | solution.py:338
  30.2 4.3 %collective-permute-start.6 = (bf16[192,128]{1,0:T(8,128)(2,1)S(1)}, bf16[192,128]{1,0:T(8,128)(2,1)S(1)}, u32[]{:S(2)}, u32[]{:S(2)}) collective-permute-start(bf16[192,128]{1,0:T(8,128)(2,1)S(1)} %get-tuple-element.14), channel_id=1, source_target_pairs={{0,511},{1,498},{2,497},{3,500},{4,499},{5,502},{6,501},{7,504},{8... | collective-permute-start | bytes 147464 | tf_op jit(solution)/shard_map/ppermute | solution.py:338
  33.3 5.9 %copy-start.2 = (f32[2,8,8,128]{3,2,1,0:T(8,128)S(1)}, f32[2,8,8,128]{3,2,1,0:T(8,128)}, u32[]{:S(2)}) copy-start(f32[2,8,8,128]{3,2,1,0:T(8,128)} %param.7) | copy-start | bytes 196612
  33.3 5.9 %copy-start.3 = (f32[2,8,8,128]{3,2,1,0:T(8,128)S(1)}, f32[2,8,8,128]{3,2,1,0:T(8,128)}, u32[]{:S(2)}) copy-start(f32[2,8,8,128]{3,2,1,0:T(8,128)} %param.8) | copy-start | bytes 196612
  33.3 5.9 %copy-start.4 = (s32[8,8,128]{2,1,0:T(8,128)S(1)}, s32[8,8,128]{2,1,0:T(8,128)}, u32[]{:S(2)}) copy-start(s32[8,8,128]{2,1,0:T(8,128)} %param.11) | copy-start | bytes 98308
  33.3 5.9 %copy-start.5 = (s32[8,8,16]{2,1,0:T(8,128)S(1)}, s32[8,8,16]{2,1,0:T(8,128)}, u32[]{:S(2)}) copy-start(s32[8,8,16]{2,1,0:T(8,128)} %param.9) | copy-start | bytes 12292
  33.3 5.1 %collective-permute-start.7 = (bf16[32,128]{1,0:T(8,128)(2,1)S(1)}, bf16[32,128]{1,0:T(8,128)(2,1)S(1)}, u32[]{:S(2)}, u32[]{:S(2)}) collective-permute-start(bf16[32,128]{1,0:T(8,128)(2,1)S(1)} %get-tuple-element.15), channel_id=1, source_target_pairs={{16,31},{17,18},{18,17},{19,20},{20,19},{21,22},{22,21},{23,24},{2... | collective-permute-start | bytes 24584 | tf_op jit(solution)/shard_map/ppermute | solution.py:338
  34.6 4.7 %collective-permute-start.8 = (bf16[32,128]{1,0:T(8,128)(2,1)S(1)}, bf16[32,128]{1,0:T(8,128)(2,1)S(1)}, u32[]{:S(2)}, u32[]{:S(2)}) collective-permute-start(bf16[32,128]{1,0:T(8,128)(2,1)S(1)} %shard_map.81), channel_id=1, source_target_pairs={{0,1},{1,0},{2,3},{3,2},{4,5},{5,4},{6,7},{7,6},{8,9},{9,8},{10,11... | collective-permute-start | bytes 24584 | tf_op jit(solution)/shard_map/ppermute | solution.py:338

commit v7 on v6

--- a/solution.py
+++ b/solution.py
@@ -183,7 +183,8 @@
     tile = lo_ref[pl.ds(96, 256), :].astype(F32) + lo_ref[pl.ds(352, 256), :].astype(F32)
     wrap = wrap_ref[pl.ds(96, 256), :].astype(F32) + wrap_ref[pl.ds(352, 256), :].astype(F32)
     up1 = jnp.where(run == 0, wrap, tile).reshape(4, 64, 128)
-    up2 = decode(jnp.where(run == 0, two_wrap_ref[...].astype(jnp.int32), two_ref[...].astype(jnp.int32))).reshape(4, 64, 128)
+    lower = (lax.axis_index("gy") & 3) < 2
+    up2 = decode(jnp.where((run == 0) & lower, two_wrap_ref[...].astype(jnp.int32), two_ref[...].astype(jnp.int32))).reshape(4, 64, 128)
     for z in range(8):
         at = pl.ds(8 * z, 8)
         idx = local[8 * z : 8 * z + 8]
@@ -200,7 +201,6 @@
     core = all_rows(own_rows(vel_ref, solid_ref, scratch), lo, hi)
     near = near_ref[...].astype(F32).reshape(4, 8, 128)
     far = jnp.where(run == 0, wide_ref[pl.ds(96, 32), :].astype(F32), far_ref[...].astype(F32)).reshape(4, 8, 128)
-    lower = (lax.axis_index("gy") & 3) < 2
     below = jnp.where(lower, lead(side_ref, 96), lead(lo_ref, 96)).reshape(3, 4, 8, 128)
     above = relay_ref[pl.ds(96, 96), :].astype(F32).reshape(3, 4, 8, 128)
     edge = []
@@ -361,8 +361,8 @@
     hi = send(head, lambda run, gx, gy: (gx - 1, gy) if run > 0 else None)
     side = send(side, lambda run, gx, gy: (gx + 1, far_side(gy)) if run == 7 and not low(gy) else None)
     wrap = send(tail, lambda run, gx, gy: (gx + 1, gy) if run == 7 else None)
-    two_wrap = send(code, lambda run, gx, gy: (gx + 2, gy) if run == 6 else None)
-    two = send(code, lambda run, gx, gy: (gx + 2, gy) if run != 6 else None)
+    two_wrap = send(code, lambda run, gx, gy: (gx + 2, gy) if run == 6 and low(gy) else None)
+    two = send(code, lambda run, gx, gy: (gx + 2, gy) if run != 6 or not low(gy) else None)
     (wide,) = call(wide_kernel, [sds((128, 128), BF16)], [VM] * 3, [trans], flops=BIG)(vel, solid, hi)
     (strip,) = call(far_kernel, [strip_type], [VM] * 4, [trans])(vel, solid, lo, hi)
     wide = send(wide, lambda run, gx, gy: (gx, far_side(gy)) if run == 0 else None)

time: 41.9 us -> 41.9 us (level)
  no operation moved by 1% of the time
where the time goes in v7:
time: 41.9 us; the launch traced here: 41.4 us
  starting transfers between devices  34.7 us (83%)
  Pallas kernels  4.26 us (10%)
  waiting for transfers between devices  1.54 us (4%)
  between operations  0.88 us (2%)
    ppermute x10, starting transfers between devices, send(): return lax.ppermute(x, ('gx', 'gy'), pairs)  34.7 us
    pallas_call x1, Pallas kernels, local(): call(main_kernel, [sds((6, 64, 128), F32), sds((4, 64, 128), F32)], [VM]...  2.13 us
    pallas_call x1, Pallas kernels, local(): call(pack_kernel, [sds((608, 128), BF16), sds((96, 128), BF16), sds((SIDE...  1.76 us
    ppermute x10, waiting for transfers between devices, send(): return lax.ppermute(x, ('gx', 'gy'), pairs)  1.54 us
  transfers between devices with their start and end apart: 10, of which 4 were waited for; matrix products, arithmetic and copies ran while one was open for 0% of the time, Pallas kernels for 1%

profile of v7, /device:TPU:1, one launch (start us, length us, event | category | flops | bytes accessed | tf_op | source)
XLA Modules:
  0.0 41.4 jit_solution(12079119107466038026)
XLA Ops:
  0.6 1.8 %shard_map.77 = (bf16[608,128]{1,0:T(8,128)(2,1)}, bf16[96,128]{1,0:T(8,128)(2,1)}, bf16[256,128]{1,0:T(8,128)(2,1)}, s16[256,128]{1,0:T(8,128)(2,1)}) custom-call(bf16[3,64,128]{2,1,0:T(8,128)(2,1)} %bitcast.8, s32[64,128]{1,0:T(8,128)} %bitcast.13, f32[128,128]{1,0:T(8,128)} %bitcast.18, f32[128,128]{1,0:T(8,128)} %bitcast.20), custom_call_target="tpu_custom_call" | custom-call | bytes 400000 | tf_op jit(solution)/shard_map/pallas_call | solution.py:352
  2.4 4.4 %collective-permute-start = (bf16[608,128]{1,0:T(8,128)(2,1)}, bf16[608,128]{1,0:T(8,128)(2,1)S(1)}, u32[]{:S(2)}, u32[]{:S(2)}) collective-permute-start(bf16[608,128]{1,0:T(8,128)(2,1)} %get-tuple-element.10), channel_id=1, source_target_pairs={{0,16},{1,17},{2,18},{3,19},{4,20},{5,21},{6,22},{7,23},{8,24},{9,... | collective-permute-start | bytes 466952 | tf_op jit(solution)/shard_map/ppermute | solution.py:338
  6.8 1.3 %collective-permute-start.2 = (bf16[96,128]{1,0:T(8,128)(2,1)}, bf16[96,128]{1,0:T(8,128)(2,1)S(1)}, u32[]{:S(2)}, u32[]{:S(2)}) collective-permute-start(bf16[96,128]{1,0:T(8,128)(2,1)} %get-tuple-element.11.head_ref), channel_id=1, source_target_pairs={{16,0},{17,1},{18,2},{19,3},{20,4},{21,5},{22,6},{23,7},{24,8},{25... | collective-permute-start | bytes 73736 | tf_op jit(solution)/shard_map/ppermute | solution.py:338
  8.1 1.3 %collective-permute-start.1 = (bf16[608,128]{1,0:T(8,128)(2,1)}, bf16[608,128]{1,0:T(8,128)(2,1)S(1)}, u32[]{:S(2)}, u32[]{:S(2)}) collective-permute-start(bf16[608,128]{1,0:T(8,128)(2,1)} %get-tuple-element.10), channel_id=1, source_target_pairs={{112,128},{113,129},{114,130},{115,131},{116,132},{117,133},{118,1... | collective-permute-start | bytes 466952 | tf_op jit(solution)/shard_map/ppermute | solution.py:338
  9.4 1.3 %collective-permute-start.4 = (bf16[256,128]{1,0:T(8,128)(2,1)}, bf16[256,128]{1,0:T(8,128)(2,1)S(1)}, u32[]{:S(2)}, u32[]{:S(2)}) collective-permute-start(bf16[256,128]{1,0:T(8,128)(2,1)} %get-tuple-element.12), channel_id=1, source_target_pairs={{114,129},{115,132},{118,133},{119,136},{122,137},{123,140},{126,1... | collective-permute-start | bytes 196616 | tf_op jit(solution)/shard_map/ppermute | solution.py:338
  10.7 1.4 %collective-permute-start.5 = (s16[256,128]{1,0:T(8,128)(2,1)}, s16[256,128]{1,0:T(8,128)(2,1)S(1)}, u32[]{:S(2)}, u32[]{:S(2)}) collective-permute-start(s16[256,128]{1,0:T(8,128)(2,1)} %get-tuple-element.13), channel_id=1, source_target_pairs={{96,128},{97,129},{100,132},{101,133},{104,136},{105,137},{108,140... | collective-permute-start | bytes 196616 | tf_op jit(solution)/shard_map/ppermute | solution.py:338
  12.2 0.1 shard_map.78
  12.3 15.9 %collective-permute-start.3 = (bf16[128,128]{1,0:T(8,128)(2,1)S(1)}, bf16[128,128]{1,0:T(8,128)(2,1)S(1)}, u32[]{:S(2)}, u32[]{:S(2)}) collective-permute-start(bf16[128,128]{1,0:T(8,128)(2,1)S(1)} %shard_map.78), channel_id=1, source_target_pairs={{0,15},{1,2},{2,1},{3,4},{4,3},{5,6},{6,5},{7,8},{8,7},{9,10},{10,... | collective-permute-start | bytes 98312 | tf_op jit(solution)/shard_map/ppermute | solution.py:338
  28.3 0.0 collective-permute-done.lo_ref
  28.3 1.3 %collective-permute-start.9 = (s16[256,128]{1,0:T(8,128)(2,1)S(1)}, s16[256,128]{1,0:T(8,128)(2,1)S(1)}, u32[]{:S(2)}, u32[]{:S(2)}) collective-permute-start(s16[256,128]{1,0:T(8,128)(2,1)S(1)} %copy-done.7), channel_id=1, source_target_pairs={{0,32},{1,33},{2,34},{3,35},{4,36},{5,37},{6,38},{7,39},{8,40},{9,... | collective-permute-start | bytes 196616 | tf_op jit(solution)/shard_map/ppermute | solution.py:338
  29.6 0.1 shard_map.79.strip_ref
  29.7 0.2 collective-permute-done.3.wide_ref
  29.9 0.2 collective-permute-done.4.side_ref
  30.2 3.1 %collective-permute-start.6 = (bf16[192,128]{1,0:T(8,128)(2,1)S(1)}, bf16[192,128]{1,0:T(8,128)(2,1)S(1)}, u32[]{:S(2)}, u32[]{:S(2)}) collective-permute-start(bf16[192,128]{1,0:T(8,128)(2,1)S(1)} %get-tuple-element.14), channel_id=1, source_target_pairs={{0,511},{1,498},{2,497},{3,500},{4,499},{5,502},{6,501},{7,504},{8... | collective-permute-start | bytes 147464 | tf_op jit(solution)/shard_map/ppermute | solution.py:338
  33.3 0.0 copy-start.2
  33.3 0.0 copy-start.3
  33.3 0.0 copy-start.4
  33.3 0.0 copy-start.5
  33.3 0.8 %collective-permute-start.7 = (bf16[32,128]{1,0:T(8,128)(2,1)S(1)}, bf16[32,128]{1,0:T(8,128)(2,1)S(1)}, u32[]{:S(2)}, u32[]{:S(2)}) collective-permute-start(bf16[32,128]{1,0:T(8,128)(2,1)S(1)} %get-tuple-element.15), channel_id=1, source_target_pairs={{16,31},{17,18},{18,17},{19,20},{20,19},{21,22},{22,21},{23,24},{2... | collective-permute-start | bytes 24584 | tf_op jit(solution)/shard_map/ppermute | solution.py:338
  34.1 0.3 collective-permute-done.6.relay_ref
  34.4 0.1 shard_map.81
  34.6 3.8 %collective-permute-start.8 = (bf16[32,128]{1,0:T(8,128)(2,1)S(1)}, bf16[32,128]{1,0:T(8,128)(2,1)S(1)}, u32[]{:S(2)}, u32[]{:S(2)}) collective-permute-start(bf16[32,128]{1,0:T(8,128)(2,1)S(1)} %shard_map.81), channel_id=1, source_target_pairs={{0,1},{1,0},{2,3},{3,2},{4,5},{5,4},{6,7},{7,6},{8,9},{9,8},{10,11... | collective-permute-start | bytes 24584 | tf_op jit(solution)/shard_map/ppermute | solution.py:338
  38.4 0.8 %collective-permute-done.8.near_ref = bf16[32,128]{1,0:T(8,128)(2,1)S(1)} collective-permute-done((bf16[32,128]{1,0:T(8,128)(2,1)S(1)}, bf16[32,128]{1,0:T(8,128)(2,1)S(1)}, u32[]{:S(2)}, u32[]{:S(2)}) %collective-permute-start.8) | collective-permute-done | bytes 8224 | tf_op jit(solution)/shard_map/ppermute | solution.py:338
  39.2 2.1 %shard_map.82 = (f32[6,64,128]{2,1,0:T(8,128)}, f32[4,64,128]{2,1,0:T(8,128)}) custom-call(bf16[3,64,128]{2,1,0:T(8,128)(2,1)S(1)} %bitcast.12, s32[64,128]{1,0:T(8,128)S(1)} %bitcast.17, s32[64,128]{1,0:T(8,128)S(1)} %bitcast.22, bf16[608,128]{1,0:T(8,128)(2,1)S(1)} %collective-permute-done.lo_ref, bf16[608,128]{1,0:T(8,128)(2,1)S(1)} %collective-permute-done.1.wrap_ref, ...), custom_call_target="tpu_custom_call" | custom-call | bytes 400000 | tf_op jit(solution)/shard_map/pallas_call | solution.py:374
  (18 shorter events, 0.0 us)
Async XLA Ops:
  0.6 11.5 %copy-start = (bf16[3,8,8,128]{3,2,1,0:T(8,128)(2,1)S(1)}, bf16[3,8,8,128]{3,2,1,0:T(8,128)(2,1)}, u32[]{:S(2)}) copy-start(bf16[3,8,8,128]{3,2,1,0:T(8,128)(2,1)} %param.6) | copy-start | bytes 147460
  0.6 11.5 %copy-start.1 = (s32[8,8,128]{2,1,0:T(8,128)S(1)}, s32[8,8,128]{2,1,0:T(8,128)}, u32[]{:S(2)}) copy-start(s32[8,8,128]{2,1,0:T(8,128)} %param.10) | copy-start | bytes 98308
  2.4 25.8 %collective-permute-start = (bf16[608,128]{1,0:T(8,128)(2,1)}, bf16[608,128]{1,0:T(8,128)(2,1)S(1)}, u32[]{:S(2)}, u32[]{:S(2)}) collective-permute-start(bf16[608,128]{1,0:T(8,128)(2,1)} %get-tuple-element.10), channel_id=1, source_target_pairs={{0,16},{1,17},{2,18},{3,19},{4,20},{5,21},{6,22},{7,23},{8,24},{9,... | collective-permute-start | bytes 466952 | tf_op jit(solution)/shard_map/ppermute | solution.py:338
  6.8 5.3 %collective-permute-start.2 = (bf16[96,128]{1,0:T(8,128)(2,1)}, bf16[96,128]{1,0:T(8,128)(2,1)S(1)}, u32[]{:S(2)}, u32[]{:S(2)}) collective-permute-start(bf16[96,128]{1,0:T(8,128)(2,1)} %get-tuple-element.11.head_ref), channel_id=1, source_target_pairs={{16,0},{17,1},{18,2},{19,3},{20,4},{21,5},{22,6},{23,7},{24,8},{25... | collective-permute-start | bytes 73736 | tf_op jit(solution)/shard_map/ppermute | solution.py:338
  8.1 26.0 %collective-permute-start.1 = (bf16[608,128]{1,0:T(8,128)(2,1)}, bf16[608,128]{1,0:T(8,128)(2,1)S(1)}, u32[]{:S(2)}, u32[]{:S(2)}) collective-permute-start(bf16[608,128]{1,0:T(8,128)(2,1)} %get-tuple-element.10), channel_id=1, source_target_pairs={{112,128},{113,129},{114,130},{115,131},{116,132},{117,133},{118,1... | collective-permute-start | bytes 466952 | tf_op jit(solution)/shard_map/ppermute | solution.py:338
  9.4 20.8 %collective-permute-start.4 = (bf16[256,128]{1,0:T(8,128)(2,1)}, bf16[256,128]{1,0:T(8,128)(2,1)S(1)}, u32[]{:S(2)}, u32[]{:S(2)}) collective-permute-start(bf16[256,128]{1,0:T(8,128)(2,1)} %get-tuple-element.12), channel_id=1, source_target_pairs={{114,129},{115,132},{118,133},{119,136},{122,137},{123,140},{126,1... | collective-permute-start | bytes 196616 | tf_op jit(solution)/shard_map/ppermute | solution.py:338
  10.7 17.6 %copy-start.7 = (s16[256,128]{1,0:T(8,128)(2,1)S(1)}, s16[256,128]{1,0:T(8,128)(2,1)}, u32[]{:S(2)}) copy-start(s16[256,128]{1,0:T(8,128)(2,1)} %get-tuple-element.13) | copy-start | bytes 196612
  10.7 19.4 %collective-permute-start.5 = (s16[256,128]{1,0:T(8,128)(2,1)}, s16[256,128]{1,0:T(8,128)(2,1)S(1)}, u32[]{:S(2)}, u32[]{:S(2)}) collective-permute-start(s16[256,128]{1,0:T(8,128)(2,1)} %get-tuple-element.13), channel_id=1, source_target_pairs={{96,128},{97,129},{100,132},{101,133},{104,136},{105,137},{108,140... | collective-permute-start | bytes 196616 | tf_op jit(solution)/shard_map/ppermute | solution.py:338
  12.3 17.9 %copy-start.6 = (bf16[96,128]{1,0:T(8,128)(2,1)S(1)}, bf16[96,128]{1,0:T(8,128)(2,1)}, u32[]{:S(2)}) copy-start(bf16[96,128]{1,0:T(8,128)(2,1)} %get-tuple-element.11.head_ref) | copy-start | bytes 73732
  12.3 17.6 %collective-permute-start.3 = (bf16[128,128]{1,0:T(8,128)(2,1)S(1)}, bf16[128,128]{1,0:T(8,128)(2,1)S(1)}, u32[]{:S(2)}, u32[]{:S(2)}) collective-permute-start(bf16[128,128]{1,0:T(8,128)(2,1)S(1)} %shard_map.78), channel_id=1, source_target_pairs={{0,15},{1,2},{2,1},{3,4},{4,3},{5,6},{6,5},{7,8},{8,7},{9,10},{10,... | collective-permute-start | bytes 98312 | tf_op jit(solution)/shard_map/ppermute | solution.py:338
  28.3 10.1 %collective-permute-start.9 = (s16[256,128]{1,0:T(8,128)(2,1)S(1)}, s16[256,128]{1,0:T(8,128)(2,1)S(1)}, u32[]{:S(2)}, u32[]{:S(2)}) collective-permute-start(s16[256,128]{1,0:T(8,128)(2,1)S(1)} %copy-done.7), channel_id=1, source_target_pairs={{0,32},{1,33},{2,34},{3,35},{4,36},{5,37},{6,38},{7,39},{8,40},{9,... | collective-permute-start | bytes 196616 | tf_op jit(solution)/shard_map/ppermute | solution.py:338
  30.2 4.3 %collective-permute-start.6 = (bf16[192,128]{1,0:T(8,128)(2,1)S(1)}, bf16[192,128]{1,0:T(8,128)(2,1)S(1)}, u32[]{:S(2)}, u32[]{:S(2)}) collective-permute-start(bf16[192,128]{1,0:T(8,128)(2,1)S(1)} %get-tuple-element.14), channel_id=1, source_target_pairs={{0,511},{1,498},{2,497},{3,500},{4,499},{5,502},{6,501},{7,504},{8... | collective-permute-start | bytes 147464 | tf_op jit(solution)/shard_map/ppermute | solution.py:338
  33.3 5.9 %copy-start.2 = (f32[2,8,8,128]{3,2,1,0:T(8,128)S(1)}, f32[2,8,8,128]{3,2,1,0:T(8,128)}, u32[]{:S(2)}) copy-start(f32[2,8,8,128]{3,2,1,0:T(8,128)} %param.7) | copy-start | bytes 196612
  33.3 5.9 %copy-start.3 = (f32[2,8,8,128]{3,2,1,0:T(8,128)S(1)}, f32[2,8,8,128]{3,2,1,0:T(8,128)}, u32[]{:S(2)}) copy-start(f32[2,8,8,128]{3,2,1,0:T(8,128)} %param.8) | copy-start | bytes 196612
  33.3 5.9 %copy-start.4 = (s32[8,8,128]{2,1,0:T(8,128)S(1)}, s32[8,8,128]{2,1,0:T(8,128)}, u32[]{:S(2)}) copy-start(s32[8,8,128]{2,1,0:T(8,128)} %param.11) | copy-start | bytes 98308
  33.3 5.9 %copy-start.5 = (s32[8,8,16]{2,1,0:T(8,128)S(1)}, s32[8,8,16]{2,1,0:T(8,128)}, u32[]{:S(2)}) copy-start(s32[8,8,16]{2,1,0:T(8,128)} %param.9) | copy-start | bytes 12292
  33.3 5.1 %collective-permute-start.7 = (bf16[32,128]{1,0:T(8,128)(2,1)S(1)}, bf16[32,128]{1,0:T(8,128)(2,1)S(1)}, u32[]{:S(2)}, u32[]{:S(2)}) collective-permute-start(bf16[32,128]{1,0:T(8,128)(2,1)S(1)} %get-tuple-element.15), channel_id=1, source_target_pairs={{16,31},{17,18},{18,17},{19,20},{20,19},{21,22},{22,21},{23,24},{2... | collective-permute-start | bytes 24584 | tf_op jit(solution)/shard_map/ppermute | solution.py:338
  34.6 4.7 %collective-permute-start.8 = (bf16[32,128]{1,0:T(8,128)(2,1)S(1)}, bf16[32,128]{1,0:T(8,128)(2,1)S(1)}, u32[]{:S(2)}, u32[]{:S(2)}) collective-permute-start(bf16[32,128]{1,0:T(8,128)(2,1)S(1)} %shard_map.81), channel_id=1, source_target_pairs={{0,1},{1,0},{2,3},{3,2},{4,5},{5,4},{6,7},{7,6},{8,9},{9,8},{10,11... | collective-permute-start | bytes 24584 | tf_op jit(solution)/shard_map/ppermute | solution.py:338

commit v8 on v7

--- a/solution.py
+++ b/solution.py
@@ -10,13 +10,14 @@
 CLIP_CAP = 0.1
 RATIO_FLOOR = 0.02
 PAIRS = ((0, 0), (1, 1), (2, 2), (0, 1), (0, 2), (1, 2))
-KEPT_SCALE = 32767.0 / 1.4142137
+KEPT_SCALE = 32767.0 / 1.1892073
 F32 = jnp.float32
 BF16 = jnp.bfloat16
 VMEM_LIMIT = 32 * 1024 * 1024
 PACK_LIMIT = 60 * 1024 * 1024
 BIG = 1_000_000_000
 SIDE = 256
+HEAD = 80
 ROWS_A = 7
 ROWS_B = 4
 ROWS_C = 2
@@ -28,7 +29,7 @@
 
 
 def encode(x):
-    root = jnp.sqrt(jnp.sqrt(jnp.abs(x)))
+    root = jnp.sqrt(jnp.sqrt(jnp.sqrt(jnp.abs(x))))
     scaled = jnp.where(x < 0, -root, root) * KEPT_SCALE
     return jnp.round(scaled).astype(jnp.int32).astype(jnp.int16)
 
@@ -36,7 +37,8 @@
 def decode(code):
     y = code.astype(jnp.int32).astype(F32) * (1.0 / KEPT_SCALE)
     y2 = y * y
-    return jnp.where(y < 0, -y2, y2) * y2
+    y4 = y2 * y2
+    return jnp.where(y < 0, -y4, y4) * y4
 
 
 def place():
@@ -67,6 +69,11 @@
     return [[row(scratch, x, c) for x in range(8)] for c in range(3)]
 
 
+def head_rows(rows):
+    none = [jnp.zeros((8, 128), F32)]
+    return jnp.concatenate([rows[c][x] for c in range(3) for x in range(3)] + none, axis=0).astype(BF16)
+
+
 def pack_kernel(vel_hbm, solid_hbm, lq_hbm, mn_hbm, tail_ref, head_ref, side_ref, code_ref,
                 vel, solid, kept, scratch, sems):
     copies = [
@@ -80,7 +87,7 @@
     copies[0].wait()
     copies[1].wait()
     rows = own_rows(vel, solid, scratch)
-    head_ref[...] = jnp.concatenate([rows[c][x] for c in range(3) for x in range(4)], axis=0).astype(BF16)
+    head_ref[...] = head_rows(rows)
     tail = jnp.concatenate([rows[c][4 + x] for c in range(3) for x in range(4)], axis=0).astype(BF16)
     tail_ref[pl.ds(0, 96), :] = tail
     side_ref[pl.ds(0, 96), :] = tail
@@ -96,7 +103,7 @@
 
 def all_rows(own, lo, hi):
     lo = lo.reshape(3, 4, 8, 128)
-    hi = hi.reshape(3, 4, 8, 128)
+    hi = hi[:72].reshape(3, 3, 8, 128)
     out = []
     for c in range(3):
         rows = [lo[c, x] for x in (1, 2, 3)]
@@ -112,23 +119,23 @@
 
 def wide_kernel(vel_ref, solid_ref, hi_ref, wide_ref, scratch):
     own = own_rows(vel_ref, solid_ref, scratch)
-    hi = lead(hi_ref, 96)
-    left, right = edges(all_rows(own, jnp.zeros_like(hi), hi), 0)
+    hi = lead(hi_ref, HEAD)
+    left, right = edges(all_rows(own, jnp.zeros((96, 128), F32), hi), 0)
     _, even = place()
-    wide_ref[pl.ds(96, 32), :] = jnp.where(even, left, right).astype(BF16)
-    wide_ref[pl.ds(0, 96), :] = jnp.concatenate([own[c][x] for c in range(3) for x in range(4)], axis=0).astype(BF16)
+    wide_ref[pl.ds(HEAD, 32), :] = jnp.where(even, left, right).astype(BF16)
+    wide_ref[pl.ds(0, HEAD), :] = head_rows(own)
 
 
 def far_kernel(vel_ref, solid_ref, lo_ref, hi_ref, strip_ref, scratch):
-    rows = all_rows(own_rows(vel_ref, solid_ref, scratch), lead(lo_ref, 96), lead(hi_ref, 96))
+    rows = all_rows(own_rows(vel_ref, solid_ref, scratch), lead(lo_ref, 96), lead(hi_ref, HEAD))
     left, right = edges(rows, 0)
     _, even = place()
     strip_ref[...] = jnp.where(even, left, right).astype(BF16)
 
 
-def relay_kernel(wide_ref, strip_ref, head_ref, side_ref, two_ref, relay_ref, strip_out):
-    relay_ref[pl.ds(0, 96), :] = wide_ref[pl.ds(0, 96), :]
-    relay_ref[pl.ds(96, 96), :] = head_ref[...]
+def relay_kernel(wide_ref, strip_ref, side_ref, two_ref, relay_ref, strip_out):
+    relay_ref[pl.ds(0, HEAD), :] = wide_ref[pl.ds(0, HEAD), :]
+    relay_ref[pl.ds(HEAD, 32), :] = strip_ref[...]
     strip_out[...] = strip_ref[...]
 
 
@@ -136,7 +143,7 @@
     at, even = place()
     own = own_rows(vel_ref, solid_ref, scratch)
     lo = jnp.where(at == 0, lead(wrap_ref, 96), lead(lo_ref, 96))
-    hi = jnp.where(at == 7, lead(relay_ref, 96), lead(hi_ref, 96))
+    hi = jnp.where(at == 7, lead(relay_ref, HEAD), lead(hi_ref, HEAD))
     left, right = edges(all_rows(own, lo, hi), 0)
     strip_ref[...] = jnp.where(even, right, left).astype(BF16)
 
@@ -197,12 +204,13 @@
             two = jnp.take_along_axis(up2[f, 8 * z : 8 * z + 8], inner, axis=0)
             old[f, at, :] = jnp.where(idx < 8, two, jnp.where(idx < 16, one, got))
     lo = jnp.where(run == 0, lead(wrap_ref, 96), lead(lo_ref, 96))
-    hi = jnp.where(run == 7, lead(relay_ref, 96), lead(hi_ref, 96))
+    hi = jnp.where(run == 7, lead(relay_ref, HEAD), lead(hi_ref, HEAD))
     core = all_rows(own_rows(vel_ref, solid_ref, scratch), lo, hi)
     near = near_ref[...].astype(F32).reshape(4, 8, 128)
-    far = jnp.where(run == 0, wide_ref[pl.ds(96, 32), :].astype(F32), far_ref[...].astype(F32)).reshape(4, 8, 128)
+    far = jnp.where(run == 0, wide_ref[pl.ds(HEAD, 32), :].astype(F32), far_ref[...].astype(F32)).reshape(4, 8, 128)
     below = jnp.where(lower, lead(side_ref, 96), lead(lo_ref, 96)).reshape(3, 4, 8, 128)
-    above = relay_ref[pl.ds(96, 96), :].astype(F32).reshape(3, 4, 8, 128)
+    above = relay_ref[pl.ds(HEAD, 32), :].astype(F32).reshape(4, 8, 128)
+    far = [jnp.where((run == 7) & (lane >= 44), pltpu.roll(above[c], 32, 1), far[c]) for c in range(3)]
     edge = []
     for c in range(3):
         left = jnp.where(even, far[c], near[c])
@@ -214,8 +222,6 @@
             value = jnp.where(lane < 64, r, l)
             if i < 3:
                 value = jnp.where((run == 0) & ((lane >= 64) == even), below[c, i + 1], value)
-            if i > 10:
-                value = jnp.where((run == 7) & ((lane >= 64) == even), above[c, i - 11], value)
             rows.append(value)
         edge.append(jnp.stack(rows))
     core = [jnp.stack(rows) for rows in core]
@@ -351,7 +357,7 @@
     trans = pltpu.VMEM((3, 64, 128), F32)
     tail, head, side, code = call(
         pack_kernel,
-        [sds((608, 128), BF16), sds((96, 128), BF16), sds((SIDE, 128), BF16), code_type],
+        [sds((608, 128), BF16), sds((HEAD, 128), BF16), sds((SIDE, 128), BF16), code_type],
         [HBM] * 4,
         [pltpu.VMEM((3, 64, 128), BF16), pltpu.VMEM((64, 128), jnp.int32), pltpu.VMEM((256, 128), F32),
          trans, pltpu.SemaphoreType.DMA((4,))],
@@ -363,10 +369,10 @@
     wrap = send(tail, lambda run, gx, gy: (gx + 1, gy) if run == 7 else None)
     two_wrap = send(code, lambda run, gx, gy: (gx + 2, gy) if run == 6 and low(gy) else None)
     two = send(code, lambda run, gx, gy: (gx + 2, gy) if run != 6 or not low(gy) else None)
-    (wide,) = call(wide_kernel, [sds((128, 128), BF16)], [VM] * 3, [trans], flops=BIG)(vel, solid, hi)
+    (wide,) = call(wide_kernel, [sds((HEAD + 32, 128), BF16)], [VM] * 3, [trans], flops=BIG)(vel, solid, hi)
     (strip,) = call(far_kernel, [strip_type], [VM] * 4, [trans])(vel, solid, lo, hi)
     wide = send(wide, lambda run, gx, gy: (gx, far_side(gy)) if run == 0 else None)
-    relay, strip = call(relay_kernel, [sds((192, 128), BF16), strip_type], [VM] * 5, [])(wide, strip, head, side, two_wrap)
+    relay, strip = call(relay_kernel, [sds((HEAD + 32, 128), BF16), strip_type], [VM] * 4, [])(wide, strip, side, two_wrap)
     relay = send(relay, lambda run, gx, gy: (gx - 1, far_side(gy)) if run == 0 else None)
     far = send(strip, lambda run, gx, gy: (gx, far_side(gy)) if run > 0 else None)
     (near,) = call(near_kernel, [strip_type], [VM] * 6, [trans])(vel, solid, lo, wrap, hi, relay)

time: 41.9 us -> 41.7 us (level)
  no operation moved by 1% of the time
where the time goes in v8:
time: 41.7 us; the launch traced here: 41.3 us
  starting transfers between devices  34.6 us (83%)
  Pallas kernels  4.36 us (10%)
  waiting for transfers between devices  1.4 us (3%)
  between operations  0.87 us (2%)
    ppermute x10, starting transfers between devices, send(): return lax.ppermute(x, ('gx', 'gy'), pairs)  34.6 us
    pallas_call x1, Pallas kernels, local(): call(main_kernel, [sds((6, 64, 128), F32), sds((4, 64, 128), F32)], [VM]...  2.21 us
    pallas_call x1, Pallas kernels, local(): call(pack_kernel, [sds((608, 128), BF16), sds((HEAD, 128), BF16), sds((SI...  1.78 us
    ppermute x10, waiting for transfers between devices, send(): return lax.ppermute(x, ('gx', 'gy'), pairs)  1.4 us
  transfers between devices with their start and end apart: 10, of which 4 were waited for; matrix products, arithmetic and copies ran while one was open for 0% of the time, Pallas kernels for 1%

profile of v8, /device:TPU:1, one launch (start us, length us, event | category | flops | bytes accessed | tf_op | source)
XLA Modules:
  0.0 41.3 jit_solution(9426557087108528665)
XLA Ops:
  0.6 1.8 %shard_map.77 = (bf16[608,128]{1,0:T(8,128)(2,1)}, bf16[80,128]{1,0:T(8,128)(2,1)}, bf16[256,128]{1,0:T(8,128)(2,1)}, s16[256,128]{1,0:T(8,128)(2,1)}) custom-call(bf16[3,64,128]{2,1,0:T(8,128)(2,1)} %bitcast.8, s32[64,128]{1,0:T(8,128)} %bitcast.13, f32[128,128]{1,0:T(8,128)} %bitcast.18, f32[128,128]{1,0:T(8,128)} %bitcast.20), custom_call_target="tpu_custom_call" | custom-call | bytes 400000 | tf_op jit(solution)/shard_map/pallas_call | solution.py:358
  2.4 4.4 %collective-permute-start = (bf16[608,128]{1,0:T(8,128)(2,1)}, bf16[608,128]{1,0:T(8,128)(2,1)S(1)}, u32[]{:S(2)}, u32[]{:S(2)}) collective-permute-start(bf16[608,128]{1,0:T(8,128)(2,1)} %get-tuple-element.10), channel_id=1, source_target_pairs={{0,16},{1,17},{2,18},{3,19},{4,20},{5,21},{6,22},{7,23},{8,24},{9,... | collective-permute-start | bytes 466952 | tf_op jit(solution)/shard_map/ppermute | solution.py:344
  6.8 1.3 %collective-permute-start.2 = (bf16[80,128]{1,0:T(8,128)(2,1)}, bf16[80,128]{1,0:T(8,128)(2,1)S(1)}, u32[]{:S(2)}, u32[]{:S(2)}) collective-permute-start(bf16[80,128]{1,0:T(8,128)(2,1)} %get-tuple-element.11), channel_id=1, source_target_pairs={{16,0},{17,1},{18,2},{19,3},{20,4},{21,5},{22,6},{23,7},{24,8},{25... | collective-permute-start | bytes 61448 | tf_op jit(solution)/shard_map/ppermute | solution.py:344
  8.1 1.3 %collective-permute-start.1 = (bf16[608,128]{1,0:T(8,128)(2,1)}, bf16[608,128]{1,0:T(8,128)(2,1)S(1)}, u32[]{:S(2)}, u32[]{:S(2)}) collective-permute-start(bf16[608,128]{1,0:T(8,128)(2,1)} %get-tuple-element.10), channel_id=1, source_target_pairs={{112,128},{113,129},{114,130},{115,131},{116,132},{117,133},{118,1... | collective-permute-start | bytes 466952 | tf_op jit(solution)/shard_map/ppermute | solution.py:344
  9.4 1.3 %collective-permute-start.4 = (bf16[256,128]{1,0:T(8,128)(2,1)}, bf16[256,128]{1,0:T(8,128)(2,1)S(1)}, u32[]{:S(2)}, u32[]{:S(2)}) collective-permute-start(bf16[256,128]{1,0:T(8,128)(2,1)} %get-tuple-element.12), channel_id=1, source_target_pairs={{114,129},{115,132},{118,133},{119,136},{122,137},{123,140},{126,1... | collective-permute-start | bytes 196616 | tf_op jit(solution)/shard_map/ppermute | solution.py:344
  10.7 1.4 %collective-permute-start.5 = (s16[256,128]{1,0:T(8,128)(2,1)}, s16[256,128]{1,0:T(8,128)(2,1)S(1)}, u32[]{:S(2)}, u32[]{:S(2)}) collective-permute-start(s16[256,128]{1,0:T(8,128)(2,1)} %get-tuple-element.13), channel_id=1, source_target_pairs={{96,128},{97,129},{100,132},{101,133},{104,136},{105,137},{108,140... | collective-permute-start | bytes 196616 | tf_op jit(solution)/shard_map/ppermute | solution.py:344
  12.2 0.1 shard_map.78
  12.3 15.9 %collective-permute-start.3 = (bf16[112,128]{1,0:T(8,128)(2,1)S(1)}, bf16[112,128]{1,0:T(8,128)(2,1)S(1)}, u32[]{:S(2)}, u32[]{:S(2)}) collective-permute-start(bf16[112,128]{1,0:T(8,128)(2,1)S(1)} %shard_map.78), channel_id=1, source_target_pairs={{0,15},{1,2},{2,1},{3,4},{4,3},{5,6},{6,5},{7,8},{8,7},{9,10},{10,... | collective-permute-start | bytes 86024 | tf_op jit(solution)/shard_map/ppermute | solution.py:344
  28.2 1.3 %collective-permute-start.9 = (s16[256,128]{1,0:T(8,128)(2,1)S(1)}, s16[256,128]{1,0:T(8,128)(2,1)S(1)}, u32[]{:S(2)}, u32[]{:S(2)}) collective-permute-start(s16[256,128]{1,0:T(8,128)(2,1)S(1)} %copy-done.6), channel_id=1, source_target_pairs={{0,32},{1,33},{2,34},{3,35},{4,36},{5,37},{6,38},{7,39},{8,40},{9,... | collective-permute-start | bytes 196616 | tf_op jit(solution)/shard_map/ppermute | solution.py:344
  29.5 0.1 shard_map.79.strip_ref
  29.7 0.1 collective-permute-done.3.wide_ref
  29.8 0.4 collective-permute-done.4.side_ref
  30.2 0.0 collective-permute-done.5.two_ref.two_wrap_ref
  30.2 3.0 %collective-permute-start.6 = (bf16[112,128]{1,0:T(8,128)(2,1)S(1)}, bf16[112,128]{1,0:T(8,128)(2,1)S(1)}, u32[]{:S(2)}, u32[]{:S(2)}) collective-permute-start(bf16[112,128]{1,0:T(8,128)(2,1)S(1)} %get-tuple-element.14), channel_id=1, source_target_pairs={{0,511},{1,498},{2,497},{3,500},{4,499},{5,502},{6,501},{7,504},{8... | collective-permute-start | bytes 86024 | tf_op jit(solution)/shard_map/ppermute | solution.py:344
  33.2 0.0 copy-start.2
  33.3 0.0 copy-start.3
  33.3 0.0 copy-start.4
  33.3 0.0 copy-start.5
  33.3 0.8 %collective-permute-start.7 = (bf16[32,128]{1,0:T(8,128)(2,1)S(1)}, bf16[32,128]{1,0:T(8,128)(2,1)S(1)}, u32[]{:S(2)}, u32[]{:S(2)}) collective-permute-start(bf16[32,128]{1,0:T(8,128)(2,1)S(1)} %get-tuple-element.15), channel_id=1, source_target_pairs={{16,31},{17,18},{18,17},{19,20},{20,19},{21,22},{22,21},{23,24},{2... | collective-permute-start | bytes 24584 | tf_op jit(solution)/shard_map/ppermute | solution.py:344
  34.1 0.1 collective-permute-done.6.relay_ref
  34.2 0.1 shard_map.81
  34.3 3.9 %collective-permute-start.8 = (bf16[32,128]{1,0:T(8,128)(2,1)S(1)}, bf16[32,128]{1,0:T(8,128)(2,1)S(1)}, u32[]{:S(2)}, u32[]{:S(2)}) collective-permute-start(bf16[32,128]{1,0:T(8,128)(2,1)S(1)} %shard_map.81), channel_id=1, source_target_pairs={{0,1},{1,0},{2,3},{3,2},{4,5},{5,4},{6,7},{7,6},{8,9},{9,8},{10,11... | collective-permute-start | bytes 24584 | tf_op jit(solution)/shard_map/ppermute | solution.py:344
  38.2 0.8 %collective-permute-done.8.near_ref = bf16[32,128]{1,0:T(8,128)(2,1)S(1)} collective-permute-done((bf16[32,128]{1,0:T(8,128)(2,1)S(1)}, bf16[32,128]{1,0:T(8,128)(2,1)S(1)}, u32[]{:S(2)}, u32[]{:S(2)}) %collective-permute-start.8) | collective-permute-done | bytes 8224 | tf_op jit(solution)/shard_map/ppermute | solution.py:344
  39.0 2.2 %shard_map.82 = (f32[6,64,128]{2,1,0:T(8,128)}, f32[4,64,128]{2,1,0:T(8,128)}) custom-call(bf16[3,64,128]{2,1,0:T(8,128)(2,1)S(1)} %bitcast.12, s32[64,128]{1,0:T(8,128)S(1)} %bitcast.17, s32[64,128]{1,0:T(8,128)S(1)} %bitcast.22, bf16[608,128]{1,0:T(8,128)(2,1)S(1)} %collective-permute-done.lo_ref, bf16[608,128]{1,0:T(8,128)(2,1)S(1)} %collective-permute-done.1.wrap_ref, ...), custom_call_target="tpu_custom_call" | custom-call | bytes 400000 | tf_op jit(solution)/shard_map/pallas_call | solution.py:380
  (16 shorter events, 0.0 us)
Async XLA Ops:
  0.6 11.5 %copy-start = (bf16[3,8,8,128]{3,2,1,0:T(8,128)(2,1)S(1)}, bf16[3,8,8,128]{3,2,1,0:T(8,128)(2,1)}, u32[]{:S(2)}) copy-start(bf16[3,8,8,128]{3,2,1,0:T(8,128)(2,1)} %param.6) | copy-start | bytes 147460
  0.6 11.5 %copy-start.1 = (s32[8,8,128]{2,1,0:T(8,128)S(1)}, s32[8,8,128]{2,1,0:T(8,128)}, u32[]{:S(2)}) copy-start(s32[8,8,128]{2,1,0:T(8,128)} %param.10) | copy-start | bytes 98308
  2.4 25.8 %collective-permute-start = (bf16[608,128]{1,0:T(8,128)(2,1)}, bf16[608,128]{1,0:T(8,128)(2,1)S(1)}, u32[]{:S(2)}, u32[]{:S(2)}) collective-permute-start(bf16[608,128]{1,0:T(8,128)(2,1)} %get-tuple-element.10), channel_id=1, source_target_pairs={{0,16},{1,17},{2,18},{3,19},{4,20},{5,21},{6,22},{7,23},{8,24},{9,... | collective-permute-start | bytes 466952 | tf_op jit(solution)/shard_map/ppermute | solution.py:344
  6.8 5.3 %collective-permute-start.2 = (bf16[80,128]{1,0:T(8,128)(2,1)}, bf16[80,128]{1,0:T(8,128)(2,1)S(1)}, u32[]{:S(2)}, u32[]{:S(2)}) collective-permute-start(bf16[80,128]{1,0:T(8,128)(2,1)} %get-tuple-element.11), channel_id=1, source_target_pairs={{16,0},{17,1},{18,2},{19,3},{20,4},{21,5},{22,6},{23,7},{24,8},{25... | collective-permute-start | bytes 61448 | tf_op jit(solution)/shard_map/ppermute | solution.py:344
  8.1 26.0 %collective-permute-start.1 = (bf16[608,128]{1,0:T(8,128)(2,1)}, bf16[608,128]{1,0:T(8,128)(2,1)S(1)}, u32[]{:S(2)}, u32[]{:S(2)}) collective-permute-start(bf16[608,128]{1,0:T(8,128)(2,1)} %get-tuple-element.10), channel_id=1, source_target_pairs={{112,128},{113,129},{114,130},{115,131},{116,132},{117,133},{118,1... | collective-permute-start | bytes 466952 | tf_op jit(solution)/shard_map/ppermute | solution.py:344
  9.4 20.7 %collective-permute-start.4 = (bf16[256,128]{1,0:T(8,128)(2,1)}, bf16[256,128]{1,0:T(8,128)(2,1)S(1)}, u32[]{:S(2)}, u32[]{:S(2)}) collective-permute-start(bf16[256,128]{1,0:T(8,128)(2,1)} %get-tuple-element.12), channel_id=1, source_target_pairs={{114,129},{115,132},{118,133},{119,136},{122,137},{123,140},{126,1... | collective-permute-start | bytes 196616 | tf_op jit(solution)/shard_map/ppermute | solution.py:344
  10.7 17.5 %copy-start.6 = (s16[256,128]{1,0:T(8,128)(2,1)S(1)}, s16[256,128]{1,0:T(8,128)(2,1)}, u32[]{:S(2)}) copy-start(s16[256,128]{1,0:T(8,128)(2,1)} %get-tuple-element.13) | copy-start | bytes 196612
  10.7 19.4 %collective-permute-start.5 = (s16[256,128]{1,0:T(8,128)(2,1)}, s16[256,128]{1,0:T(8,128)(2,1)S(1)}, u32[]{:S(2)}, u32[]{:S(2)}) collective-permute-start(s16[256,128]{1,0:T(8,128)(2,1)} %get-tuple-element.13), channel_id=1, source_target_pairs={{96,128},{97,129},{100,132},{101,133},{104,136},{105,137},{108,140... | collective-permute-start | bytes 196616 | tf_op jit(solution)/shard_map/ppermute | solution.py:344
  12.3 17.5 %collective-permute-start.3 = (bf16[112,128]{1,0:T(8,128)(2,1)S(1)}, bf16[112,128]{1,0:T(8,128)(2,1)S(1)}, u32[]{:S(2)}, u32[]{:S(2)}) collective-permute-start(bf16[112,128]{1,0:T(8,128)(2,1)S(1)} %shard_map.78), channel_id=1, source_target_pairs={{0,15},{1,2},{2,1},{3,4},{4,3},{5,6},{6,5},{7,8},{8,7},{9,10},{10,... | collective-permute-start | bytes 86024 | tf_op jit(solution)/shard_map/ppermute | solution.py:344
  28.2 10.0 %collective-permute-start.9 = (s16[256,128]{1,0:T(8,128)(2,1)S(1)}, s16[256,128]{1,0:T(8,128)(2,1)S(1)}, u32[]{:S(2)}, u32[]{:S(2)}) collective-permute-start(s16[256,128]{1,0:T(8,128)(2,1)S(1)} %copy-done.6), channel_id=1, source_target_pairs={{0,32},{1,33},{2,34},{3,35},{4,36},{5,37},{6,38},{7,39},{8,40},{9,... | collective-permute-start | bytes 196616 | tf_op jit(solution)/shard_map/ppermute | solution.py:344
  30.2 4.0 %collective-permute-start.6 = (bf16[112,128]{1,0:T(8,128)(2,1)S(1)}, bf16[112,128]{1,0:T(8,128)(2,1)S(1)}, u32[]{:S(2)}, u32[]{:S(2)}) collective-permute-start(bf16[112,128]{1,0:T(8,128)(2,1)S(1)} %get-tuple-element.14), channel_id=1, source_target_pairs={{0,511},{1,498},{2,497},{3,500},{4,499},{5,502},{6,501},{7,504},{8... | collective-permute-start | bytes 86024 | tf_op jit(solution)/shard_map/ppermute | solution.py:344
  33.2 5.8 %copy-start.2 = (f32[2,8,8,128]{3,2,1,0:T(8,128)S(1)}, f32[2,8,8,128]{3,2,1,0:T(8,128)}, u32[]{:S(2)}) copy-start(f32[2,8,8,128]{3,2,1,0:T(8,128)} %param.7) | copy-start | bytes 196612
  33.3 5.8 %copy-start.3 = (f32[2,8,8,128]{3,2,1,0:T(8,128)S(1)}, f32[2,8,8,128]{3,2,1,0:T(8,128)}, u32[]{:S(2)}) copy-start(f32[2,8,8,128]{3,2,1,0:T(8,128)} %param.8) | copy-start | bytes 196612
  33.3 5.8 %copy-start.4 = (s32[8,8,128]{2,1,0:T(8,128)S(1)}, s32[8,8,128]{2,1,0:T(8,128)}, u32[]{:S(2)}) copy-start(s32[8,8,128]{2,1,0:T(8,128)} %param.11) | copy-start | bytes 98308
  33.3 5.8 %copy-start.5 = (s32[8,8,16]{2,1,0:T(8,128)S(1)}, s32[8,8,16]{2,1,0:T(8,128)}, u32[]{:S(2)}) copy-start(s32[8,8,16]{2,1,0:T(8,128)} %param.9) | copy-start | bytes 12292
  33.3 5.0 %collective-permute-start.7 = (bf16[32,128]{1,0:T(8,128)(2,1)S(1)}, bf16[32,128]{1,0:T(8,128)(2,1)S(1)}, u32[]{:S(2)}, u32[]{:S(2)}) collective-permute-start(bf16[32,128]{1,0:T(8,128)(2,1)S(1)} %get-tuple-element.15), channel_id=1, source_target_pairs={{16,31},{17,18},{18,17},{19,20},{20,19},{21,22},{22,21},{23,24},{2... | collective-permute-start | bytes 24584 | tf_op jit(solution)/shard_map/ppermute | solution.py:344
  34.3 4.7 %collective-permute-start.8 = (bf16[32,128]{1,0:T(8,128)(2,1)S(1)}, bf16[32,128]{1,0:T(8,128)(2,1)S(1)}, u32[]{:S(2)}, u32[]{:S(2)}) collective-permute-start(bf16[32,128]{1,0:T(8,128)(2,1)S(1)} %shard_map.81), channel_id=1, source_target_pairs={{0,1},{1,0},{2,3},{3,2},{4,5},{5,4},{6,7},{7,6},{8,9},{9,8},{10,11... | collective-permute-start | bytes 24584 | tf_op jit(solution)/shard_map/ppermute | solution.py:344

commit v9 on v8

--- a/solution.py
+++ b/solution.py
@@ -174,11 +174,11 @@
 
 def relax_weight(product):
     inverse = lax.rsqrt(lax.rsqrt(lax.rsqrt(jnp.maximum(product, PRODUCT_FLOOR))))
-    return 1.0 / (1.0 + (1.0 / RATE_SCALE) * inverse)
+    return pl.reciprocal(1.0 + (1.0 / RATE_SCALE) * inverse)
 
 
 def main_kernel(vel_ref, solid_ref, clip_ref, lo_ref, wrap_ref, hi_ref, relay_ref, far_ref, wide_ref, side_ref,
-                near_ref, src_ref, lq_ref, mn_ref, two_ref, two_wrap_ref, stress_ref, new_ref, scratch, old):
+                near_ref, src_ref, lq_ref, mn_ref, two_ref, two_wrap_ref, stress_ref, new_ref, scratch, old, tiles):
     lane = lax.broadcasted_iota(jnp.int32, (8, 128), 1)
     sub = lax.broadcasted_iota(jnp.int32, (8, 128), 0)
     run, even = place()
@@ -187,10 +187,14 @@
     spread = (lax.broadcasted_iota(jnp.int32, (16, 128), 1) // 8 == lax.broadcasted_iota(jnp.int32, (16, 128), 0))
     local = jnp.dot((16 + here - back).astype(F32), spread.astype(F32), preferred_element_type=F32)
     local = (local + 0.5).astype(jnp.int32)
-    tile = lo_ref[pl.ds(96, 256), :].astype(F32) + lo_ref[pl.ds(352, 256), :].astype(F32)
-    wrap = wrap_ref[pl.ds(96, 256), :].astype(F32) + wrap_ref[pl.ds(352, 256), :].astype(F32)
-    up1 = jnp.where(run == 0, wrap, tile).reshape(4, 64, 128)
     lower = (lax.axis_index("gy") & 3) < 2
+
+    def add_up(ref):
+        tiles[...] = ref[pl.ds(96, 256), :].astype(F32) + ref[pl.ds(352, 256), :].astype(F32)
+
+    pl.when(run == 0)(lambda: add_up(wrap_ref))
+    pl.when(run != 0)(lambda: add_up(lo_ref))
+    up1 = tiles[...].reshape(4, 64, 128)
     up2 = decode(jnp.where((run == 0) & lower, two_wrap_ref[...].astype(jnp.int32), two_ref[...].astype(jnp.int32))).reshape(4, 64, 128)
     for z in range(8):
         at = pl.ds(8 * z, 8)
@@ -298,9 +302,9 @@
         new_mm = wn * mm + (1.0 - wn) * o_mm
         new_qn = ww * qn + (1.0 - ww) * o_qn
         new_nn = ww * nn + (1.0 - ww) * o_nn
-        c2 = jnp.maximum(new_lm, 0.0) / new_mm
-        c4 = jnp.maximum(new_qn, 0.0) / new_nn
-        cs = c2 * c2 / jnp.maximum(jnp.maximum(c4, 0.125 * c2), RATIO_FLOOR)
+        c2 = jnp.maximum(new_lm, 0.0) * pl.reciprocal(new_mm)
+        c4 = jnp.maximum(new_qn, 0.0) * pl.reciprocal(new_nn)
+        cs = c2 * c2 * pl.reciprocal(jnp.maximum(jnp.maximum(c4, 0.125 * c2), RATIO_FLOOR))
         clipped = jnp.stack([row(clip_ref, x) for x in span]) == 1
         blocked = jnp.stack([row(solid_ref, x) for x in span]) == 1
         cs = jnp.where(clipped, jnp.minimum(cs, CLIP_CAP), cs)
@@ -378,7 +382,7 @@
     (near,) = call(near_kernel, [strip_type], [VM] * 6, [trans])(vel, solid, lo, wrap, hi, relay)
     near = send(near, lambda run, gx, gy: (gx, gy ^ 1))
     stress, new = call(
-        main_kernel, [sds((6, 64, 128), F32), sds((4, 64, 128), F32)], [VM] * 16, [trans, pltpu.VMEM((4, 64, 128), F32)],
+        main_kernel, [sds((6, 64, 128), F32), sds((4, 64, 128), F32)], [VM] * 16, [trans, pltpu.VMEM((4, 64, 128), F32), pltpu.VMEM((256, 128), F32)],
     )(vel, solid, clip, lo, wrap, hi, relay, far, wide, side, near, src, lq, mn, two, two_wrap)
     return stress.reshape(6, 8, 8, 128), new.reshape(4, 8, 8, 128)
 

time: 41.7 us -> 41.8 us (level)
  no operation moved by 1% of the time
where the time goes in v9:
time: 41.8 us; the launch traced here: 41.4 us
  starting transfers between devices  34.6 us (83%)
  Pallas kernels  4.49 us (11%)
  waiting for transfers between devices  1.4 us (3%)
  between operations  0.87 us (2%)
    ppermute x10, starting transfers between devices, send(): return lax.ppermute(x, ('gx', 'gy'), pairs)  34.6 us
    pallas_call x1, Pallas kernels, local(): call(main_kernel, [sds((6, 64, 128), F32), sds((4, 64, 128), F32)], [VM]...  2.34 us
    pallas_call x1, Pallas kernels, local(): call(pack_kernel, [sds((608, 128), BF16), sds((HEAD, 128), BF16), sds((SI...  1.78 us
    ppermute x10, waiting for transfers between devices, send(): return lax.ppermute(x, ('gx', 'gy'), pairs)  1.4 us
  transfers between devices with their start and end apart: 10, of which 4 were waited for; matrix products, arithmetic and copies ran while one was open for 0% of the time, Pallas kernels for 1%

profile of v9, /device:TPU:1, one launch (start us, length us, event | category | flops | bytes accessed | tf_op | source)
XLA Modules:
  0.0 41.4 jit_solution(4583060593223718973)
XLA Ops:
  0.6 1.8 %shard_map.77 = (bf16[608,128]{1,0:T(8,128)(2,1)}, bf16[80,128]{1,0:T(8,128)(2,1)}, bf16[256,128]{1,0:T(8,128)(2,1)}, s16[256,128]{1,0:T(8,128)(2,1)}) custom-call(bf16[3,64,128]{2,1,0:T(8,128)(2,1)} %bitcast.8, s32[64,128]{1,0:T(8,128)} %bitcast.13, f32[128,128]{1,0:T(8,128)} %bitcast.18, f32[128,128]{1,0:T(8,128)} %bitcast.20), custom_call_target="tpu_custom_call" | custom-call | bytes 400000 | tf_op jit(solution)/shard_map/pallas_call | solution.py:362
  2.4 4.4 %collective-permute-start = (bf16[608,128]{1,0:T(8,128)(2,1)}, bf16[608,128]{1,0:T(8,128)(2,1)S(1)}, u32[]{:S(2)}, u32[]{:S(2)}) collective-permute-start(bf16[608,128]{1,0:T(8,128)(2,1)} %get-tuple-element.10), channel_id=1, source_target_pairs={{0,16},{1,17},{2,18},{3,19},{4,20},{5,21},{6,22},{7,23},{8,24},{9,... | collective-permute-start | bytes 466952 | tf_op jit(solution)/shard_map/ppermute | solution.py:348
  6.8 1.3 %collective-permute-start.2 = (bf16[80,128]{1,0:T(8,128)(2,1)}, bf16[80,128]{1,0:T(8,128)(2,1)S(1)}, u32[]{:S(2)}, u32[]{:S(2)}) collective-permute-start(bf16[80,128]{1,0:T(8,128)(2,1)} %get-tuple-element.11), channel_id=1, source_target_pairs={{16,0},{17,1},{18,2},{19,3},{20,4},{21,5},{22,6},{23,7},{24,8},{25... | collective-permute-start | bytes 61448 | tf_op jit(solution)/shard_map/ppermute | solution.py:348
  8.1 1.3 %collective-permute-start.1 = (bf16[608,128]{1,0:T(8,128)(2,1)}, bf16[608,128]{1,0:T(8,128)(2,1)S(1)}, u32[]{:S(2)}, u32[]{:S(2)}) collective-permute-start(bf16[608,128]{1,0:T(8,128)(2,1)} %get-tuple-element.10), channel_id=1, source_target_pairs={{112,128},{113,129},{114,130},{115,131},{116,132},{117,133},{118,1... | collective-permute-start | bytes 466952 | tf_op jit(solution)/shard_map/ppermute | solution.py:348
  9.4 1.3 %collective-permute-start.4 = (bf16[256,128]{1,0:T(8,128)(2,1)}, bf16[256,128]{1,0:T(8,128)(2,1)S(1)}, u32[]{:S(2)}, u32[]{:S(2)}) collective-permute-start(bf16[256,128]{1,0:T(8,128)(2,1)} %get-tuple-element.12), channel_id=1, source_target_pairs={{114,129},{115,132},{118,133},{119,136},{122,137},{123,140},{126,1... | collective-permute-start | bytes 196616 | tf_op jit(solution)/shard_map/ppermute | solution.py:348
  10.7 1.4 %collective-permute-start.5 = (s16[256,128]{1,0:T(8,128)(2,1)}, s16[256,128]{1,0:T(8,128)(2,1)S(1)}, u32[]{:S(2)}, u32[]{:S(2)}) collective-permute-start(s16[256,128]{1,0:T(8,128)(2,1)} %get-tuple-element.13), channel_id=1, source_target_pairs={{96,128},{97,129},{100,132},{101,133},{104,136},{105,137},{108,140... | collective-permute-start | bytes 196616 | tf_op jit(solution)/shard_map/ppermute | solution.py:348
  12.2 0.0 collective-permute-done.2.hi_ref
  12.2 0.1 shard_map.78
  12.3 15.9 %collective-permute-start.3 = (bf16[112,128]{1,0:T(8,128)(2,1)S(1)}, bf16[112,128]{1,0:T(8,128)(2,1)S(1)}, u32[]{:S(2)}, u32[]{:S(2)}) collective-permute-start(bf16[112,128]{1,0:T(8,128)(2,1)S(1)} %shard_map.78), channel_id=1, source_target_pairs={{0,15},{1,2},{2,1},{3,4},{4,3},{5,6},{6,5},{7,8},{8,7},{9,10},{10,... | collective-permute-start | bytes 86024 | tf_op jit(solution)/shard_map/ppermute | solution.py:348
  28.2 1.3 %collective-permute-start.9 = (s16[256,128]{1,0:T(8,128)(2,1)S(1)}, s16[256,128]{1,0:T(8,128)(2,1)S(1)}, u32[]{:S(2)}, u32[]{:S(2)}) collective-permute-start(s16[256,128]{1,0:T(8,128)(2,1)S(1)} %copy-done.6), channel_id=1, source_target_pairs={{0,32},{1,33},{2,34},{3,35},{4,36},{5,37},{6,38},{7,39},{8,40},{9,... | collective-permute-start | bytes 196616 | tf_op jit(solution)/shard_map/ppermute | solution.py:348
  29.5 0.1 shard_map.79.strip_ref
  29.7 0.1 collective-permute-done.3.wide_ref
  29.8 0.4 collective-permute-done.4.side_ref
  30.2 3.0 %collective-permute-start.6 = (bf16[112,128]{1,0:T(8,128)(2,1)S(1)}, bf16[112,128]{1,0:T(8,128)(2,1)S(1)}, u32[]{:S(2)}, u32[]{:S(2)}) collective-permute-start(bf16[112,128]{1,0:T(8,128)(2,1)S(1)} %get-tuple-element.14), channel_id=1, source_target_pairs={{0,511},{1,498},{2,497},{3,500},{4,499},{5,502},{6,501},{7,504},{8... | collective-permute-start | bytes 86024 | tf_op jit(solution)/shard_map/ppermute | solution.py:348
  33.2 0.0 copy-start.2
  33.3 0.0 copy-start.3
  33.3 0.0 copy-start.4
  33.3 0.0 copy-start.5
  33.3 0.8 %collective-permute-start.7 = (bf16[32,128]{1,0:T(8,128)(2,1)S(1)}, bf16[32,128]{1,0:T(8,128)(2,1)S(1)}, u32[]{:S(2)}, u32[]{:S(2)}) collective-permute-start(bf16[32,128]{1,0:T(8,128)(2,1)S(1)} %get-tuple-element.15), channel_id=1, source_target_pairs={{16,31},{17,18},{18,17},{19,20},{20,19},{21,22},{22,21},{23,24},{2... | collective-permute-start | bytes 24584 | tf_op jit(solution)/shard_map/ppermute | solution.py:348
  34.1 0.1 collective-permute-done.6.relay_ref
  34.2 0.1 shard_map.81
  34.3 3.9 %collective-permute-start.8 = (bf16[32,128]{1,0:T(8,128)(2,1)S(1)}, bf16[32,128]{1,0:T(8,128)(2,1)S(1)}, u32[]{:S(2)}, u32[]{:S(2)}) collective-permute-start(bf16[32,128]{1,0:T(8,128)(2,1)S(1)} %shard_map.81), channel_id=1, source_target_pairs={{0,1},{1,0},{2,3},{3,2},{4,5},{5,4},{6,7},{7,6},{8,9},{9,8},{10,11... | collective-permute-start | bytes 24584 | tf_op jit(solution)/shard_map/ppermute | solution.py:348
  38.2 0.8 %collective-permute-done.8.near_ref = bf16[32,128]{1,0:T(8,128)(2,1)S(1)} collective-permute-done((bf16[32,128]{1,0:T(8,128)(2,1)S(1)}, bf16[32,128]{1,0:T(8,128)(2,1)S(1)}, u32[]{:S(2)}, u32[]{:S(2)}) %collective-permute-start.8) | collective-permute-done | bytes 8224 | tf_op jit(solution)/shard_map/ppermute | solution.py:348
  39.0 2.3 %shard_map.82 = (f32[6,64,128]{2,1,0:T(8,128)}, f32[4,64,128]{2,1,0:T(8,128)}) custom-call(bf16[3,64,128]{2,1,0:T(8,128)(2,1)S(1)} %bitcast.12, s32[64,128]{1,0:T(8,128)S(1)} %bitcast.17, s32[64,128]{1,0:T(8,128)S(1)} %bitcast.22, bf16[608,128]{1,0:T(8,128)(2,1)S(1)} %collective-permute-done.lo_ref, bf16[608,128]{1,0:T(8,128)(2,1)S(1)} %collective-permute-done.1.wrap_ref, ...), custom_call_target="tpu_custom_call" | custom-call | bytes 400000 | tf_op jit(solution)/shard_map/pallas_call | solution.py:384
  (16 shorter events, 0.0 us)
Async XLA Ops:
  0.6 11.5 %copy-start = (bf16[3,8,8,128]{3,2,1,0:T(8,128)(2,1)S(1)}, bf16[3,8,8,128]{3,2,1,0:T(8,128)(2,1)}, u32[]{:S(2)}) copy-start(bf16[3,8,8,128]{3,2,1,0:T(8,128)(2,1)} %param.6) | copy-start | bytes 147460
  0.6 11.5 %copy-start.1 = (s32[8,8,128]{2,1,0:T(8,128)S(1)}, s32[8,8,128]{2,1,0:T(8,128)}, u32[]{:S(2)}) copy-start(s32[8,8,128]{2,1,0:T(8,128)} %param.10) | copy-start | bytes 98308
  2.4 25.8 %collective-permute-start = (bf16[608,128]{1,0:T(8,128)(2,1)}, bf16[608,128]{1,0:T(8,128)(2,1)S(1)}, u32[]{:S(2)}, u32[]{:S(2)}) collective-permute-start(bf16[608,128]{1,0:T(8,128)(2,1)} %get-tuple-element.10), channel_id=1, source_target_pairs={{0,16},{1,17},{2,18},{3,19},{4,20},{5,21},{6,22},{7,23},{8,24},{9,... | collective-permute-start | bytes 466952 | tf_op jit(solution)/shard_map/ppermute | solution.py:348
  6.8 5.3 %collective-permute-start.2 = (bf16[80,128]{1,0:T(8,128)(2,1)}, bf16[80,128]{1,0:T(8,128)(2,1)S(1)}, u32[]{:S(2)}, u32[]{:S(2)}) collective-permute-start(bf16[80,128]{1,0:T(8,128)(2,1)} %get-tuple-element.11), channel_id=1, source_target_pairs={{16,0},{17,1},{18,2},{19,3},{20,4},{21,5},{22,6},{23,7},{24,8},{25... | collective-permute-start | bytes 61448 | tf_op jit(solution)/shard_map/ppermute | solution.py:348
  8.1 26.0 %collective-permute-start.1 = (bf16[608,128]{1,0:T(8,128)(2,1)}, bf16[608,128]{1,0:T(8,128)(2,1)S(1)}, u32[]{:S(2)}, u32[]{:S(2)}) collective-permute-start(bf16[608,128]{1,0:T(8,128)(2,1)} %get-tuple-element.10), channel_id=1, source_target_pairs={{112,128},{113,129},{114,130},{115,131},{116,132},{117,133},{118,1... | collective-permute-start | bytes 466952 | tf_op jit(solution)/shard_map/ppermute | solution.py:348
  9.4 20.7 %collective-permute-start.4 = (bf16[256,128]{1,0:T(8,128)(2,1)}, bf16[256,128]{1,0:T(8,128)(2,1)S(1)}, u32[]{:S(2)}, u32[]{:S(2)}) collective-permute-start(bf16[256,128]{1,0:T(8,128)(2,1)} %get-tuple-element.12), channel_id=1, source_target_pairs={{114,129},{115,132},{118,133},{119,136},{122,137},{123,140},{126,1... | collective-permute-start | bytes 196616 | tf_op jit(solution)/shard_map/ppermute | solution.py:348
  10.7 17.5 %copy-start.6 = (s16[256,128]{1,0:T(8,128)(2,1)S(1)}, s16[256,128]{1,0:T(8,128)(2,1)}, u32[]{:S(2)}) copy-start(s16[256,128]{1,0:T(8,128)(2,1)} %get-tuple-element.13) | copy-start | bytes 196612
  10.7 19.4 %collective-permute-start.5 = (s16[256,128]{1,0:T(8,128)(2,1)}, s16[256,128]{1,0:T(8,128)(2,1)S(1)}, u32[]{:S(2)}, u32[]{:S(2)}) collective-permute-start(s16[256,128]{1,0:T(8,128)(2,1)} %get-tuple-element.13), channel_id=1, source_target_pairs={{96,128},{97,129},{100,132},{101,133},{104,136},{105,137},{108,140... | collective-permute-start | bytes 196616 | tf_op jit(solution)/shard_map/ppermute | solution.py:348
  12.3 17.5 %collective-permute-start.3 = (bf16[112,128]{1,0:T(8,128)(2,1)S(1)}, bf16[112,128]{1,0:T(8,128)(2,1)S(1)}, u32[]{:S(2)}, u32[]{:S(2)}) collective-permute-start(bf16[112,128]{1,0:T(8,128)(2,1)S(1)} %shard_map.78), channel_id=1, source_target_pairs={{0,15},{1,2},{2,1},{3,4},{4,3},{5,6},{6,5},{7,8},{8,7},{9,10},{10,... | collective-permute-start | bytes 86024 | tf_op jit(solution)/shard_map/ppermute | solution.py:348
  28.2 10.0 %collective-permute-start.9 = (s16[256,128]{1,0:T(8,128)(2,1)S(1)}, s16[256,128]{1,0:T(8,128)(2,1)S(1)}, u32[]{:S(2)}, u32[]{:S(2)}) collective-permute-start(s16[256,128]{1,0:T(8,128)(2,1)S(1)} %copy-done.6), channel_id=1, source_target_pairs={{0,32},{1,33},{2,34},{3,35},{4,36},{5,37},{6,38},{7,39},{8,40},{9,... | collective-permute-start | bytes 196616 | tf_op jit(solution)/shard_map/ppermute | solution.py:348
  30.2 4.0 %collective-permute-start.6 = (bf16[112,128]{1,0:T(8,128)(2,1)S(1)}, bf16[112,128]{1,0:T(8,128)(2,1)S(1)}, u32[]{:S(2)}, u32[]{:S(2)}) collective-permute-start(bf16[112,128]{1,0:T(8,128)(2,1)S(1)} %get-tuple-element.14), channel_id=1, source_target_pairs={{0,511},{1,498},{2,497},{3,500},{4,499},{5,502},{6,501},{7,504},{8... | collective-permute-start | bytes 86024 | tf_op jit(solution)/shard_map/ppermute | solution.py:348
  33.2 5.8 %copy-start.2 = (f32[2,8,8,128]{3,2,1,0:T(8,128)S(1)}, f32[2,8,8,128]{3,2,1,0:T(8,128)}, u32[]{:S(2)}) copy-start(f32[2,8,8,128]{3,2,1,0:T(8,128)} %param.7) | copy-start | bytes 196612
  33.3 5.8 %copy-start.3 = (f32[2,8,8,128]{3,2,1,0:T(8,128)S(1)}, f32[2,8,8,128]{3,2,1,0:T(8,128)}, u32[]{:S(2)}) copy-start(f32[2,8,8,128]{3,2,1,0:T(8,128)} %param.8) | copy-start | bytes 196612
  33.3 5.8 %copy-start.4 = (s32[8,8,128]{2,1,0:T(8,128)S(1)}, s32[8,8,128]{2,1,0:T(8,128)}, u32[]{:S(2)}) copy-start(s32[8,8,128]{2,1,0:T(8,128)} %param.11) | copy-start | bytes 98308
  33.3 5.8 %copy-start.5 = (s32[8,8,16]{2,1,0:T(8,128)S(1)}, s32[8,8,16]{2,1,0:T(8,128)}, u32[]{:S(2)}) copy-start(s32[8,8,16]{2,1,0:T(8,128)} %param.9) | copy-start | bytes 12292
  33.3 5.0 %collective-permute-start.7 = (bf16[32,128]{1,0:T(8,128)(2,1)S(1)}, bf16[32,128]{1,0:T(8,128)(2,1)S(1)}, u32[]{:S(2)}, u32[]{:S(2)}) collective-permute-start(bf16[32,128]{1,0:T(8,128)(2,1)S(1)} %get-tuple-element.15), channel_id=1, source_target_pairs={{16,31},{17,18},{18,17},{19,20},{20,19},{21,22},{22,21},{23,24},{2... | collective-permute-start | bytes 24584 | tf_op jit(solution)/shard_map/ppermute | solution.py:348
  34.3 4.7 %collective-permute-start.8 = (bf16[32,128]{1,0:T(8,128)(2,1)S(1)}, bf16[32,128]{1,0:T(8,128)(2,1)S(1)}, u32[]{:S(2)}, u32[]{:S(2)}) collective-permute-start(bf16[32,128]{1,0:T(8,128)(2,1)S(1)} %shard_map.81), channel_id=1, source_target_pairs={{0,1},{1,0},{2,3},{3,2},{4,5},{5,4},{6,7},{7,6},{8,9},{9,8},{10,11... | collective-permute-start | bytes 24584 | tf_op jit(solution)/shard_map/ppermute | solution.py:348

commit v10 on v9

--- a/solution.py
+++ b/solution.py
@@ -16,7 +16,7 @@
 VMEM_LIMIT = 32 * 1024 * 1024
 PACK_LIMIT = 60 * 1024 * 1024
 BIG = 1_000_000_000
-SIDE = 256
+SIDE = 112
 HEAD = 80
 ROWS_A = 7
 ROWS_B = 4

time: 41.8 us -> 41.8 us (level)
  transfers between devices with their start and end apart: 10 -> 10, of which waited for: 4 -> 3; matrix products, arithmetic and copies ran while one was open for 0% -> 0% of each run, Pallas kernels for 1% -> 1%
where the time goes in v10:
time: 41.8 us; the launch traced here: 41.4 us
  starting transfers between devices  35 us (84%)
  Pallas kernels  4.5 us (11%)
  waiting for transfers between devices  1.01 us (2%)
  between operations  0.87 us (2%)
    ppermute x10, starting transfers between devices, send(): return lax.ppermute(x, ('gx', 'gy'), pairs)  35 us
    pallas_call x1, Pallas kernels, local(): call(main_kernel, [sds((6, 64, 128), F32), sds((4, 64, 128), F32)], [VM]...  2.35 us
    pallas_call x1, Pallas kernels, local(): call(pack_kernel, [sds((608, 128), BF16), sds((HEAD, 128), BF16), sds((SI...  1.78 us
    ppermute x10, waiting for transfers between devices, send(): return lax.ppermute(x, ('gx', 'gy'), pairs)  1.01 us
  transfers between devices with their start and end apart: 10, of which 3 were waited for; matrix products, arithmetic and copies ran while one was open for 0% of the time, Pallas kernels for 1%

profile of v10, /device:TPU:1, one launch (start us, length us, event | category | flops | bytes accessed | tf_op | source)
XLA Modules:
  0.0 41.4 jit_solution(7418293067726522754)
XLA Ops:
  0.6 1.8 %shard_map.77 = (bf16[608,128]{1,0:T(8,128)(2,1)}, bf16[80,128]{1,0:T(8,128)(2,1)}, bf16[112,128]{1,0:T(8,128)(2,1)}, s16[256,128]{1,0:T(8,128)(2,1)}) custom-call(bf16[3,64,128]{2,1,0:T(8,128)(2,1)} %bitcast.8, s32[64,128]{1,0:T(8,128)} %bitcast.13, f32[128,128]{1,0:T(8,128)} %bitcast.18, f32[128,128]{1,0:T(8,128)} %bitcast.20), custom_call_target="tpu_custom_call" | custom-call | bytes 400000 | tf_op jit(solution)/shard_map/pallas_call | solution.py:362
  2.4 4.4 %collective-permute-start = (bf16[608,128]{1,0:T(8,128)(2,1)}, bf16[608,128]{1,0:T(8,128)(2,1)S(1)}, u32[]{:S(2)}, u32[]{:S(2)}) collective-permute-start(bf16[608,128]{1,0:T(8,128)(2,1)} %get-tuple-element.10), channel_id=1, source_target_pairs={{0,16},{1,17},{2,18},{3,19},{4,20},{5,21},{6,22},{7,23},{8,24},{9,... | collective-permute-start | bytes 466952 | tf_op jit(solution)/shard_map/ppermute | solution.py:348
  6.8 1.3 %collective-permute-start.2 = (bf16[80,128]{1,0:T(8,128)(2,1)}, bf16[80,128]{1,0:T(8,128)(2,1)S(1)}, u32[]{:S(2)}, u32[]{:S(2)}) collective-permute-start(bf16[80,128]{1,0:T(8,128)(2,1)} %get-tuple-element.11), channel_id=1, source_target_pairs={{16,0},{17,1},{18,2},{19,3},{20,4},{21,5},{22,6},{23,7},{24,8},{25... | collective-permute-start | bytes 61448 | tf_op jit(solution)/shard_map/ppermute | solution.py:348
  8.1 1.3 %collective-permute-start.1 = (bf16[608,128]{1,0:T(8,128)(2,1)}, bf16[608,128]{1,0:T(8,128)(2,1)S(1)}, u32[]{:S(2)}, u32[]{:S(2)}) collective-permute-start(bf16[608,128]{1,0:T(8,128)(2,1)} %get-tuple-element.10), channel_id=1, source_target_pairs={{112,128},{113,129},{114,130},{115,131},{116,132},{117,133},{118,1... | collective-permute-start | bytes 466952 | tf_op jit(solution)/shard_map/ppermute | solution.py:348
  9.4 1.3 %collective-permute-start.4 = (bf16[112,128]{1,0:T(8,128)(2,1)}, bf16[112,128]{1,0:T(8,128)(2,1)S(1)}, u32[]{:S(2)}, u32[]{:S(2)}) collective-permute-start(bf16[112,128]{1,0:T(8,128)(2,1)} %get-tuple-element.12), channel_id=1, source_target_pairs={{114,129},{115,132},{118,133},{119,136},{122,137},{123,140},{126,1... | collective-permute-start | bytes 86024 | tf_op jit(solution)/shard_map/ppermute | solution.py:348
  10.7 0.0 copy-start.6
  10.7 1.4 %collective-permute-start.5 = (s16[256,128]{1,0:T(8,128)(2,1)}, s16[256,128]{1,0:T(8,128)(2,1)S(1)}, u32[]{:S(2)}, u32[]{:S(2)}) collective-permute-start(s16[256,128]{1,0:T(8,128)(2,1)} %get-tuple-element.13), channel_id=1, source_target_pairs={{96,128},{97,129},{100,132},{101,133},{104,136},{105,137},{108,140... | collective-permute-start | bytes 196616 | tf_op jit(solution)/shard_map/ppermute | solution.py:348
  12.2 0.0 collective-permute-done.2.hi_ref
  12.2 0.1 shard_map.78
  12.3 15.9 %collective-permute-start.3 = (bf16[112,128]{1,0:T(8,128)(2,1)S(1)}, bf16[112,128]{1,0:T(8,128)(2,1)S(1)}, u32[]{:S(2)}, u32[]{:S(2)}) collective-permute-start(bf16[112,128]{1,0:T(8,128)(2,1)S(1)} %shard_map.78), channel_id=1, source_target_pairs={{0,15},{1,2},{2,1},{3,4},{4,3},{5,6},{6,5},{7,8},{8,7},{9,10},{10,... | collective-permute-start | bytes 86024 | tf_op jit(solution)/shard_map/ppermute | solution.py:348
  28.2 1.3 %collective-permute-start.9 = (s16[256,128]{1,0:T(8,128)(2,1)S(1)}, s16[256,128]{1,0:T(8,128)(2,1)S(1)}, u32[]{:S(2)}, u32[]{:S(2)}) collective-permute-start(s16[256,128]{1,0:T(8,128)(2,1)S(1)} %copy-done.6), channel_id=1, source_target_pairs={{0,32},{1,33},{2,34},{3,35},{4,36},{5,37},{6,38},{7,39},{8,40},{9,... | collective-permute-start | bytes 196616 | tf_op jit(solution)/shard_map/ppermute | solution.py:348
  29.6 0.1 shard_map.79.strip_ref
  29.7 0.1 collective-permute-done.3.wide_ref
  29.8 3.4 %collective-permute-start.6 = (bf16[112,128]{1,0:T(8,128)(2,1)S(1)}, bf16[112,128]{1,0:T(8,128)(2,1)S(1)}, u32[]{:S(2)}, u32[]{:S(2)}) collective-permute-start(bf16[112,128]{1,0:T(8,128)(2,1)S(1)} %get-tuple-element.14), channel_id=1, source_target_pairs={{0,511},{1,498},{2,497},{3,500},{4,499},{5,502},{6,501},{7,504},{8... | collective-permute-start | bytes 86024 | tf_op jit(solution)/shard_map/ppermute | solution.py:348
  33.2 0.0 copy-start.2
  33.3 0.0 copy-start.3
  33.3 0.0 copy-start.4
  33.3 0.0 copy-start.5
  33.3 0.8 %collective-permute-start.7 = (bf16[32,128]{1,0:T(8,128)(2,1)S(1)}, bf16[32,128]{1,0:T(8,128)(2,1)S(1)}, u32[]{:S(2)}, u32[]{:S(2)}) collective-permute-start(bf16[32,128]{1,0:T(8,128)(2,1)S(1)} %get-tuple-element.15), channel_id=1, source_target_pairs={{16,31},{17,18},{18,17},{19,20},{20,19},{21,22},{22,21},{23,24},{2... | collective-permute-start | bytes 24584 | tf_op jit(solution)/shard_map/ppermute | solution.py:348
  34.1 0.1 collective-permute-done.6.relay_ref
  34.2 0.1 shard_map.81
  34.3 3.9 %collective-permute-start.8 = (bf16[32,128]{1,0:T(8,128)(2,1)S(1)}, bf16[32,128]{1,0:T(8,128)(2,1)S(1)}, u32[]{:S(2)}, u32[]{:S(2)}) collective-permute-start(bf16[32,128]{1,0:T(8,128)(2,1)S(1)} %shard_map.81), channel_id=1, source_target_pairs={{0,1},{1,0},{2,3},{3,2},{4,5},{5,4},{6,7},{7,6},{8,9},{9,8},{10,11... | collective-permute-start | bytes 24584 | tf_op jit(solution)/shard_map/ppermute | solution.py:348
  38.2 0.8 %collective-permute-done.8.near_ref = bf16[32,128]{1,0:T(8,128)(2,1)S(1)} collective-permute-done((bf16[32,128]{1,0:T(8,128)(2,1)S(1)}, bf16[32,128]{1,0:T(8,128)(2,1)S(1)}, u32[]{:S(2)}, u32[]{:S(2)}) %collective-permute-start.8) | collective-permute-done | bytes 8224 | tf_op jit(solution)/shard_map/ppermute | solution.py:348
  39.0 2.3 %shard_map.82 = (f32[6,64,128]{2,1,0:T(8,128)}, f32[4,64,128]{2,1,0:T(8,128)}) custom-call(bf16[3,64,128]{2,1,0:T(8,128)(2,1)S(1)} %bitcast.12, s32[64,128]{1,0:T(8,128)S(1)} %bitcast.17, s32[64,128]{1,0:T(8,128)S(1)} %bitcast.22, bf16[608,128]{1,0:T(8,128)(2,1)S(1)} %collective-permute-done.lo_ref, bf16[608,128]{1,0:T(8,128)(2,1)S(1)} %collective-permute-done.1.wrap_ref, ...), custom_call_target="tpu_custom_call" | custom-call | bytes 400000 | tf_op jit(solution)/shard_map/pallas_call | solution.py:384
  (16 shorter events, 0.0 us)
Async XLA Ops:
  0.6 11.6 %copy-start = (bf16[3,8,8,128]{3,2,1,0:T(8,128)(2,1)S(1)}, bf16[3,8,8,128]{3,2,1,0:T(8,128)(2,1)}, u32[]{:S(2)}) copy-start(bf16[3,8,8,128]{3,2,1,0:T(8,128)(2,1)} %param.6) | copy-start | bytes 147460
  0.6 11.6 %copy-start.1 = (s32[8,8,128]{2,1,0:T(8,128)S(1)}, s32[8,8,128]{2,1,0:T(8,128)}, u32[]{:S(2)}) copy-start(s32[8,8,128]{2,1,0:T(8,128)} %param.10) | copy-start | bytes 98308
  2.4 25.8 %collective-permute-start = (bf16[608,128]{1,0:T(8,128)(2,1)}, bf16[608,128]{1,0:T(8,128)(2,1)S(1)}, u32[]{:S(2)}, u32[]{:S(2)}) collective-permute-start(bf16[608,128]{1,0:T(8,128)(2,1)} %get-tuple-element.10), channel_id=1, source_target_pairs={{0,16},{1,17},{2,18},{3,19},{4,20},{5,21},{6,22},{7,23},{8,24},{9,... | collective-permute-start | bytes 466952 | tf_op jit(solution)/shard_map/ppermute | solution.py:348
  6.8 5.3 %collective-permute-start.2 = (bf16[80,128]{1,0:T(8,128)(2,1)}, bf16[80,128]{1,0:T(8,128)(2,1)S(1)}, u32[]{:S(2)}, u32[]{:S(2)}) collective-permute-start(bf16[80,128]{1,0:T(8,128)(2,1)} %get-tuple-element.11), channel_id=1, source_target_pairs={{16,0},{17,1},{18,2},{19,3},{20,4},{21,5},{22,6},{23,7},{24,8},{25... | collective-permute-start | bytes 61448 | tf_op jit(solution)/shard_map/ppermute | solution.py:348
  8.1 26.0 %collective-permute-start.1 = (bf16[608,128]{1,0:T(8,128)(2,1)}, bf16[608,128]{1,0:T(8,128)(2,1)S(1)}, u32[]{:S(2)}, u32[]{:S(2)}) collective-permute-start(bf16[608,128]{1,0:T(8,128)(2,1)} %get-tuple-element.10), channel_id=1, source_target_pairs={{112,128},{113,129},{114,130},{115,131},{116,132},{117,133},{118,1... | collective-permute-start | bytes 466952 | tf_op jit(solution)/shard_map/ppermute | solution.py:348
  9.4 20.3 %collective-permute-start.4 = (bf16[112,128]{1,0:T(8,128)(2,1)}, bf16[112,128]{1,0:T(8,128)(2,1)S(1)}, u32[]{:S(2)}, u32[]{:S(2)}) collective-permute-start(bf16[112,128]{1,0:T(8,128)(2,1)} %get-tuple-element.12), channel_id=1, source_target_pairs={{114,129},{115,132},{118,133},{119,136},{122,137},{123,140},{126,1... | collective-permute-start | bytes 86024 | tf_op jit(solution)/shard_map/ppermute | solution.py:348
  10.7 17.5 %copy-start.6 = (s16[256,128]{1,0:T(8,128)(2,1)S(1)}, s16[256,128]{1,0:T(8,128)(2,1)}, u32[]{:S(2)}) copy-start(s16[256,128]{1,0:T(8,128)(2,1)} %get-tuple-element.13) | copy-start | bytes 196612
  10.7 19.1 %collective-permute-start.5 = (s16[256,128]{1,0:T(8,128)(2,1)}, s16[256,128]{1,0:T(8,128)(2,1)S(1)}, u32[]{:S(2)}, u32[]{:S(2)}) collective-permute-start(s16[256,128]{1,0:T(8,128)(2,1)} %get-tuple-element.13), channel_id=1, source_target_pairs={{96,128},{97,129},{100,132},{101,133},{104,136},{105,137},{108,140... | collective-permute-start | bytes 196616 | tf_op jit(solution)/shard_map/ppermute | solution.py:348
  12.3 17.5 %collective-permute-start.3 = (bf16[112,128]{1,0:T(8,128)(2,1)S(1)}, bf16[112,128]{1,0:T(8,128)(2,1)S(1)}, u32[]{:S(2)}, u32[]{:S(2)}) collective-permute-start(bf16[112,128]{1,0:T(8,128)(2,1)S(1)} %shard_map.78), channel_id=1, source_target_pairs={{0,15},{1,2},{2,1},{3,4},{4,3},{5,6},{6,5},{7,8},{8,7},{9,10},{10,... | collective-permute-start | bytes 86024 | tf_op jit(solution)/shard_map/ppermute | solution.py:348
  28.2 10.0 %collective-permute-start.9 = (s16[256,128]{1,0:T(8,128)(2,1)S(1)}, s16[256,128]{1,0:T(8,128)(2,1)S(1)}, u32[]{:S(2)}, u32[]{:S(2)}) collective-permute-start(s16[256,128]{1,0:T(8,128)(2,1)S(1)} %copy-done.6), channel_id=1, source_target_pairs={{0,32},{1,33},{2,34},{3,35},{4,36},{5,37},{6,38},{7,39},{8,40},{9,... | collective-permute-start | bytes 196616 | tf_op jit(solution)/shard_map/ppermute | solution.py:348
  29.8 4.4 %collective-permute-start.6 = (bf16[112,128]{1,0:T(8,128)(2,1)S(1)}, bf16[112,128]{1,0:T(8,128)(2,1)S(1)}, u32[]{:S(2)}, u32[]{:S(2)}) collective-permute-start(bf16[112,128]{1,0:T(8,128)(2,1)S(1)} %get-tuple-element.14), channel_id=1, source_target_pairs={{0,511},{1,498},{2,497},{3,500},{4,499},{5,502},{6,501},{7,504},{8... | collective-permute-start | bytes 86024 | tf_op jit(solution)/shard_map/ppermute | solution.py:348
  33.2 5.8 %copy-start.2 = (f32[2,8,8,128]{3,2,1,0:T(8,128)S(1)}, f32[2,8,8,128]{3,2,1,0:T(8,128)}, u32[]{:S(2)}) copy-start(f32[2,8,8,128]{3,2,1,0:T(8,128)} %param.7) | copy-start | bytes 196612
  33.3 5.8 %copy-start.3 = (f32[2,8,8,128]{3,2,1,0:T(8,128)S(1)}, f32[2,8,8,128]{3,2,1,0:T(8,128)}, u32[]{:S(2)}) copy-start(f32[2,8,8,128]{3,2,1,0:T(8,128)} %param.8) | copy-start | bytes 196612
  33.3 5.8 %copy-start.4 = (s32[8,8,128]{2,1,0:T(8,128)S(1)}, s32[8,8,128]{2,1,0:T(8,128)}, u32[]{:S(2)}) copy-start(s32[8,8,128]{2,1,0:T(8,128)} %param.11) | copy-start | bytes 98308
  33.3 5.8 %copy-start.5 = (s32[8,8,16]{2,1,0:T(8,128)S(1)}, s32[8,8,16]{2,1,0:T(8,128)}, u32[]{:S(2)}) copy-start(s32[8,8,16]{2,1,0:T(8,128)} %param.9) | copy-start | bytes 12292
  33.3 5.0 %collective-permute-start.7 = (bf16[32,128]{1,0:T(8,128)(2,1)S(1)}, bf16[32,128]{1,0:T(8,128)(2,1)S(1)}, u32[]{:S(2)}, u32[]{:S(2)}) collective-permute-start(bf16[32,128]{1,0:T(8,128)(2,1)S(1)} %get-tuple-element.15), channel_id=1, source_target_pairs={{16,31},{17,18},{18,17},{19,20},{20,19},{21,22},{22,21},{23,24},{2... | collective-permute-start | bytes 24584 | tf_op jit(solution)/shard_map/ppermute | solution.py:348
  34.3 4.7 %collective-permute-start.8 = (bf16[32,128]{1,0:T(8,128)(2,1)S(1)}, bf16[32,128]{1,0:T(8,128)(2,1)S(1)}, u32[]{:S(2)}, u32[]{:S(2)}) collective-permute-start(bf16[32,128]{1,0:T(8,128)(2,1)S(1)} %shard_map.81), channel_id=1, source_target_pairs={{0,1},{1,0},{2,3},{3,2},{4,5},{5,4},{6,7},{7,6},{8,9},{9,8},{10,11... | collective-permute-start | bytes 24584 | tf_op jit(solution)/shard_map/ppermute | solution.py:348

commit v11 on v10

--- a/solution.py
+++ b/solution.py
@@ -62,6 +62,11 @@
     return jnp.concatenate(left + none, axis=0), jnp.concatenate(right + none, axis=0)
 
 
+def code_kernel(lq_ref, mn_ref, code_ref):
+    code_ref[pl.ds(0, 128), :] = encode(lq_ref[...])
+    code_ref[pl.ds(128, 128), :] = encode(mn_ref[...])
+
+
 def own_rows(vel_ref, solid_ref, scratch):
     inside = solid_ref[...] == 1
     for c in range(3):
@@ -74,7 +79,7 @@
     return jnp.concatenate([rows[c][x] for c in range(3) for x in range(3)] + none, axis=0).astype(BF16)
 
 
-def pack_kernel(vel_hbm, solid_hbm, lq_hbm, mn_hbm, tail_ref, head_ref, side_ref, code_ref,
+def pack_kernel(vel_hbm, solid_hbm, lq_hbm, mn_hbm, tail_ref, head_ref, side_ref,
                 vel, solid, kept, scratch, sems):
     copies = [
         pltpu.make_async_copy(vel_hbm, vel, sems.at[0]),
@@ -95,7 +100,6 @@
     copies[2].wait()
     copies[3].wait()
     old = kept[...]
-    code_ref[...] = encode(old)
     high = old.astype(BF16)
     tail_ref[pl.ds(96, 256), :] = high
     tail_ref[pl.ds(352, 256), :] = (old - high.astype(F32)).astype(BF16)
@@ -359,9 +363,9 @@
     strip_type = sds((32, 128), BF16)
     code_type = sds((256, 128), jnp.int16)
     trans = pltpu.VMEM((3, 64, 128), F32)
-    tail, head, side, code = call(
+    tail, head, side = call(
         pack_kernel,
-        [sds((608, 128), BF16), sds((HEAD, 128), BF16), sds((SIDE, 128), BF16), code_type],
+        [sds((608, 128), BF16), sds((HEAD, 128), BF16), sds((SIDE, 128), BF16)],
         [HBM] * 4,
         [pltpu.VMEM((3, 64, 128), BF16), pltpu.VMEM((64, 128), jnp.int32), pltpu.VMEM((256, 128), F32),
          trans, pltpu.SemaphoreType.DMA((4,))],
@@ -371,6 +375,7 @@
     hi = send(head, lambda run, gx, gy: (gx - 1, gy) if run > 0 else None)
     side = send(side, lambda run, gx, gy: (gx + 1, far_side(gy)) if run == 7 and not low(gy) else None)
     wrap = send(tail, lambda run, gx, gy: (gx + 1, gy) if run == 7 else None)
+    (code,) = call(code_kernel, [code_type], [VM] * 2, [])(lq, mn)
     two_wrap = send(code, lambda run, gx, gy: (gx + 2, gy) if run == 6 and low(gy) else None)
     two = send(code, lambda run, gx, gy: (gx + 2, gy) if run != 6 or not low(gy) else None)
     (wide,) = call(wide_kernel, [sds((HEAD + 32, 128), BF16)], [VM] * 3, [trans], flops=BIG)(vel, solid, hi)

time: 41.8 us -> 41.9 us (level)
  waiting for transfers between devices: 1.01 us -> 1.55 us
  starting transfers between devices: 35 us -> 34.5 us
    ppermute x10, waiting for transfers between devices: 1.01 us -> 1.55 us  [send(): return lax.ppermute(x, ('gx', 'gy'), pairs)]
    ppermute x10, starting transfers between devices: 35 us -> 34.5 us  [send(): return lax.ppermute(x, ('gx', 'gy'), pairs)]
where the time goes in v11:
time: 41.9 us; the launch traced here: 41.4 us
  starting transfers between devices  34.5 us (82%)
  Pallas kernels  4.51 us (11%)
  waiting for transfers between devices  1.55 us (4%)
  between operations  0.88 us (2%)
    ppermute x10, starting transfers between devices, send(): return lax.ppermute(x, ('gx', 'gy'), pairs)  34.5 us
    pallas_call x1, Pallas kernels, local(): call(main_kernel, [sds((6, 64, 128), F32), sds((4, 64, 128), F32)], [VM]...  2.33 us
    pallas_call x1, Pallas kernels, local(): call(pack_kernel, [sds((608, 128), BF16), sds((HEAD, 128), BF16), sds((SI...  1.67 us
    ppermute x10, waiting for transfers between devices, send(): return lax.ppermute(x, ('gx', 'gy'), pairs)  1.55 us
  transfers between devices with their start and end apart: 10, of which 3 were waited for; matrix products, arithmetic and copies ran while one was open for 0% of the time, Pallas kernels for 1%

profile of v11, /device:TPU:1, one launch (start us, length us, event | category | flops | bytes accessed | tf_op | source)
XLA Modules:
  0.0 41.4 jit_solution(4460642113251193697)
XLA Ops:
  0.6 1.7 %shard_map.77 = (bf16[608,128]{1,0:T(8,128)(2,1)}, bf16[80,128]{1,0:T(8,128)(2,1)}, bf16[112,128]{1,0:T(8,128)(2,1)}) custom-call(bf16[3,64,128]{2,1,0:T(8,128)(2,1)} %bitcast.8, s32[64,128]{1,0:T(8,128)} %bitcast.19, f32[128,128]{1,0:T(8,128)} %bitcast.13, f32[128,128]{1,0:T(8,128)} %bitcast.16), custom_call_target="tpu_custom_call" | custom-call | bytes 400000 | tf_op jit(solution)/shard_map/pallas_call | solution.py:366
  2.3 4.4 %collective-permute-start = (bf16[608,128]{1,0:T(8,128)(2,1)}, bf16[608,128]{1,0:T(8,128)(2,1)S(1)}, u32[]{:S(2)}, u32[]{:S(2)}) collective-permute-start(bf16[608,128]{1,0:T(8,128)(2,1)} %get-tuple-element.9), channel_id=1, source_target_pairs={{0,16},{1,17},{2,18},{3,19},{4,20},{5,21},{6,22},{7,23},{8,24},{9,... | collective-permute-start | bytes 466952 | tf_op jit(solution)/shard_map/ppermute | solution.py:352
  6.7 0.0 copy-start.6
  6.7 0.0 copy-start
  6.7 0.0 copy-start.3
  6.7 1.4 %collective-permute-start.2 = (bf16[80,128]{1,0:T(8,128)(2,1)}, bf16[80,128]{1,0:T(8,128)(2,1)S(1)}, u32[]{:S(2)}, u32[]{:S(2)}) collective-permute-start(bf16[80,128]{1,0:T(8,128)(2,1)} %get-tuple-element.10), channel_id=1, source_target_pairs={{16,0},{17,1},{18,2},{19,3},{20,4},{21,5},{22,6},{23,7},{24,8},{25... | collective-permute-start | bytes 61448 | tf_op jit(solution)/shard_map/ppermute | solution.py:352
  8.2 1.3 %collective-permute-start.1 = (bf16[608,128]{1,0:T(8,128)(2,1)}, bf16[608,128]{1,0:T(8,128)(2,1)S(1)}, u32[]{:S(2)}, u32[]{:S(2)}) collective-permute-start(bf16[608,128]{1,0:T(8,128)(2,1)} %get-tuple-element.9), channel_id=1, source_target_pairs={{112,128},{113,129},{114,130},{115,131},{116,132},{117,133},{118,1... | collective-permute-start | bytes 466952 | tf_op jit(solution)/shard_map/ppermute | solution.py:352
  9.5 0.1 shard_map.80
  9.6 1.3 %collective-permute-start.5 = (s16[256,128]{1,0:T(8,128)(2,1)S(1)}, s16[256,128]{1,0:T(8,128)(2,1)S(1)}, u32[]{:S(2)}, u32[]{:S(2)}) collective-permute-start(s16[256,128]{1,0:T(8,128)(2,1)S(1)} %shard_map.80), channel_id=1, source_target_pairs={{96,128},{97,129},{100,132},{101,133},{104,136},{105,137},{108,140... | collective-permute-start | bytes 196616 | tf_op jit(solution)/shard_map/ppermute | solution.py:352
  10.9 1.3 %collective-permute-start.4 = (bf16[112,128]{1,0:T(8,128)(2,1)S(1)}, bf16[112,128]{1,0:T(8,128)(2,1)S(1)}, u32[]{:S(2)}, u32[]{:S(2)}) collective-permute-start(bf16[112,128]{1,0:T(8,128)(2,1)S(1)} %copy-done.6), channel_id=1, source_target_pairs={{114,129},{115,132},{118,133},{119,136},{122,137},{123,140},{126,1... | collective-permute-start | bytes 86024 | tf_op jit(solution)/shard_map/ppermute | solution.py:352
  12.3 0.1 shard_map.78
  12.4 15.9 %collective-permute-start.3 = (bf16[112,128]{1,0:T(8,128)(2,1)S(1)}, bf16[112,128]{1,0:T(8,128)(2,1)S(1)}, u32[]{:S(2)}, u32[]{:S(2)}) collective-permute-start(bf16[112,128]{1,0:T(8,128)(2,1)S(1)} %shard_map.78), channel_id=1, source_target_pairs={{0,15},{1,2},{2,1},{3,4},{4,3},{5,6},{6,5},{7,8},{8,7},{9,10},{10,... | collective-permute-start | bytes 86024 | tf_op jit(solution)/shard_map/ppermute | solution.py:352
  28.3 1.3 %collective-permute-start.9 = (s16[256,128]{1,0:T(8,128)(2,1)S(1)}, s16[256,128]{1,0:T(8,128)(2,1)S(1)}, u32[]{:S(2)}, u32[]{:S(2)}) collective-permute-start(s16[256,128]{1,0:T(8,128)(2,1)S(1)} %shard_map.80), channel_id=1, source_target_pairs={{0,32},{1,33},{2,34},{3,35},{4,36},{5,37},{6,38},{7,39},{8,40},{9,... | collective-permute-start | bytes 196616 | tf_op jit(solution)/shard_map/ppermute | solution.py:352
  29.6 0.1 shard_map.79.strip_ref
  29.7 0.5 %collective-permute-done.4.side_ref = bf16[112,128]{1,0:T(8,128)(2,1)S(1)} collective-permute-done((bf16[112,128]{1,0:T(8,128)(2,1)S(1)}, bf16[112,128]{1,0:T(8,128)(2,1)S(1)}, u32[]{:S(2)}, u32[]{:S(2)}) %collective-permute-start.4) | collective-permute-done | bytes 28704 | tf_op jit(solution)/shard_map/ppermute | solution.py:352
  30.2 3.1 %collective-permute-start.6 = (bf16[112,128]{1,0:T(8,128)(2,1)S(1)}, bf16[112,128]{1,0:T(8,128)(2,1)S(1)}, u32[]{:S(2)}, u32[]{:S(2)}) collective-permute-start(bf16[112,128]{1,0:T(8,128)(2,1)S(1)} %get-tuple-element.12), channel_id=1, source_target_pairs={{0,511},{1,498},{2,497},{3,500},{4,499},{5,502},{6,501},{7,504},{8... | collective-permute-start | bytes 86024 | tf_op jit(solution)/shard_map/ppermute | solution.py:352
  33.3 0.0 copy-start.4
  33.3 0.0 copy-start.5
  33.3 0.7 %collective-permute-start.7 = (bf16[32,128]{1,0:T(8,128)(2,1)S(1)}, bf16[32,128]{1,0:T(8,128)(2,1)S(1)}, u32[]{:S(2)}, u32[]{:S(2)}) collective-permute-start(bf16[32,128]{1,0:T(8,128)(2,1)S(1)} %get-tuple-element.13), channel_id=1, source_target_pairs={{16,31},{17,18},{18,17},{19,20},{20,19},{21,22},{22,21},{23,24},{2... | collective-permute-start | bytes 24584 | tf_op jit(solution)/shard_map/ppermute | solution.py:352
  34.0 0.3 collective-permute-done.6.relay_ref
  34.3 0.1 shard_map.82
  34.4 3.9 %collective-permute-start.8 = (bf16[32,128]{1,0:T(8,128)(2,1)S(1)}, bf16[32,128]{1,0:T(8,128)(2,1)S(1)}, u32[]{:S(2)}, u32[]{:S(2)}) collective-permute-start(bf16[32,128]{1,0:T(8,128)(2,1)S(1)} %shard_map.82), channel_id=1, source_target_pairs={{0,1},{1,0},{2,3},{3,2},{4,5},{5,4},{6,7},{7,6},{8,9},{9,8},{10,11... | collective-permute-start | bytes 24584 | tf_op jit(solution)/shard_map/ppermute | solution.py:352
  38.3 0.8 %collective-permute-done.8.near_ref = bf16[32,128]{1,0:T(8,128)(2,1)S(1)} collective-permute-done((bf16[32,128]{1,0:T(8,128)(2,1)S(1)}, bf16[32,128]{1,0:T(8,128)(2,1)S(1)}, u32[]{:S(2)}, u32[]{:S(2)}) %collective-permute-start.8) | collective-permute-done | bytes 8224 | tf_op jit(solution)/shard_map/ppermute | solution.py:352
  39.1 2.3 %shard_map.83 = (f32[6,64,128]{2,1,0:T(8,128)}, f32[4,64,128]{2,1,0:T(8,128)}) custom-call(bf16[3,64,128]{2,1,0:T(8,128)(2,1)S(1)} %bitcast.12, s32[64,128]{1,0:T(8,128)S(1)} %bitcast.23, s32[64,128]{1,0:T(8,128)S(1)} %bitcast.24, bf16[608,128]{1,0:T(8,128)(2,1)S(1)} %collective-permute-done.lo_ref, bf16[608,128]{1,0:T(8,128)(2,1)S(1)} %collective-permute-done.1.wrap_ref, ...), custom_call_target="tpu_custom_call" | custom-call | bytes 400000 | tf_op jit(solution)/shard_map/pallas_call | solution.py:389
  (17 shorter events, 0.0 us)
Async XLA Ops:
  0.6 8.9 %copy-start.1 = (f32[2,8,8,128]{3,2,1,0:T(8,128)S(1)}, f32[2,8,8,128]{3,2,1,0:T(8,128)}, u32[]{:S(2)}) copy-start(f32[2,8,8,128]{3,2,1,0:T(8,128)} %param.7) | copy-start | bytes 196612
  0.6 8.9 %copy-start.2 = (f32[2,8,8,128]{3,2,1,0:T(8,128)S(1)}, f32[2,8,8,128]{3,2,1,0:T(8,128)}, u32[]{:S(2)}) copy-start(f32[2,8,8,128]{3,2,1,0:T(8,128)} %param.8) | copy-start | bytes 196612
  2.3 26.0 %collective-permute-start = (bf16[608,128]{1,0:T(8,128)(2,1)}, bf16[608,128]{1,0:T(8,128)(2,1)S(1)}, u32[]{:S(2)}, u32[]{:S(2)}) collective-permute-start(bf16[608,128]{1,0:T(8,128)(2,1)} %get-tuple-element.9), channel_id=1, source_target_pairs={{0,16},{1,17},{2,18},{3,19},{4,20},{5,21},{6,22},{7,23},{8,24},{9,... | collective-permute-start | bytes 466952 | tf_op jit(solution)/shard_map/ppermute | solution.py:352
  6.7 4.2 %copy-start.6 = (bf16[112,128]{1,0:T(8,128)(2,1)S(1)}, bf16[112,128]{1,0:T(8,128)(2,1)}, u32[]{:S(2)}) copy-start(bf16[112,128]{1,0:T(8,128)(2,1)} %get-tuple-element.11) | copy-start | bytes 86020
  6.7 5.5 %copy-start = (bf16[3,8,8,128]{3,2,1,0:T(8,128)(2,1)S(1)}, bf16[3,8,8,128]{3,2,1,0:T(8,128)(2,1)}, u32[]{:S(2)}) copy-start(bf16[3,8,8,128]{3,2,1,0:T(8,128)(2,1)} %param.6) | copy-start | bytes 147460
  6.7 5.5 %copy-start.3 = (s32[8,8,128]{2,1,0:T(8,128)S(1)}, s32[8,8,128]{2,1,0:T(8,128)}, u32[]{:S(2)}) copy-start(s32[8,8,128]{2,1,0:T(8,128)} %param.10) | copy-start | bytes 98308
  6.7 5.5 %collective-permute-start.2 = (bf16[80,128]{1,0:T(8,128)(2,1)}, bf16[80,128]{1,0:T(8,128)(2,1)S(1)}, u32[]{:S(2)}, u32[]{:S(2)}) collective-permute-start(bf16[80,128]{1,0:T(8,128)(2,1)} %get-tuple-element.10), channel_id=1, source_target_pairs={{16,0},{17,1},{18,2},{19,3},{20,4},{21,5},{22,6},{23,7},{24,8},{25... | collective-permute-start | bytes 61448 | tf_op jit(solution)/shard_map/ppermute | solution.py:352
  8.2 25.8 %collective-permute-start.1 = (bf16[608,128]{1,0:T(8,128)(2,1)}, bf16[608,128]{1,0:T(8,128)(2,1)S(1)}, u32[]{:S(2)}, u32[]{:S(2)}) collective-permute-start(bf16[608,128]{1,0:T(8,128)(2,1)} %get-tuple-element.9), channel_id=1, source_target_pairs={{112,128},{113,129},{114,130},{115,131},{116,132},{117,133},{118,1... | collective-permute-start | bytes 466952 | tf_op jit(solution)/shard_map/ppermute | solution.py:352
  9.6 20.6 %collective-permute-start.5 = (s16[256,128]{1,0:T(8,128)(2,1)S(1)}, s16[256,128]{1,0:T(8,128)(2,1)S(1)}, u32[]{:S(2)}, u32[]{:S(2)}) collective-permute-start(s16[256,128]{1,0:T(8,128)(2,1)S(1)} %shard_map.80), channel_id=1, source_target_pairs={{96,128},{97,129},{100,132},{101,133},{104,136},{105,137},{108,140... | collective-permute-start | bytes 196616 | tf_op jit(solution)/shard_map/ppermute | solution.py:352
  10.9 19.3 %collective-permute-start.4 = (bf16[112,128]{1,0:T(8,128)(2,1)S(1)}, bf16[112,128]{1,0:T(8,128)(2,1)S(1)}, u32[]{:S(2)}, u32[]{:S(2)}) collective-permute-start(bf16[112,128]{1,0:T(8,128)(2,1)S(1)} %copy-done.6), channel_id=1, source_target_pairs={{114,129},{115,132},{118,133},{119,136},{122,137},{123,140},{126,1... | collective-permute-start | bytes 86024 | tf_op jit(solution)/shard_map/ppermute | solution.py:352
  12.4 17.8 %collective-permute-start.3 = (bf16[112,128]{1,0:T(8,128)(2,1)S(1)}, bf16[112,128]{1,0:T(8,128)(2,1)S(1)}, u32[]{:S(2)}, u32[]{:S(2)}) collective-permute-start(bf16[112,128]{1,0:T(8,128)(2,1)S(1)} %shard_map.78), channel_id=1, source_target_pairs={{0,15},{1,2},{2,1},{3,4},{4,3},{5,6},{6,5},{7,8},{8,7},{9,10},{10,... | collective-permute-start | bytes 86024 | tf_op jit(solution)/shard_map/ppermute | solution.py:352
  28.3 10.0 %collective-permute-start.9 = (s16[256,128]{1,0:T(8,128)(2,1)S(1)}, s16[256,128]{1,0:T(8,128)(2,1)S(1)}, u32[]{:S(2)}, u32[]{:S(2)}) collective-permute-start(s16[256,128]{1,0:T(8,128)(2,1)S(1)} %shard_map.80), channel_id=1, source_target_pairs={{0,32},{1,33},{2,34},{3,35},{4,36},{5,37},{6,38},{7,39},{8,40},{9,... | collective-permute-start | bytes 196616 | tf_op jit(solution)/shard_map/ppermute | solution.py:352
  30.2 4.0 %collective-permute-start.6 = (bf16[112,128]{1,0:T(8,128)(2,1)S(1)}, bf16[112,128]{1,0:T(8,128)(2,1)S(1)}, u32[]{:S(2)}, u32[]{:S(2)}) collective-permute-start(bf16[112,128]{1,0:T(8,128)(2,1)S(1)} %get-tuple-element.12), channel_id=1, source_target_pairs={{0,511},{1,498},{2,497},{3,500},{4,499},{5,502},{6,501},{7,504},{8... | collective-permute-start | bytes 86024 | tf_op jit(solution)/shard_map/ppermute | solution.py:352
  33.3 5.8 %copy-start.4 = (s32[8,8,128]{2,1,0:T(8,128)S(1)}, s32[8,8,128]{2,1,0:T(8,128)}, u32[]{:S(2)}) copy-start(s32[8,8,128]{2,1,0:T(8,128)} %param.11) | copy-start | bytes 98308
  33.3 5.8 %copy-start.5 = (s32[8,8,16]{2,1,0:T(8,128)S(1)}, s32[8,8,16]{2,1,0:T(8,128)}, u32[]{:S(2)}) copy-start(s32[8,8,16]{2,1,0:T(8,128)} %param.9) | copy-start | bytes 12292
  33.3 5.0 %collective-permute-start.7 = (bf16[32,128]{1,0:T(8,128)(2,1)S(1)}, bf16[32,128]{1,0:T(8,128)(2,1)S(1)}, u32[]{:S(2)}, u32[]{:S(2)}) collective-permute-start(bf16[32,128]{1,0:T(8,128)(2,1)S(1)} %get-tuple-element.13), channel_id=1, source_target_pairs={{16,31},{17,18},{18,17},{19,20},{20,19},{21,22},{22,21},{23,24},{2... | collective-permute-start | bytes 24584 | tf_op jit(solution)/shard_map/ppermute | solution.py:352
  34.4 4.7 %collective-permute-start.8 = (bf16[32,128]{1,0:T(8,128)(2,1)S(1)}, bf16[32,128]{1,0:T(8,128)(2,1)S(1)}, u32[]{:S(2)}, u32[]{:S(2)}) collective-permute-start(bf16[32,128]{1,0:T(8,128)(2,1)S(1)} %shard_map.82), channel_id=1, source_target_pairs={{0,1},{1,0},{2,3},{3,2},{4,5},{5,4},{6,7},{7,6},{8,9},{9,8},{10,11... | collective-permute-start | bytes 24584 | tf_op jit(solution)/shard_map/ppermute | solution.py:352
